TPU v7x, 32 devices: a whole 2x2x4 slice. The times are simulated.
32 devices in a mesh: fsdp: 8 (over z, core), tp: 4 (over y, x).
Axes of the slice: x: 2, y: 2, z: 4, core: 2. Of those that a mesh axis runs over, the one named last changes fastest.
Arguments:
- states: bfloat16 [256, 4, 8192], P('fsdp'), may hold values from -6 to 6
- norm_gain: float32 [8192], replicated, may hold values from 0.5 to 1.5
- query_base: bfloat16 [8192, 8192], P(('fsdp', 'tp')), may hold values from -0.0625 to 0.0625
- key_base: bfloat16 [8192, 1024], P(('fsdp', 'tp')), may hold values from -0.0625 to 0.0625
- value_base: bfloat16 [8192, 1024], P(('fsdp', 'tp')), may hold values from -0.0625 to 0.0625
- output_base: bfloat16 [8192, 8192], P(('fsdp', 'tp')), may hold values from -0.5 to 0.5
- query_down: bfloat16 [4, 8192, 64], P(None, ('fsdp', 'tp')), may hold values from -0.0625 to 0.0625
- query_up: bfloat16 [4, 64, 8192], replicated, may hold values from -0.75 to 0.75
- key_down: bfloat16 [4, 8192, 64], P(None, ('fsdp', 'tp')), may hold values from -0.0625 to 0.0625
- key_up: bfloat16 [4, 64, 1024], replicated, may hold values from -0.75 to 0.75
- value_down: bfloat16 [4, 8192, 64], P(None, ('fsdp', 'tp')), may hold values from -0.0625 to 0.0625
- value_up: bfloat16 [4, 64, 1024], replicated, may hold values from -0.75 to 0.75
- output_down: bfloat16 [4, 8192, 64], P(None, ('fsdp', 'tp')), may hold values from -0.5 to 0.5
- output_up: bfloat16 [4, 64, 8192], replicated, may hold values from -0.75 to 0.75
- adapter_layer: int32 [1], replicated, may hold values from 0 to 3
- kv_lengths: int32 [256], P('fsdp'), may hold values from 8 to 512
- cache_keys: bfloat16 [256, 512, 8, 128], P('fsdp', None, 'tp'), may hold values from -320 to 320
- cache_values: bfloat16 [256, 512, 8, 128], P('fsdp', None, 'tp'), may hold values from -6 to 6
Outputs:
- layer_update: bfloat16 [256, 4, 8192], P('fsdp', None, 'tp')
Inputs may be any that keep to these rules, and one draw needn't show every extreme that they name: `kv_lengths`: slots at and beyond a sequence's length hold no cached position.
All inputs are finite; a program needn't handle non-finite values.
Results may differ from a plain program's by a relative error of at most 0.012.
The roundings to bfloat16 on the way count: a program that leaves them out, or rounds other values in their place, can miss the bound.
Values may be sent and summed in bfloat16 or wider, within the bound.
No kernel may reach another device: no remote copies, remote signals or barrier semaphores. Data moves between devices by JAX's collectives and lax.ppermute only.
A program may use at most 128 MiB of HBM per device.

v0:
```python
import jax
import jax.numpy as jnp
from jax import lax
from jax.experimental import pallas as pl
from jax.experimental.pallas import tpu as pltpu
from jax.sharding import Mesh, PartitionSpec as P

HQ = 64
KVH = 8
DH = 128

rope_theta = 1000000.0
low_rank_scale = 0.5
epsilon = 1e-06
CHUNKS = 1


def GROUPS(count):
    return [[0]] + [list(range(1, count))]


def merge_block(base, down, up):
    delta = lax.dot_general(
        down, up, (((0,), (0,)), ((), ())), preferred_element_type=jnp.float32
    )
    return (base.astype(jnp.float32) + low_rank_scale * delta).astype(jnp.bfloat16)


def merge_kernel(slot_ref, base_ref, down_ref, up_ref, out_ref):
    cores, _, _, piece = out_ref.shape
    for c in range(cores):
        part = slice(c * piece, (c + 1) * piece)
        out_ref[c, 0] = merge_block(base_ref[:, part], down_ref[0], up_ref[0, :, part])


def merge_input_kernel(
    slot_ref, qb_ref, kb_ref, vb_ref, qd_ref, kd_ref, vd_ref, qu_ref, ku_ref, vu_ref, out_ref
):
    cores = out_ref.shape[0]
    piece = qb_ref.shape[1] // cores
    for c in range(cores):
        part = slice(c * piece, (c + 1) * piece)
        out_ref[c, 0, :, :piece] = merge_block(qb_ref[:, part], qd_ref[0], qu_ref[0, :, part])
    out_ref[0, 0, :, piece:] = merge_block(kb_ref[...], kd_ref[0], ku_ref[0])
    out_ref[1, 0, :, piece:] = merge_block(vb_ref[...], vd_ref[0], vu_ref[0])


def flipped(down):
    return jnp.swapaxes(down, 1, 2)


def merge_output(slot, base, down, up, cores, cols):
    depth, width = base.shape
    rank = up.shape[1]
    piece = width // (cols * cores)
    grid = pltpu.PrefetchScalarGridSpec(
        num_scalar_prefetch=1,
        grid=(cols,),
        in_specs=[
            pl.BlockSpec((depth, piece * cores), lambda t, s: (0, t)),
            pl.BlockSpec((1, rank, depth), lambda t, s: (s[0], 0, 0)),
            pl.BlockSpec((1, rank, piece * cores), lambda t, s: (s[0], 0, t)),
        ],
        out_specs=pl.BlockSpec((cores, 1, depth, piece), lambda t, s: (0, t, 0, 0)),
    )
    return pl.pallas_call(
        merge_kernel,
        grid_spec=grid,
        out_shape=jax.ShapeDtypeStruct((cores, cols, depth, piece), base.dtype),
        cost_estimate=pl.CostEstimate(
            flops=2 * depth * rank * width, bytes_accessed=5 * depth * width, transcendentals=0
        ),
        compiler_params=pltpu.CompilerParams(vmem_limit_bytes=32 * 1024 * 1024),
        name="merge_output",
    )(slot, base, flipped(down), up)


def merge_inputs(slot, bases, downs, ups, cores, cols):
    depth, width = bases[0].shape
    rank = ups[0].shape[1]
    piece = width // (cols * cores)
    side = bases[1].shape[1] // cols
    whole = pl.BlockSpec((1, rank, depth), lambda t, s: (s[0], 0, 0))
    grid = pltpu.PrefetchScalarGridSpec(
        num_scalar_prefetch=1,
        grid=(cols,),
        in_specs=[
            pl.BlockSpec((depth, piece * cores), lambda t, s: (0, t)),
            pl.BlockSpec((depth, side), lambda t, s: (0, t)),
            pl.BlockSpec((depth, side), lambda t, s: (0, t)),
            whole,
            whole,
            whole,
            pl.BlockSpec((1, rank, piece * cores), lambda t, s: (s[0], 0, t)),
            pl.BlockSpec((1, rank, side), lambda t, s: (s[0], 0, t)),
            pl.BlockSpec((1, rank, side), lambda t, s: (s[0], 0, t)),
        ],
        out_specs=pl.BlockSpec((cores, 1, depth, piece + side), lambda t, s: (0, t, 0, 0)),
    )
    return pl.pallas_call(
        merge_input_kernel,
        grid_spec=grid,
        out_shape=jax.ShapeDtypeStruct((cores, cols, depth, piece + side), bases[0].dtype),
        cost_estimate=pl.CostEstimate(
            flops=3 * depth * rank * width, bytes_accessed=6 * depth * width, transcendentals=0
        ),
        compiler_params=pltpu.CompilerParams(vmem_limit_bytes=32 * 1024 * 1024),
        name="merge_inputs",
    )(slot, *bases, *[flipped(d) for d in downs], *ups)


def norm_kernel(z_ref, x_ref, gain_ref, *refs):
    outs, scratch = refs[:-1], refs[-1]
    x = x_ref[...].astype(jnp.float32)
    mean = jnp.mean(x * x, axis=-1, keepdims=True)
    scratch[...] = (x * lax.rsqrt(mean + epsilon) * gain_ref[...]).astype(jnp.bfloat16)
    block = outs[0].shape[1]
    for k, out_ref in enumerate(outs):
        start = pl.multiple_of((z_ref[0] ^ k) * block, block)
        out_ref[...] = scratch[:, pl.ds(start, block)]


def normed_blocks(z, x, gain, planes):
    rows, width = x.shape
    step = min(rows, 32)
    block = width // planes
    grid = pltpu.PrefetchScalarGridSpec(
        num_scalar_prefetch=1,
        grid=(rows // step,),
        in_specs=[
            pl.BlockSpec((step, width), lambda i, z: (i, 0)),
            pl.BlockSpec((1, width), lambda i, z: (0, 0)),
        ],
        out_specs=[pl.BlockSpec((step, block), lambda i, z: (i, 0))] * planes,
        scratch_shapes=[pltpu.VMEM((step, width), jnp.bfloat16)],
    )
    return pl.pallas_call(
        norm_kernel,
        grid_spec=grid,
        out_shape=[jax.ShapeDtypeStruct((rows, block), jnp.bfloat16)] * planes,
        cost_estimate=pl.CostEstimate(
            flops=6 * rows * width, bytes_accessed=4 * rows * width, transcendentals=rows
        ),
        name="normed_blocks",
    )(z.astype(jnp.int32).reshape(1), x, gain.reshape(1, width))


def rotate(vectors, positions):
    head_dim = vectors.shape[-1]
    half_dim = head_dim // 2
    frequency = rope_theta ** (-2.0 * jnp.arange(half_dim, dtype=jnp.float32) / head_dim)
    phases = positions[:, :, None] * frequency[None, None, :]
    cosine = jnp.concatenate((jnp.cos(phases), jnp.cos(phases)), -1)[:, :, None, :]
    sine = jnp.concatenate((jnp.sin(phases), jnp.sin(phases)), -1)[:, :, None, :]
    turned = jnp.concatenate((-vectors[..., half_dim:], vectors[..., :half_dim]), -1)
    return vectors * cosine + turned * sine


def attend(queries, keys_new, values_new, cache_k, cache_v, lengths):
    seq_count, step_count, head_count, head_dim = queries.shape
    kv_count = keys_new.shape[2]
    grouped = queries.reshape(seq_count, step_count, kv_count, head_count // kv_count, head_dim)
    score_scale = head_dim ** (-0.5)
    old_scores = (
        jnp.einsum("bskgd,blkd->bskgl", grouped, cache_k, preferred_element_type=jnp.float32)
        * score_scale
    )
    new_scores = (
        jnp.einsum("bskgd,btkd->bskgt", grouped, keys_new, preferred_element_type=jnp.float32)
        * score_scale
    )
    live_slots = jnp.arange(cache_k.shape[1], dtype=jnp.int32)[None, :] < lengths[:, None]
    old_scores = jnp.where(live_slots[:, None, None, None, :], old_scores, -1e30)
    causal = jnp.arange(step_count)[:, None] >= jnp.arange(step_count)[None, :]
    new_scores = jnp.where(causal[None, :, None, None, :], new_scores, -1e30)
    highest = jnp.maximum(jnp.max(old_scores, -1), jnp.max(new_scores, -1))[..., None]
    old_exp = jnp.exp(old_scores - highest)
    new_exp = jnp.exp(new_scores - highest)
    denominator = jnp.sum(old_exp, -1, keepdims=True) + jnp.sum(new_exp, -1, keepdims=True)
    old_weights = (old_exp / denominator).astype(jnp.bfloat16)
    new_weights = (new_exp / denominator).astype(jnp.bfloat16)
    mixture = jnp.einsum(
        "bskgl,blkd->bskgd", old_weights, cache_v, preferred_element_type=jnp.float32
    )
    mixture = mixture + jnp.einsum(
        "bskgt,btkd->bskgd", new_weights, values_new, preferred_element_type=jnp.float32
    )
    return mixture.astype(jnp.bfloat16).reshape(seq_count * step_count, head_count * head_dim)


def by_xor(blocks, index):
    count = len(blocks)
    bit = 1
    while bit < count:
        odd = (index & bit) != 0
        blocks = [jnp.where(odd, blocks[i ^ bit], blocks[i]) for i in range(count)]
        bit *= 2
    return blocks


def local(
    states,
    norm_gain,
    query_base,
    key_base,
    value_base,
    output_base,
    query_down,
    query_up,
    key_down,
    key_up,
    value_down,
    value_up,
    output_down,
    output_up,
    adapter_layer,
    kv_lengths,
    cache_keys,
    cache_values,
):
    planes, cores, cols = lax.axis_size("z"), lax.axis_size("core"), lax.axis_size("tp")
    z, t = lax.axis_index("z"), lax.axis_index("tp")
    core = lax.axis_index("core")
    plane_pairs = [[(a, a ^ k) for a in range(planes)] for k in range(planes)]
    tp_pairs = [[(a, a ^ k) for a in range(cols)] for k in range(cols)]
    core_pairs = [(0, 1), (1, 0)]
    depth = query_base.shape[0]
    seqs, steps, width = states.shape
    rows = seqs * steps

    blocks = normed_blocks(z, states.reshape(rows, width), norm_gain, planes)
    joined = merge_inputs(
        adapter_layer,
        (query_base, key_base, value_base),
        (query_down, key_down, value_down),
        (query_up, key_up, value_up),
        cores,
        cols,
    )
    (joined, output_base, *blocks) = lax.optimization_barrier((joined, output_base, *blocks))
    joined = joined.reshape(cores * cols * depth, -1)
    weights = lax.all_to_all(joined, ("core", "tp"), 0, 0, tiled=True)
    mine = [lax.ppermute(blocks[k], "z", plane_pairs[k]) for k in range(1, planes)]
    mine = [blocks[0]] + mine
    other = [lax.ppermute(block, "core", core_pairs) for block in mine]
    merged = merge_output(adapter_layer, output_base, output_down, output_up, cores, cols)
    merged = merged.reshape(cores * cols * depth, -1)
    (weights, merged, *both) = lax.optimization_barrier((weights, merged, *mine, *other))
    mine, other = both[:planes], both[planes:]
    output_weights = lax.all_to_all(merged, ("core", "tp"), 0, 0, tiled=True)

    half_q = HQ * DH // (cols * cores)
    kv_cols = KVH * DH // cols
    part = rows // CHUNKS
    seq_part = seqs // CHUNKS
    outs = []
    for h in range(CHUNKS):
        sl = slice(h * part, (h + 1) * part)
        total = None
        for k in list(range(1, planes)) + [0]:
            block = jnp.concatenate((mine[k][sl], other[k][sl]))
            product = jnp.dot(block, weights, preferred_element_type=jnp.float32)
            if k:
                product = lax.ppermute(product.astype(jnp.float16), "z", plane_pairs[k])
                product = product.astype(jnp.float32)
            total = product if total is None else total + product
        if h == 0:
            total, output_weights = lax.optimization_barrier((total, output_weights))
        here = total[:part]
        there = lax.ppermute(total[part:], "core", core_pairs)
        low = jnp.where(core == 0, here, there)
        high = jnp.where(core == 0, there, here)
        lengths = kv_lengths[h * seq_part : (h + 1) * seq_part]
        positions = (
            lengths.astype(jnp.float32)[:, None] + jnp.arange(steps, dtype=jnp.float32)[None, :]
        )
        queries = jnp.concatenate((low[:, :half_q], high[:, :half_q]), 1)
        queries = rotate(queries.reshape(seq_part, steps, -1, DH), positions).astype(jnp.bfloat16)
        keys_new = rotate(low[:, half_q:].reshape(seq_part, steps, -1, DH), positions)
        keys_new = keys_new.astype(jnp.bfloat16)
        values_new = high[:, half_q:].reshape(seq_part, steps, -1, DH).astype(jnp.bfloat16)
        ss = slice(h * seq_part, (h + 1) * seq_part)
        attended = attend(
            queries, keys_new, values_new, cache_keys[ss], cache_values[ss], lengths
        )

        attended = attended.reshape(cols, part // cols, -1)
        turned = []
        for j in range(cols):
            block = lax.dynamic_index_in_dim(attended, t ^ j, 0, keepdims=False)
            turned.append(lax.ppermute(block, "tp", tp_pairs[j]) if j else block)
        turned = jnp.stack(turned)
        heads = []
        for k in range(planes):
            block = lax.dynamic_index_in_dim(turned, t ^ z ^ k, 0, keepdims=False)
            heads.append(lax.ppermute(block, "z", plane_pairs[k]) if k else block)
        heads = jnp.stack(heads)
        piece = part // cols
        gathered = [lax.ppermute(heads, "tp", tp_pairs[j]) if j else heads for j in range(cols)]
        crossed = [lax.ppermute(block, "core", core_pairs) for block in gathered]
        lows, highs = [], []
        for group in GROUPS(cols):
            total = None
            for k in list(range(1, planes)) + [0]:
                block = jnp.concatenate(
                    [gathered[j][k] for j in group] + [crossed[j][k] for j in group]
                )
                product = jnp.dot(block, output_weights, preferred_element_type=jnp.float32)
                if k:
                    product = lax.ppermute(product.astype(jnp.bfloat16), "z", plane_pairs[k])
                    product = product.astype(jnp.float32)
                total = product if total is None else total + product
            total = total.astype(jnp.bfloat16)
            here, there = jnp.split(total, 2)
            there = lax.ppermute(there, "core", core_pairs)
            lows.append(jnp.where(core == 0, here, there))
            highs.append(jnp.where(core == 0, there, here))
        low, high = jnp.concatenate(lows), jnp.concatenate(highs)
        full = jnp.concatenate((low, high), 1).reshape(cols, part // cols, -1)
        full = jnp.stack(by_xor([full[j] for j in range(cols)], t))
        outs.append(full.reshape(seq_part, steps, -1))
    return jnp.concatenate(outs)


def solution(mesh):
    tp_size = mesh.shape["tp"]
    fine = Mesh(mesh.devices.reshape(-1, 2, tp_size), ("z", "core", "tp"))
    fsdp = ("z", "core")
    split = ("z", "core", "tp")
    in_specs = (
        P(fsdp, None, None),
        P(),
        P(split, None),
        P(split, None),
        P(split, None),
        P(split, None),
        P(None, split, None),
        P(),
        P(None, split, None),
        P(),
        P(None, split, None),
        P(),
        P(None, split, None),
        P(),
        P(),
        P(fsdp),
        P(fsdp, None, "tp", None),
        P(fsdp, None, "tp", None),
    )
    out_specs = P(fsdp, None, "tp")
    return jax.shard_map(local, mesh=fine, in_specs=in_specs, out_specs=out_specs, check_vma=False)
```

profile of v0, /device:TPU:0, one launch (start us, length us, event | category | flops | bytes accessed | tf_op | source)
XLA Modules:
  0.0 281.7 jit_solution(15229958852538229050)
XLA Ops:
  0.8 4.0 %reshape.113.x_ref = bf16[128,8192]{1,0:T(8,128)(2,1)} reshape(bf16[32,4,8192]{2,1,0:T(4,128)(2,1)} %param.18) | data formatting | bytes 4194304 | tf_op jit(solution)/shard_map/reshape | solution.py:231
  4.8 4.4 %normed_blocks.1 = (bf16[128,2048]{1,0:T(8,128)(2,1)}, bf16[128,2048]{1,0:T(8,128)(2,1)}, bf16[128,2048]{1,0:T(8,128)(2,1)}, bf16[128,2048]{1,0:T(8,128)(2,1)}) custom-call(s32[1]{0:T(128)} %bitcast.3.z_ref, bf16[128,8192]{1,0:T(8,128)(2,1)} %reshape.113.x_ref, f32[1,8192]{1,0:T(1,128)} %bitcast.222), custom_call_target="tpu_custom_call" | custom-call | flops 6291456 | bytes 4194304 | tf_op jit(solution)/shard_map/normed_blocks/pallas_call | solution.py:137
  9.3 2.2 copy-done.2
  11.4 2.2 copy-done.3
  13.6 3.2 %merge_inputs.1 = bf16[2,4,256,1280]{3,2,1,0:T(8,128)(2,1)S(1)} custom-call(s32[1]{0:T(128)S(6)} %copy.91.slot_ref, bf16[256,8192]{1,0:T(8,128)(2,1)S(1)} %copy-done.2, bf16[256,1024]{1,0:T(8,128)(2,1)S(1)} %copy-done.6, bf16[256,1024]{1,0:T(8,128)(2,1)S(1)} %copy-done.7, bf16[4,64,256]{2,1,0:T(8,128)(2,1)S(1)} %bitcast.207, ...), custom_call_target="tpu_custom_call" | custom-call | flops 402653184 | bytes 12582912 | tf_op jit(solution)/shard_map/merge_inputs/pallas_call | solution.py:100
  16.8 2.4 copy-done
  19.2 5.3 %all-to-all-start = ((bf16[8,256,1280]{2,1,0:T(8,128)(2,1)}), bf16[8,256,1280]{2,1,0:T(8,128)(2,1)}, u32[]{:S(2)}, u32[]{:S(2)}) async-start(bf16[8,256,1280]{2,1,0:T(8,128)(2,1)} %bitcast.205), calls=%async_computation | async-start | bytes 10485760 | tf_op jit(solution)/shard_map/all_to_all | solution.py:242
  24.5 2.6 collective-permute-start
  27.1 2.6 collective-permute-start.1
  29.7 20.4 %collective-permute-done = bf16[128,2048]{1,0:T(8,128)(2,1)S(1)} collective-permute-done((bf16[128,2048]{1,0:T(8,128)(2,1)S(1)}, bf16[128,2048]{1,0:T(8,128)(2,1)S(1)}, u32[]{:S(2)}, u32[]{:S(2)}) %collective-permute-start) | collective-permute-done | bytes 524320 | tf_op jit(solution)/shard_map/ppermute | solution.py:243
  50.2 15.4 %collective-permute-done.1 = bf16[128,2048]{1,0:T(8,128)(2,1)S(1)} collective-permute-done((bf16[128,2048]{1,0:T(8,128)(2,1)}, bf16[128,2048]{1,0:T(8,128)(2,1)S(1)}, u32[]{:S(2)}, u32[]{:S(2)}) %collective-permute-start.1) | collective-permute-done | bytes 524320 | tf_op jit(solution)/shard_map/ppermute | solution.py:243
  66.1 2.2 copy-done.4
  68.2 2.2 copy-done.5
  70.4 2.5 merge_output.1
  73.0 2.0 copy-done.1
  76.6 7.5 %all-to-all-done = bf16[8,256,1280]{2,1,0:T(8,128)(2,1)} async-done(((bf16[8,256,1280]{2,1,0:T(8,128)(2,1)}), bf16[8,256,1280]{2,1,0:T(8,128)(2,1)}, u32[]{:S(2)}, u32[]{:S(2)}) %all-to-all-start) | async-done | bytes 5242912 | tf_op jit(solution)/shard_map/all_to_all | solution.py:242
  84.1 4.7 %all-to-all-start.1 = ((bf16[8,256,1024]{2,1,0:T(8,128)(2,1)}), bf16[8,256,1024]{2,1,0:T(8,128)(2,1)}, u32[]{:S(2)}, u32[]{:S(2)}) async-start(bf16[8,256,1024]{2,1,0:T(8,128)(2,1)} %bitcast.206), calls=%async_computation.1 | async-start | bytes 8388608 | tf_op jit(solution)/shard_map/all_to_all | solution.py:250
  88.9 4.2 %convolution_convert_fusion = f16[256,1280]{1,0:T(8,128)(2,1)S(1)} fusion(bf16[2048,1280]{1,0:T(8,128)(2,1)} %bitcast.6, bf16[128,2048]{1,0:T(8,128)(2,1)} %collective-permute-done.6, bf16[128,2048]{1,0:T(8,128)(2,1)S(1)} %collective-permute-done.2), kind=kOutput, calls=%fused_computation.11 | convolution fusion | flops 1344602112 | bytes 6946816 | tf_op jit(solution)/shard_map/dot_general | solution.py:262
  93.1 4.9 %collective-permute-start.9 = (f16[256,1280]{1,0:T(8,128)(2,1)S(1)}, f16[256,1280]{1,0:T(8,128)(2,1)S(1)}, u32[]{:S(2)}, u32[]{:S(2)}) collective-permute-start(f16[256,1280]{1,0:T(8,128)(2,1)S(1)} %convolution_convert_fusion), channel_id=1, source_target_pairs={{0,24},{8,16},{16,8},{24,0},{1,25},{9,17},{17,9},{25,1},{2,26},{10... | collective-permute-start | bytes 1966088 | tf_op jit(solution)/shard_map/ppermute | solution.py:264
  98.0 4.9 %convolution_convert_fusion.1 = f16[256,1280]{1,0:T(8,128)(2,1)} fusion(bf16[2048,1280]{1,0:T(8,128)(2,1)} %bitcast.6, bf16[128,2048]{1,0:T(8,128)(2,1)S(1)} %copy-done.20, bf16[128,2048]{1,0:T(8,128)(2,1)S(1)} %collective-permute-done.1), kind=kOutput, calls=%fused_computation.12 | convolution fusion | flops 1344602112 | bytes 6946816 | tf_op jit(solution)/shard_map/dot_general | solution.py:262
  102.8 4.9 %convolution_convert_fusion.2 = f16[256,1280]{1,0:T(8,128)(2,1)} fusion(bf16[2048,1280]{1,0:T(8,128)(2,1)} %bitcast.6, bf16[128,2048]{1,0:T(8,128)(2,1)S(1)} %collective-permute-done.4, bf16[128,2048]{1,0:T(8,128)(2,1)S(1)} %collective-permute-done), kind=kOutput, calls=%fused_computation.13 | convolution fusion | flops 1344602112 | bytes 6946816 | tf_op jit(solution)/shard_map/dot_general | solution.py:262
  108.4 5.2 %collective-permute-done.9 = f16[256,1280]{1,0:T(8,128)(2,1)S(1)} collective-permute-done((f16[256,1280]{1,0:T(8,128)(2,1)S(1)}, f16[256,1280]{1,0:T(8,128)(2,1)S(1)}, u32[]{:S(2)}, u32[]{:S(2)}) %collective-permute-start.9) | collective-permute-done | bytes 655392 | tf_op jit(solution)/shard_map/ppermute | solution.py:264
  113.6 41.2 %collective-permute-done.8 = f16[256,1280]{1,0:T(8,128)(2,1)S(1)} collective-permute-done((f16[256,1280]{1,0:T(8,128)(2,1)}, f16[256,1280]{1,0:T(8,128)(2,1)S(1)}, u32[]{:S(2)}, u32[]{:S(2)}) %collective-permute-start.8) | collective-permute-done | bytes 655392 | tf_op jit(solution)/shard_map/ppermute | solution.py:264
  154.8 4.4 %convolution_add_fusion = f32[256,1280]{1,0:T(8,128)S(1)} fusion(bf16[2048,1280]{1,0:T(8,128)(2,1)} %bitcast.6, f16[256,1280]{1,0:T(8,128)(2,1)S(1)} %collective-permute-done.9, f16[256,1280]{1,0:T(8,128)(2,1)S(1)} %collective-permute-done.8, f16[256,1280]{1,0:T(8,128)(2,1)S(1)} %collective-permute-done.7, bf16[128,2048]{1,0:T(8,128)(2,1)} %copy-done.18, ...), kind=kOutput, calls=%fused_computation.10 | convolution fusion | flops 1346240512 | bytes 9568256 | tf_op jit(solution)/shard_map/dot_general | solution.py:262
  163.9 6.4 %bitcast_reduce_fusion = (f32[32,4,2,8]{3,1,2,0:T(4,128)S(1)}, f32[32,2,4,8,512]{4,3,2,1,0:T(8,128)S(1)}) fusion(pred[32,512]{1,0:T(8,128)(4,1)S(1)} %iota_compare_fusion, bf16[32,512,2,128,1]{3,2,1,0,4:T(2,128)(2,1)} %bitcast.213, bf16[32,4,2,8,128]{4,3,2,1,0:T(8,128)(2,1)S(1)} %fusion.33), kind=kOutput, calls=%fused_computation.5 | convolution fusion | flops 271579136 | bytes 13131776 | tf_op jit(solution)/shard_map/bskgd,blkd->bskgl/dot_general | solution.py:165
  170.3 2.5 fusion.96
  172.8 2.0 fusion.5
  175.4 6.0 %fusion.11 = f32[32,4,2,8,128]{4,3,1,2,0:T(8,128)S(1)} fusion(bf16[32,512,2,128,1]{3,2,1,0,4:T(2,128)(2,1)} %bitcast.223, f32[32,2,4,8,512]{4,3,2,1,0:T(8,128)} %copy-done.14, f32[32,4,2,8]{3,1,2,0:T(4,128)S(1)} %add.95, f32[32,4,2,8]{3,1,2,0:T(4,128)S(1)} %max.7, pred[32,512]{1,0:T(8,128)(4,1)S(1)} %iota_compare_fusion), kind=kOutput, calls=%fused_computation.19 | convolution fusion | flops 273678336 | bytes 13664256 | tf_op jit(solution)/shard_map/bskgl,blkd->bskgd/dot_general | solution.py:182
  182.3 2.6 collective-permute-start.13
  185.9 3.4 %collective-permute-done.13 = bf16[32,2048]{1,0:T(8,128)(2,1)S(1)} collective-permute-done((bf16[32,2048]{1,0:T(8,128)(2,1)S(1)}, bf16[32,2048]{1,0:T(8,128)(2,1)S(1)}, u32[]{:S(2)}, u32[]{:S(2)}) %collective-permute-start.13) | collective-permute-done | bytes 131104 | tf_op jit(solution)/shard_map/ppermute | solution.py:291
  189.3 2.6 collective-permute-done.12
  192.2 2.5 collective-permute-start.16
  196.6 3.9 %collective-permute-done.16 = bf16[32,2048]{1,0:T(8,128)(2,1)S(1)} collective-permute-done((bf16[32,2048]{1,0:T(8,128)(2,1)S(1)}, bf16[32,2048]{1,0:T(8,128)(2,1)S(1)}, u32[]{:S(2)}, u32[]{:S(2)}) %collective-permute-start.16) | collective-permute-done | bytes 131104 | tf_op jit(solution)/shard_map/ppermute | solution.py:296
  200.5 4.6 %collective-permute-done.15 = bf16[32,2048]{1,0:T(8,128)(2,1)S(1)} collective-permute-done((bf16[32,2048]{1,0:T(8,128)(2,1)S(1)}, bf16[32,2048]{1,0:T(8,128)(2,1)S(1)}, u32[]{:S(2)}, u32[]{:S(2)}) %collective-permute-start.15) | collective-permute-done | bytes 131104 | tf_op jit(solution)/shard_map/ppermute | solution.py:296
  208.9 3.0 %convolution_convert_fusion.6 = bf16[64,1024]{1,0:T(8,128)(2,1)S(1)} fusion(bf16[2048,1024]{1,0:T(8,128)(2,1)} %bitcast.10, bf16[32,2048]{1,0:T(8,128)(2,1)S(1)} %get-tuple-element.60, bf16[32,2048]{1,0:T(8,128)(2,1)S(1)} %collective-permute-done.16), kind=kOutput, calls=%fused_computation.31 | convolution fusion | flops 269025280 | bytes 4587520 | tf_op jit(solution)/shard_map/dot_general | solution.py:308
  211.9 2.3 collective-permute-start.20
  214.2 3.0 %convolution_convert_fusion.7 = bf16[64,1024]{1,0:T(8,128)(2,1)S(1)} fusion(bf16[2048,1024]{1,0:T(8,128)(2,1)} %bitcast.10, bf16[32,2048]{1,0:T(8,128)(2,1)S(1)} %get-tuple-element.61, bf16[32,2048]{1,0:T(8,128)(2,1)S(1)} %collective-permute-done.15), kind=kOutput, calls=%fused_computation.32 | convolution fusion | flops 269025280 | bytes 4587520 | tf_op jit(solution)/shard_map/dot_general | solution.py:308
  217.4 3.0 %convolution_convert_fusion.8 = bf16[64,1024]{1,0:T(8,128)(2,1)S(1)} fusion(bf16[2048,1024]{1,0:T(8,128)(2,1)} %bitcast.10, bf16[32,2048]{1,0:T(8,128)(2,1)S(1)} %get-tuple-element.62, bf16[32,2048]{1,0:T(8,128)(2,1)S(1)} %collective-permute-done.14), kind=kOutput, calls=%fused_computation.33 | convolution fusion | flops 269025280 | bytes 4587520 | tf_op jit(solution)/shard_map/dot_general | solution.py:308
  220.4 2.2 collective-permute-start.18
  222.6 9.6 %collective-permute-done.23 = bf16[4,32,2048]{2,1,0:T(8,128)(2,1)S(1)} collective-permute-done((bf16[4,32,2048]{2,1,0:T(8,128)(2,1)S(1)}, bf16[4,32,2048]{2,1,0:T(8,128)(2,1)S(1)}, u32[]{:S(2)}, u32[]{:S(2)}) %collective-permute-start.23) | collective-permute-done | bytes 524320 | tf_op jit(solution)/shard_map/ppermute | solution.py:299
  236.1 3.2 %convolution_convert_fusion.3 = bf16[192,1024]{1,0:T(8,128)(2,1)S(1)} fusion(bf16[192,2048]{1,0:T(8,128)(2,1)S(1)} %get-tuple-element.65, bf16[2048,1024]{1,0:T(8,128)(2,1)} %bitcast.10), kind=kOutput, calls=%fused_computation.25 | convolution fusion | flops 805502976 | bytes 5373952 | tf_op jit(solution)/shard_map/dot_general | solution.py:308
  239.3 2.3 collective-permute-start.30
  241.6 3.2 %convolution_convert_fusion.4 = bf16[192,1024]{1,0:T(8,128)(2,1)S(1)} fusion(bf16[192,2048]{1,0:T(8,128)(2,1)S(1)} %get-tuple-element.66, bf16[2048,1024]{1,0:T(8,128)(2,1)} %bitcast.10), kind=kOutput, calls=%fused_computation.26 | convolution fusion | flops 805502976 | bytes 5373952 | tf_op jit(solution)/shard_map/dot_general | solution.py:308
  244.9 3.9 %convolution_convert_fusion.5 = bf16[192,1024]{1,0:T(8,128)(2,1)} fusion(bf16[192,2048]{1,0:T(8,128)(2,1)S(1)} %get-tuple-element.63, bf16[2048,1024]{1,0:T(8,128)(2,1)} %bitcast.10), kind=kOutput, calls=%fused_computation.27 | convolution fusion | flops 805502976 | bytes 5373952 | tf_op jit(solution)/shard_map/dot_general | solution.py:308
  248.8 2.1 collective-permute-start.28
  250.9 3.0 %add_convert_fusion = bf16[64,1024]{1,0:T(8,128)(2,1)S(1)} fusion(bf16[64,1024]{1,0:T(8,128)(2,1)S(1)} %collective-permute-done.20, bf16[64,1024]{1,0:T(8,128)(2,1)S(1)} %collective-permute-done.19, bf16[64,1024]{1,0:T(8,128)(2,1)S(1)} %collective-permute-done.18, bf16[2048,1024]{1,0:T(8,128)(2,1)} %bitcast.10, bf16[32,2048]{1,0:T(8,128)(2,1)S(1)} %get-tuple-element.59, ...), kind=kOutput, calls=%fused_computation.77 | convolution fusion | flops 269418496 | bytes 4980736 | tf_op jit(solution)/shard_map/dot_general | solution.py:308
  254.1 21.7 %collective-permute-done.29 = bf16[192,1024]{1,0:T(8,128)(2,1)S(1)} collective-permute-done((bf16[192,1024]{1,0:T(8,128)(2,1)S(1)}, bf16[192,1024]{1,0:T(8,128)(2,1)S(1)}, u32[]{:S(2)}, u32[]{:S(2)}) %collective-permute-start.29) | collective-permute-done | bytes 393248 | tf_op jit(solution)/shard_map/ppermute | solution.py:310
  275.7 3.3 %fusion.16 = bf16[192,1024]{1,0:T(8,128)(2,1)S(1)} fusion(bf16[192,2048]{1,0:T(8,128)(2,1)S(1)} %get-tuple-element.64, bf16[2048,1024]{1,0:T(8,128)(2,1)} %bitcast.10, bf16[192,1024]{1,0:T(8,128)(2,1)S(1)} %collective-permute-done.30, bf16[192,1024]{1,0:T(8,128)(2,1)S(1)} %collective-permute-done.29, bf16[192,1024]{1,0:T(8,128)(2,1)} %collective-permute-done.28), kind=kOutput, calls=%fused_computation.24 | convolution fusion | flops 806682624 | bytes 6553600 | tf_op jit(solution)/shard_map/dot_general | solution.py:308
  (132 shorter events, 22.5 us)
Async XLA Ops:
  0.0 9.2 %copy-start.6 = (bf16[256,1024]{1,0:T(8,128)(2,1)S(1)}, bf16[256,1024]{1,0:T(8,128)(2,1)}, u32[]{:S(2)}) copy-start(bf16[256,1024]{1,0:T(8,128)(2,1)} %kb_ref.1) | copy-start | bytes 1572868
  0.0 9.2 %copy-start.7 = (bf16[256,1024]{1,0:T(8,128)(2,1)S(1)}, bf16[256,1024]{1,0:T(8,128)(2,1)}, u32[]{:S(2)}) copy-start(bf16[256,1024]{1,0:T(8,128)(2,1)} %vb_ref.1) | copy-start | bytes 1572868
  0.0 9.2 %copy-start.10 = (bf16[4,256,64]{1,2,0:T(8,128)(2,1)S(1)}, bf16[4,256,64]{1,2,0:T(8,128)(2,1)}, u32[]{:S(2)}) copy-start(bf16[4,256,64]{1,2,0:T(8,128)(2,1)} %param.24) | copy-start | bytes 393220
  0.0 9.2 %copy-start.11 = (bf16[4,256,64]{1,2,0:T(8,128)(2,1)S(1)}, bf16[4,256,64]{1,2,0:T(8,128)(2,1)}, u32[]{:S(2)}) copy-start(bf16[4,256,64]{1,2,0:T(8,128)(2,1)} %param.26) | copy-start | bytes 393220
  0.0 9.2 %copy-start.12 = (bf16[4,256,64]{1,2,0:T(8,128)(2,1)S(1)}, bf16[4,256,64]{1,2,0:T(8,128)(2,1)}, u32[]{:S(2)}) copy-start(bf16[4,256,64]{1,2,0:T(8,128)(2,1)} %param.28) | copy-start | bytes 393220
  0.0 9.2 %copy-start.8 = (bf16[4,64,1024]{2,1,0:T(8,128)(2,1)S(1)}, bf16[4,64,1024]{2,1,0:T(8,128)(2,1)}, u32[]{:S(2)}) copy-start(bf16[4,64,1024]{2,1,0:T(8,128)(2,1)} %ku_ref.1) | copy-start | bytes 1572868
  0.0 9.2 %copy-start.9 = (bf16[4,64,1024]{2,1,0:T(8,128)(2,1)S(1)}, bf16[4,64,1024]{2,1,0:T(8,128)(2,1)}, u32[]{:S(2)}) copy-start(bf16[4,64,1024]{2,1,0:T(8,128)(2,1)} %vu_ref.1) | copy-start | bytes 1572868
  19.2 5.3 %copy-start.21 = (bf16[128,2048]{1,0:T(8,128)(2,1)S(1)}, bf16[128,2048]{1,0:T(8,128)(2,1)}, u32[]{:S(2)}) copy-start(bf16[128,2048]{1,0:T(8,128)(2,1)} %get-tuple-element.34) | copy-start | bytes 1572868
  19.2 10.5 %copy-start.17 = (bf16[128,2048]{1,0:T(8,128)(2,1)S(1)}, bf16[128,2048]{1,0:T(8,128)(2,1)}, u32[]{:S(2)}) copy-start(bf16[128,2048]{1,0:T(8,128)(2,1)} %get-tuple-element.44) | copy-start | bytes 1572868
  19.2 46.9 %copy-start.13 = (bf16[4,256,64]{1,2,0:T(8,128)(2,1)S(1)}, bf16[4,256,64]{1,2,0:T(8,128)(2,1)}, u32[]{:S(2)}) copy-start(bf16[4,256,64]{1,2,0:T(8,128)(2,1)} %param.30) | copy-start | bytes 393220
  19.2 64.9 %all-to-all-start = ((bf16[8,256,1280]{2,1,0:T(8,128)(2,1)}), bf16[8,256,1280]{2,1,0:T(8,128)(2,1)}, u32[]{:S(2)}, u32[]{:S(2)}) async-start(bf16[8,256,1280]{2,1,0:T(8,128)(2,1)} %bitcast.205), calls=%async_computation | async-start | bytes 10485760 | tf_op jit(solution)/shard_map/all_to_all | solution.py:242
  24.5 25.6 %collective-permute-start = (bf16[128,2048]{1,0:T(8,128)(2,1)S(1)}, bf16[128,2048]{1,0:T(8,128)(2,1)S(1)}, u32[]{:S(2)}, u32[]{:S(2)}) collective-permute-start(bf16[128,2048]{1,0:T(8,128)(2,1)S(1)} %copy-done.21), channel_id=1, source_target_pairs={{0,8},{8,0},{16,24},{24,16},{1,9},{9,1},{17,25},{25,17},{2,10},{10... | collective-permute-start | bytes 1572872 | tf_op jit(solution)/shard_map/ppermute | solution.py:243
  27.1 38.4 %collective-permute-start.1 = (bf16[128,2048]{1,0:T(8,128)(2,1)}, bf16[128,2048]{1,0:T(8,128)(2,1)S(1)}, u32[]{:S(2)}, u32[]{:S(2)}) collective-permute-start(bf16[128,2048]{1,0:T(8,128)(2,1)} %get-tuple-element.35), channel_id=1, source_target_pairs={{0,16},{8,24},{16,0},{24,8},{1,17},{9,25},{17,1},{25,9},{2,18},{10... | collective-permute-start | bytes 1572872 | tf_op jit(solution)/shard_map/ppermute | solution.py:243
  29.7 35.8 %collective-permute-start.2 = (bf16[128,2048]{1,0:T(8,128)(2,1)}, bf16[128,2048]{1,0:T(8,128)(2,1)S(1)}, u32[]{:S(2)}, u32[]{:S(2)}) collective-permute-start(bf16[128,2048]{1,0:T(8,128)(2,1)} %get-tuple-element.36), channel_id=1, source_target_pairs={{0,24},{8,16},{16,8},{24,0},{1,25},{9,17},{17,9},{25,1},{2,26},{10... | collective-permute-start | bytes 1572872 | tf_op jit(solution)/shard_map/ppermute | solution.py:243
  29.7 45.3 %collective-permute-start.3 = (bf16[128,2048]{1,0:T(8,128)(2,1)S(1)}, bf16[128,2048]{1,0:T(8,128)(2,1)S(1)}, u32[]{:S(2)}, u32[]{:S(2)}) collective-permute-start(bf16[128,2048]{1,0:T(8,128)(2,1)S(1)} %copy-done.17), channel_id=1, source_target_pairs={{0,4},{4,0},{1,5},{5,1},{2,6},{6,2},{3,7},{7,3},{8,12},{12,8},{9,1... | collective-permute-start | bytes 1572872 | tf_op jit(solution)/shard_map/ppermute | solution.py:245
  50.2 25.7 %collective-permute-start.4 = (bf16[128,2048]{1,0:T(8,128)(2,1)S(1)}, bf16[128,2048]{1,0:T(8,128)(2,1)S(1)}, u32[]{:S(2)}, u32[]{:S(2)}) collective-permute-start(bf16[128,2048]{1,0:T(8,128)(2,1)S(1)} %collective-permute-done), channel_id=1, source_target_pairs={{0,4},{4,0},{1,5},{5,1},{2,6},{6,2},{3,7},{7,3},{8,12},{12,8},{9,1... | collective-permute-start | bytes 1572872 | tf_op jit(solution)/shard_map/ppermute | solution.py:245
  65.5 10.3 %collective-permute-start.5 = (bf16[128,2048]{1,0:T(8,128)(2,1)S(1)}, bf16[128,2048]{1,0:T(8,128)(2,1)S(1)}, u32[]{:S(2)}, u32[]{:S(2)}) collective-permute-start(bf16[128,2048]{1,0:T(8,128)(2,1)S(1)} %collective-permute-done.1), channel_id=1, source_target_pairs={{0,4},{4,0},{1,5},{5,1},{2,6},{6,2},{3,7},{7,3},{8,12},{12,8},{9,1... | collective-permute-start | bytes 1572872 | tf_op jit(solution)/shard_map/ppermute | solution.py:245
  65.5 11.1 %collective-permute-start.6 = (bf16[128,2048]{1,0:T(8,128)(2,1)S(1)}, bf16[128,2048]{1,0:T(8,128)(2,1)}, u32[]{:S(2)}, u32[]{:S(2)}) collective-permute-start(bf16[128,2048]{1,0:T(8,128)(2,1)S(1)} %collective-permute-done.2), channel_id=1, source_target_pairs={{0,4},{4,0},{1,5},{5,1},{2,6},{6,2},{3,7},{7,3},{8,12},{12,8},{9,1... | collective-permute-start | bytes 1572872 | tf_op jit(solution)/shard_map/ppermute | solution.py:245
  84.1 75.1 %all-to-all-start.1 = ((bf16[8,256,1024]{2,1,0:T(8,128)(2,1)}), bf16[8,256,1024]{2,1,0:T(8,128)(2,1)}, u32[]{:S(2)}, u32[]{:S(2)}) async-start(bf16[8,256,1024]{2,1,0:T(8,128)(2,1)} %bitcast.206), calls=%async_computation.1 | async-start | bytes 8388608 | tf_op jit(solution)/shard_map/all_to_all | solution.py:250
  88.8 9.1 %copy-start.20 = (bf16[128,2048]{1,0:T(8,128)(2,1)S(1)}, bf16[128,2048]{1,0:T(8,128)(2,1)}, u32[]{:S(2)}) copy-start(bf16[128,2048]{1,0:T(8,128)(2,1)} %copy-done.19) | copy-start | bytes 1572868
  93.1 20.5 %collective-permute-start.9 = (f16[256,1280]{1,0:T(8,128)(2,1)S(1)}, f16[256,1280]{1,0:T(8,128)(2,1)S(1)}, u32[]{:S(2)}, u32[]{:S(2)}) collective-permute-start(f16[256,1280]{1,0:T(8,128)(2,1)S(1)} %convolution_convert_fusion), channel_id=1, source_target_pairs={{0,24},{8,16},{16,8},{24,0},{1,25},{9,17},{17,9},{25,1},{2,26},{10... | collective-permute-start | bytes 1966088 | tf_op jit(solution)/shard_map/ppermute | solution.py:264
  102.8 5.5 %copy-start.16 = (s32[32]{0:T(128)S(1)}, s32[32]{0:T(128)}, u32[]{:S(2)}) copy-start(s32[32]{0:T(128)} %param.33) | copy-start | bytes 388
  102.8 51.9 %collective-permute-start.8 = (f16[256,1280]{1,0:T(8,128)(2,1)}, f16[256,1280]{1,0:T(8,128)(2,1)S(1)}, u32[]{:S(2)}, u32[]{:S(2)}) collective-permute-start(f16[256,1280]{1,0:T(8,128)(2,1)} %convolution_convert_fusion.1), channel_id=1, source_target_pairs={{0,16},{8,24},{16,0},{24,8},{1,17},{9,25},{17,1},{25,9},{2,18},{10... | collective-permute-start | bytes 1966088 | tf_op jit(solution)/shard_map/ppermute | solution.py:264
  107.7 47.0 %collective-permute-start.7 = (f16[256,1280]{1,0:T(8,128)(2,1)}, f16[256,1280]{1,0:T(8,128)(2,1)S(1)}, u32[]{:S(2)}, u32[]{:S(2)}) collective-permute-start(f16[256,1280]{1,0:T(8,128)(2,1)} %convolution_convert_fusion.2), channel_id=1, source_target_pairs={{0,8},{8,0},{16,24},{24,16},{1,9},{9,1},{17,25},{25,17},{2,10},{10... | collective-permute-start | bytes 1966088 | tf_op jit(solution)/shard_map/ppermute | solution.py:264
  159.2 2.2 collective-permute-start.10
  163.8 6.4 %copy-start.15 = (f32[32,4,128]{2,1,0:T(4,128)S(1)}, f32[32,4,128]{2,1,0:T(4,128)}, u32[]{:S(2)}) copy-start(f32[32,4,128]{2,1,0:T(4,128)} %get-tuple-element.106) | copy-start | bytes 196612
  163.8 6.4 %copy-start.22 = (pred[4,4]{1,0:T(4,128)(4,1)S(1)}, pred[4,4]{1,0:T(4,128)(4,1)}, u32[]{:S(2)}) copy-start(pred[4,4]{1,0:T(4,128)(4,1)} %iota_compare_fusion.1) | copy-start | bytes 52
  182.3 6.9 %collective-permute-start.13 = (bf16[32,2048]{1,0:T(8,128)(2,1)S(1)}, bf16[32,2048]{1,0:T(8,128)(2,1)S(1)}, u32[]{:S(2)}, u32[]{:S(2)}) collective-permute-start(bf16[32,2048]{1,0:T(8,128)(2,1)S(1)} %get-tuple-element.92), channel_id=1, source_target_pairs={{0,3},{1,2},{2,1},{3,0},{4,7},{5,6},{6,5},{7,4},{8,11},{9,10},{10,... | collective-permute-start | bytes 393224 | tf_op jit(solution)/shard_map/ppermute | solution.py:291
  184.9 6.9 %collective-permute-start.12 = (bf16[32,2048]{1,0:T(8,128)(2,1)S(1)}, bf16[32,2048]{1,0:T(8,128)(2,1)S(1)}, u32[]{:S(2)}, u32[]{:S(2)}) collective-permute-start(bf16[32,2048]{1,0:T(8,128)(2,1)S(1)} %get-tuple-element.93), channel_id=1, source_target_pairs={{0,2},{1,3},{2,0},{3,1},{4,6},{5,7},{6,4},{7,5},{8,10},{9,11},{10,... | collective-permute-start | bytes 393224 | tf_op jit(solution)/shard_map/ppermute | solution.py:291
  185.5 6.5 %collective-permute-start.11 = (bf16[32,2048]{1,0:T(8,128)(2,1)S(1)}, bf16[32,2048]{1,0:T(8,128)(2,1)S(1)}, u32[]{:S(2)}, u32[]{:S(2)}) collective-permute-start(bf16[32,2048]{1,0:T(8,128)(2,1)S(1)} %get-tuple-element.94), channel_id=1, source_target_pairs={{0,1},{1,0},{2,3},{3,2},{4,5},{5,4},{6,7},{7,6},{8,9},{9,8},{10,11... | collective-permute-start | bytes 393224 | tf_op jit(solution)/shard_map/ppermute | solution.py:291
  192.2 8.3 %collective-permute-start.16 = (bf16[32,2048]{1,0:T(8,128)(2,1)S(1)}, bf16[32,2048]{1,0:T(8,128)(2,1)S(1)}, u32[]{:S(2)}, u32[]{:S(2)}) collective-permute-start(bf16[32,2048]{1,0:T(8,128)(2,1)S(1)} %get-tuple-element.88), channel_id=1, source_target_pairs={{0,24},{8,16},{16,8},{24,0},{1,25},{9,17},{17,9},{25,1},{2,26},{10... | collective-permute-start | bytes 393224 | tf_op jit(solution)/shard_map/ppermute | solution.py:296
  194.7 10.4 %collective-permute-start.15 = (bf16[32,2048]{1,0:T(8,128)(2,1)S(1)}, bf16[32,2048]{1,0:T(8,128)(2,1)S(1)}, u32[]{:S(2)}, u32[]{:S(2)}) collective-permute-start(bf16[32,2048]{1,0:T(8,128)(2,1)S(1)} %get-tuple-element.89), channel_id=1, source_target_pairs={{0,16},{8,24},{16,0},{24,8},{1,17},{9,25},{17,1},{25,9},{2,18},{10... | collective-permute-start | bytes 393224 | tf_op jit(solution)/shard_map/ppermute | solution.py:296
  194.7 10.4 %collective-permute-start.14 = (bf16[32,2048]{1,0:T(8,128)(2,1)S(1)}, bf16[32,2048]{1,0:T(8,128)(2,1)S(1)}, u32[]{:S(2)}, u32[]{:S(2)}) collective-permute-start(bf16[32,2048]{1,0:T(8,128)(2,1)S(1)} %get-tuple-element.90), channel_id=1, source_target_pairs={{0,8},{8,0},{16,24},{24,16},{1,9},{9,1},{17,25},{25,17},{2,10},{10... | collective-permute-start | bytes 393224 | tf_op jit(solution)/shard_map/ppermute | solution.py:296
  205.2 3.6 %collective-permute-start.17 = (bf16[4,32,2048]{2,1,0:T(8,128)(2,1)S(1)}, bf16[4,32,2048]{2,1,0:T(8,128)(2,1)S(1)}, u32[]{:S(2)}, u32[]{:S(2)}) collective-permute-start(bf16[4,32,2048]{2,1,0:T(8,128)(2,1)S(1)} %pad_maximum_fusion.1), channel_id=1, source_target_pairs={{0,4},{4,0},{1,5},{5,1},{2,6},{6,2},{3,7},{7,3},{8,12},{12,8},{9,1... | collective-permute-start | bytes 1572872 | tf_op jit(solution)/shard_map/ppermute | solution.py:300
  205.3 15.1 %collective-permute-start.22 = (bf16[4,32,2048]{2,1,0:T(8,128)(2,1)S(1)}, bf16[4,32,2048]{2,1,0:T(8,128)(2,1)S(1)}, u32[]{:S(2)}, u32[]{:S(2)}) collective-permute-start(bf16[4,32,2048]{2,1,0:T(8,128)(2,1)S(1)} %pad_maximum_fusion.1), channel_id=1, source_target_pairs={{0,1},{1,0},{2,3},{3,2},{4,5},{5,4},{6,7},{7,6},{8,9},{9,8},{10,11... | collective-permute-start | bytes 1572872 | tf_op jit(solution)/shard_map/ppermute | solution.py:299
  207.0 25.2 %collective-permute-start.23 = (bf16[4,32,2048]{2,1,0:T(8,128)(2,1)S(1)}, bf16[4,32,2048]{2,1,0:T(8,128)(2,1)S(1)}, u32[]{:S(2)}, u32[]{:S(2)}) collective-permute-start(bf16[4,32,2048]{2,1,0:T(8,128)(2,1)S(1)} %pad_maximum_fusion.1), channel_id=1, source_target_pairs={{0,2},{1,3},{2,0},{3,1},{4,6},{5,7},{6,4},{7,5},{8,10},{9,11},{10,... | collective-permute-start | bytes 1572872 | tf_op jit(solution)/shard_map/ppermute | solution.py:299
  207.2 25.1 %collective-permute-start.24 = (bf16[4,32,2048]{2,1,0:T(8,128)(2,1)S(1)}, bf16[4,32,2048]{2,1,0:T(8,128)(2,1)S(1)}, u32[]{:S(2)}, u32[]{:S(2)}) collective-permute-start(bf16[4,32,2048]{2,1,0:T(8,128)(2,1)S(1)} %pad_maximum_fusion.1), channel_id=1, source_target_pairs={{0,3},{1,2},{2,1},{3,0},{4,7},{5,6},{6,5},{7,4},{8,11},{9,10},{10,... | collective-permute-start | bytes 1572872 | tf_op jit(solution)/shard_map/ppermute | solution.py:299
  211.9 36.9 %collective-permute-start.20 = (bf16[64,1024]{1,0:T(8,128)(2,1)S(1)}, bf16[64,1024]{1,0:T(8,128)(2,1)S(1)}, u32[]{:S(2)}, u32[]{:S(2)}) collective-permute-start(bf16[64,1024]{1,0:T(8,128)(2,1)S(1)} %convolution_convert_fusion.6), channel_id=1, source_target_pairs={{0,24},{8,16},{16,8},{24,0},{1,25},{9,17},{17,9},{25,1},{2,26},{10... | collective-permute-start | bytes 393224 | tf_op jit(solution)/shard_map/ppermute | solution.py:310
  217.3 33.6 %collective-permute-start.19 = (bf16[64,1024]{1,0:T(8,128)(2,1)S(1)}, bf16[64,1024]{1,0:T(8,128)(2,1)S(1)}, u32[]{:S(2)}, u32[]{:S(2)}) collective-permute-start(bf16[64,1024]{1,0:T(8,128)(2,1)S(1)} %convolution_convert_fusion.7), channel_id=1, source_target_pairs={{0,16},{8,24},{16,0},{24,8},{1,17},{9,25},{17,1},{25,9},{2,18},{10... | collective-permute-start | bytes 393224 | tf_op jit(solution)/shard_map/ppermute | solution.py:310
  220.4 30.5 %collective-permute-start.18 = (bf16[64,1024]{1,0:T(8,128)(2,1)S(1)}, bf16[64,1024]{1,0:T(8,128)(2,1)S(1)}, u32[]{:S(2)}, u32[]{:S(2)}) collective-permute-start(bf16[64,1024]{1,0:T(8,128)(2,1)S(1)} %convolution_convert_fusion.8), channel_id=1, source_target_pairs={{0,8},{8,0},{16,24},{24,16},{1,9},{9,1},{17,25},{25,17},{2,10},{10... | collective-permute-start | bytes 393224 | tf_op jit(solution)/shard_map/ppermute | solution.py:310
  232.2 1.9 collective-permute-start.25
  232.3 2.6 collective-permute-start.26
  234.1 1.9 collective-permute-start.27
  239.3 14.8 %collective-permute-start.30 = (bf16[192,1024]{1,0:T(8,128)(2,1)S(1)}, bf16[192,1024]{1,0:T(8,128)(2,1)S(1)}, u32[]{:S(2)}, u32[]{:S(2)}) collective-permute-start(bf16[192,1024]{1,0:T(8,128)(2,1)S(1)} %convolution_convert_fusion.3), channel_id=1, source_target_pairs={{0,24},{8,16},{16,8},{24,0},{1,25},{9,17},{17,9},{25,1},{2,26},{10... | collective-permute-start | bytes 1179656 | tf_op jit(solution)/shard_map/ppermute | solution.py:310
  244.8 30.9 %collective-permute-start.29 = (bf16[192,1024]{1,0:T(8,128)(2,1)S(1)}, bf16[192,1024]{1,0:T(8,128)(2,1)S(1)}, u32[]{:S(2)}, u32[]{:S(2)}) collective-permute-start(bf16[192,1024]{1,0:T(8,128)(2,1)S(1)} %convolution_convert_fusion.4), channel_id=1, source_target_pairs={{0,16},{8,24},{16,0},{24,8},{1,17},{9,25},{17,1},{25,9},{2,18},{10... | collective-permute-start | bytes 1179656 | tf_op jit(solution)/shard_map/ppermute | solution.py:310
  248.8 26.9 %collective-permute-start.28 = (bf16[192,1024]{1,0:T(8,128)(2,1)}, bf16[192,1024]{1,0:T(8,128)(2,1)}, u32[]{:S(2)}, u32[]{:S(2)}) collective-permute-start(bf16[192,1024]{1,0:T(8,128)(2,1)} %convolution_convert_fusion.5), channel_id=1, source_target_pairs={{0,8},{8,0},{16,24},{24,16},{1,9},{9,1},{17,25},{25,17},{2,10},{10... | collective-permute-start | bytes 1179656 | tf_op jit(solution)/shard_map/ppermute | solution.py:310
  254.0 25.1 %collective-permute-start.21 = (bf16[32,1024]{1,0:T(8,128)(2,1)S(1)}, bf16[32,1024]{1,0:T(8,128)(2,1)S(1)}, u32[]{:S(2)}, u32[]{:S(2)}) collective-permute-start(bf16[32,1024]{1,0:T(8,128)(2,1)S(1)} %split.17), channel_id=1, source_target_pairs={{0,4},{4,0},{1,5},{5,1},{2,6},{6,2},{3,7},{7,3},{8,12},{12,8},{9,1... | collective-permute-start | bytes 196616 | tf_op jit(solution)/shard_map/ppermute | solution.py:315
  279.0 1.5 collective-permute-start.31
  (9 other events, 17.3 us)
where the time goes:
time: 283 us; the launch traced here: 282 us
  waiting for transfers between devices  140 us (49%)
  matrix products  59.4 us (21%)
  starting transfers between devices  42.8 us (15%)
  local copies, waits for them, and re-layouts  21 us (7%)
  Pallas kernels  10.1 us (4%)
  other arithmetic  6.87 us (2%)
    ppermute x3, waiting for transfers between devices, local(): product = lax.ppermute(product.astype(jnp.float16), 'z', plane_pairs[k])  46.4 us
    ppermute x3, waiting for transfers between devices, local(): lax.ppermute(blocks[k], 'z', plane_pairs[k])  35.8 us
    dot_general x8, matrix products, local(): product = jnp.dot(block, output_weights, preferred_element_type=jnp.float32)  25.6 us
    ppermute x6, waiting for transfers between devices, local(): product = lax.ppermute(product.astype(jnp.bfloat16), 'z', plane_pairs[k])  21.7 us
    dot_general x4, matrix products, local(): product = jnp.dot(block, weights, preferred_element_type=jnp.float32)  18.4 us
    unnamed x52, local copies, waits for them, and re-layouts  15.2 us
    ppermute x3, waiting for transfers between devices, local(): lax.ppermute(heads, 'tp', tp_pairs[j])  9.61 us
    ppermute x6, starting transfers between devices, local(): product = lax.ppermute(product.astype(jnp.bfloat16), 'z', plane_pairs[k])  9.08 us
  transfers between devices with their start and end apart: 34, of which 17 were waited for; matrix products, arithmetic and copies ran while one was open for 16% of the time, Pallas kernels for 1%

commit v1 on v0

--- a/solution.py
+++ b/solution.py
@@ -1,3 +1,5 @@
+import functools
+
 import jax
 import jax.numpy as jnp
 from jax import lax
@@ -12,11 +14,9 @@
 rope_theta = 1000000.0
 low_rank_scale = 0.5
 epsilon = 1e-06
-CHUNKS = 1
-
-
-def GROUPS(count):
-    return [[0]] + [list(range(1, count))]
+CHUNKS = 2
+WIRE = jnp.float16
+VMEM_BYTES = 60 * 1024 * 1024
 
 
 def merge_block(base, down, up):
@@ -70,7 +70,7 @@
         cost_estimate=pl.CostEstimate(
             flops=2 * depth * rank * width, bytes_accessed=5 * depth * width, transcendentals=0
         ),
-        compiler_params=pltpu.CompilerParams(vmem_limit_bytes=32 * 1024 * 1024),
+        compiler_params=pltpu.CompilerParams(vmem_limit_bytes=VMEM_BYTES),
         name="merge_output",
     )(slot, base, flipped(down), up)
 
@@ -104,7 +104,7 @@
         cost_estimate=pl.CostEstimate(
             flops=3 * depth * rank * width, bytes_accessed=6 * depth * width, transcendentals=0
         ),
-        compiler_params=pltpu.CompilerParams(vmem_limit_bytes=32 * 1024 * 1024),
+        compiler_params=pltpu.CompilerParams(vmem_limit_bytes=VMEM_BYTES),
         name="merge_inputs",
     )(slot, *bases, *[flipped(d) for d in downs], *ups)
 
@@ -186,6 +186,46 @@
         "bskgt,btkd->bskgd", new_weights, values_new, preferred_element_type=jnp.float32
     )
     return mixture.astype(jnp.bfloat16).reshape(seq_count * step_count, head_count * head_dim)
+
+
+def product_kernel(counts, waits, *refs):
+    total = sum(counts)
+    ins, weight_ref = refs[:total], refs[total]
+    outs, rows_ref = refs[total + 1 + waits : -1], refs[-1]
+
+    @pl.when(pl.program_id(0) == 0)
+    def _():
+        place = 0
+        for ref in ins:
+            rows_ref[place : place + ref.shape[0], :] = ref[...]
+            place += ref.shape[0]
+
+    product = jnp.dot(rows_ref[...], weight_ref[...], preferred_element_type=jnp.float32)
+    place = 0
+    for out_ref in outs:
+        out_ref[...] = product[place : place + out_ref.shape[0]].astype(out_ref.dtype)
+        place += out_ref.shape[0]
+
+
+def products(groups, weights, kind, after=()):
+    depth, width = weights.shape
+    tile = 256 if width % 256 == 0 else 128
+    counts = [len(group) for group in groups]
+    blocks = [block for group in groups for block in group]
+    sizes = [sum(block.shape[0] for block in group) for group in groups]
+    return pl.pallas_call(
+        functools.partial(product_kernel, counts, len(after)),
+        grid=(width // tile,),
+        in_specs=[pl.BlockSpec(block.shape, lambda i: (0, 0)) for block in blocks]
+        + [pl.BlockSpec((depth, tile), lambda i: (0, i))]
+        + [pl.BlockSpec(memory_space=pl.ANY)] * len(after),
+        out_specs=[pl.BlockSpec((size, tile), lambda i: (0, i)) for size in sizes],
+        out_shape=[jax.ShapeDtypeStruct((size, width), kind) for size in sizes],
+        scratch_shapes=[pltpu.VMEM((sum(sizes), depth), jnp.bfloat16)],
+        compiler_params=pltpu.CompilerParams(vmem_limit_bytes=40 * 1024 * 1024),
+        cost_estimate=pl.CostEstimate(flops=1, bytes_accessed=1, transcendentals=0),
+        name="products",
+    )(*blocks, weights, *after)
 
 
 def by_xor(blocks, index):
@@ -228,7 +268,6 @@
     seqs, steps, width = states.shape
     rows = seqs * steps
 
-    blocks = normed_blocks(z, states.reshape(rows, width), norm_gain, planes)
     joined = merge_inputs(
         adapter_layer,
         (query_base, key_base, value_base),
@@ -237,11 +276,15 @@
         cores,
         cols,
     )
-    (joined, output_base, *blocks) = lax.optimization_barrier((joined, output_base, *blocks))
+    joined, states = lax.optimization_barrier((joined, states))
     joined = joined.reshape(cores * cols * depth, -1)
     weights = lax.all_to_all(joined, ("core", "tp"), 0, 0, tiled=True)
-    mine = [lax.ppermute(blocks[k], "z", plane_pairs[k]) for k in range(1, planes)]
-    mine = [blocks[0]] + mine
+    blocks = normed_blocks(z, states.reshape(rows, width), norm_gain, planes)
+    (output_base, *blocks) = lax.optimization_barrier((output_base, *blocks))
+    mine = {0: blocks[0]}
+    for k in reversed(range(1, planes)):
+        mine[k] = lax.ppermute(blocks[k], "z", plane_pairs[k])
+    mine = [mine[k] for k in range(planes)]
     other = [lax.ppermute(block, "core", core_pairs) for block in mine]
     merged = merge_output(adapter_layer, output_base, output_down, output_up, cores, cols)
     merged = merged.reshape(cores * cols * depth, -1)
@@ -250,22 +293,27 @@
     output_weights = lax.all_to_all(merged, ("core", "tp"), 0, 0, tiled=True)
 
     half_q = HQ * DH // (cols * cores)
-    kv_cols = KVH * DH // cols
     part = rows // CHUNKS
     seq_part = seqs // CHUNKS
-    outs = []
+    sums = []
+    sent = list(reversed(range(1, planes)))
+    before = []
     for h in range(CHUNKS):
         sl = slice(h * part, (h + 1) * part)
-        total = None
-        for k in list(range(1, planes)) + [0]:
-            block = jnp.concatenate((mine[k][sl], other[k][sl]))
-            product = jnp.dot(block, weights, preferred_element_type=jnp.float32)
-            if k:
-                product = lax.ppermute(product.astype(jnp.float16), "z", plane_pairs[k])
-                product = product.astype(jnp.float32)
-            total = product if total is None else total + product
-        if h == 0:
-            total, output_weights = lax.optimization_barrier((total, output_weights))
+        pieces = [[mine[k][sl], other[k][sl]] for k in sent]
+        terms = products(pieces, weights, jnp.float32, before[:1])
+        before = terms
+        terms = [lax.ppermute(x.astype(WIRE), "z", plane_pairs[k]) for k, x in zip(sent, terms)]
+        sums.append(terms)
+    attended = None
+    crossing = []
+    for h in range(CHUNKS):
+        sl = slice(h * part, (h + 1) * part)
+        waits = (before[0], output_weights) if attended is None else (attended,)
+        terms = sums[h]
+        (total,) = products([[mine[0][sl], other[0][sl]]], weights, jnp.float32, waits)
+        for term in terms:
+            total = total + term.astype(jnp.float32)
         here = total[:part]
         there = lax.ppermute(total[part:], "core", core_pairs)
         low = jnp.where(core == 0, here, there)
@@ -284,38 +332,38 @@
             queries, keys_new, values_new, cache_keys[ss], cache_values[ss], lengths
         )
 
-        attended = attended.reshape(cols, part // cols, -1)
+        quarters = attended.reshape(cols, part // cols, -1)
         turned = []
         for j in range(cols):
-            block = lax.dynamic_index_in_dim(attended, t ^ j, 0, keepdims=False)
+            block = lax.dynamic_index_in_dim(quarters, t ^ j, 0, keepdims=False)
             turned.append(lax.ppermute(block, "tp", tp_pairs[j]) if j else block)
         turned = jnp.stack(turned)
         heads = []
         for k in range(planes):
             block = lax.dynamic_index_in_dim(turned, t ^ z ^ k, 0, keepdims=False)
             heads.append(lax.ppermute(block, "z", plane_pairs[k]) if k else block)
-        heads = jnp.stack(heads)
-        piece = part // cols
-        gathered = [lax.ppermute(heads, "tp", tp_pairs[j]) if j else heads for j in range(cols)]
+        held = jnp.stack(heads)
+        gathered = [lax.ppermute(held, "tp", tp_pairs[j]) if j else held for j in range(cols)]
         crossed = [lax.ppermute(block, "core", core_pairs) for block in gathered]
-        lows, highs = [], []
-        for group in GROUPS(cols):
-            total = None
-            for k in list(range(1, planes)) + [0]:
-                block = jnp.concatenate(
-                    [gathered[j][k] for j in group] + [crossed[j][k] for j in group]
-                )
-                product = jnp.dot(block, output_weights, preferred_element_type=jnp.float32)
-                if k:
-                    product = lax.ppermute(product.astype(jnp.bfloat16), "z", plane_pairs[k])
-                    product = product.astype(jnp.float32)
-                total = product if total is None else total + product
-            total = total.astype(jnp.bfloat16)
-            here, there = jnp.split(total, 2)
-            there = lax.ppermute(there, "core", core_pairs)
-            lows.append(jnp.where(core == 0, here, there))
-            highs.append(jnp.where(core == 0, there, here))
-        low, high = jnp.concatenate(lows), jnp.concatenate(highs)
+        pieces = [
+            [side[j][k] for side in (gathered, crossed) for j in range(cols)]
+            for k in range(planes)
+        ]
+        terms = products([pieces[k] for k in sent], output_weights, jnp.bfloat16)
+        crossing.append(
+            (pieces[0], terms, [lax.ppermute(x, "z", plane_pairs[k]) for k, x in zip(sent, terms)])
+        )
+    outs = []
+    after = crossing[-1][1]
+    for own, _, terms in crossing:
+        (total,) = products([own], output_weights, jnp.float32, after[:1])
+        for term in terms:
+            total = total + term.astype(jnp.float32)
+        total = total.astype(jnp.bfloat16)
+        here = total[:part]
+        there = lax.ppermute(total[part:], "core", core_pairs)
+        low = jnp.where(core == 0, here, there)
+        high = jnp.where(core == 0, there, here)
         full = jnp.concatenate((low, high), 1).reshape(cols, part // cols, -1)
         full = jnp.stack(by_xor([full[j] for j in range(cols)], t))
         outs.append(full.reshape(seq_part, steps, -1))

time: 283 us -> 261 us (0.922)
  matrix products: 59.4 us -> 8.98 us
  Pallas kernels: 10.1 us -> 53.7 us
  waiting for transfers between devices: 140 us -> 96.9 us
  starting transfers between devices: 42.8 us -> 61.1 us
  other arithmetic: 6.87 us -> 12.5 us
  local copies, waits for them, and re-layouts: 21 us -> 25.1 us
    ppermute x17 -> x21, waiting for transfers between devices: 115 us -> 64.6 us  [the longest x6 22.5 us: local(): lax.ppermute(x, 'z', plane_pairs[k])]
    dot_general x12 -> x0, matrix products: 44.1 us -> none  [the longest x8 25.6 us: local(): product = jnp.dot(block, output_weights, preferred_element_type=jnp.float32)]
    pallas_call x0 -> x8, Pallas kernels: none -> 37.1 us  [products(): pl.pallas_call(functools.partial(product_kernel, counts, len(after)), gri...]
    slice x0 -> x6, local copies, waits for them, and re-layouts: none -> 18.2 us  [the longest x1 8.45 us: local(): cache_keys[ss]]
    all_to_all x1, waiting for transfers between devices: 0.01 us -> 16.4 us  [local(): output_weights = lax.all_to_all(merged, ('core', 'tp'), 0, 0, tiled=True)]
    unnamed x52 -> x24, local copies, waits for them, and re-layouts: 15.2 us -> 3.52 us
    ppermute x3 -> x6, waiting for transfers between devices: 8.49 us -> 0.22 us  [local(): heads.append(lax.ppermute(block, 'z', plane_pairs[k]) if k else block)]
    ppermute x17 -> x21, starting transfers between devices: 23.4 us -> 31.2 us  [the longest x6 10.2 us: local(): lax.ppermute(x.astype(WIRE), 'z', plane_pairs[k])]
  transfers between devices with their start and end apart: 34 -> 51, of which waited for: 17 -> 19; matrix products, arithmetic and copies ran while one was open for 16% -> 15% of each run, Pallas kernels for 1% -> 18%
where the time goes in v1:
time: 261 us; the launch traced here: 260 us
  waiting for transfers between devices  96.9 us (37%)
  starting transfers between devices  61.1 us (23%)
  Pallas kernels  53.7 us (21%)
  local copies, waits for them, and re-layouts  25.1 us (10%)
  other arithmetic  12.5 us (5%)
  matrix products  8.98 us (3%)
    pallas_call x8, Pallas kernels, products(): pl.pallas_call(functools.partial(product_kernel, counts, len(after)), gri...  37.1 us
    ppermute x6, waiting for transfers between devices, local(): lax.ppermute(x, 'z', plane_pairs[k])  22.5 us
    ppermute x3, waiting for transfers between devices, local(): mine[k] = lax.ppermute(blocks[k], 'z', plane_pairs[k])  21.6 us
    all_to_all x1, waiting for transfers between devices, local(): output_weights = lax.all_to_all(merged, ('core', 'tp'), 0, 0, tiled=True)  16.4 us
    ppermute x6, waiting for transfers between devices, local(): lax.ppermute(x.astype(WIRE), 'z', plane_pairs[k])  12.8 us
    ppermute x6, starting transfers between devices, local(): lax.ppermute(x.astype(WIRE), 'z', plane_pairs[k])  10.2 us
    ppermute x6, starting transfers between devices, local(): heads.append(lax.ppermute(block, 'z', plane_pairs[k]) if k else block)  10.1 us
    all_to_all x1, waiting for transfers between devices, local(): weights = lax.all_to_all(joined, ('core', 'tp'), 0, 0, tiled=True)  9.4 us
  transfers between devices with their start and end apart: 51, of which 19 were waited for; matrix products, arithmetic and copies ran while one was open for 15% of the time, Pallas kernels for 18%

profile of v1, /device:TPU:0, one launch (start us, length us, event | category | flops | bytes accessed | tf_op | source)
XLA Modules:
  0.0 259.9 jit_solution(9867309317870566399)
XLA Ops:
  0.7 6.6 %merge_inputs.1 = bf16[2,4,256,1280]{3,2,1,0:T(8,128)(2,1)} custom-call(s32[1]{0:T(128)S(6)} %copy.123.slot_ref, bf16[256,8192]{1,0:T(8,128)(2,1)} %qb_ref.1, bf16[256,1024]{1,0:T(8,128)(2,1)} %kb_ref.1, bf16[256,1024]{1,0:T(8,128)(2,1)} %vb_ref.1, bf16[4,64,256]{2,1,0:T(8,128)(2,1)} %bitcast.307, bf16[4,64,256]{2,1,0:T(8,128)(2,1)} %bitcast.308, ...), custom_call_target="tpu_custom_call" | custom-call | flops 402653184 | bytes 12582912 | tf_op jit(solution)/shard_map/merge_inputs/pallas_call | solution.py:100
  7.2 5.3 %all-to-all-start = ((bf16[8,256,1280]{2,1,0:T(8,128)(2,1)}), bf16[8,256,1280]{2,1,0:T(8,128)(2,1)}, u32[]{:S(2)}, u32[]{:S(2)}) async-start(bf16[8,256,1280]{2,1,0:T(8,128)(2,1)} %bitcast.301), calls=%async_computation | async-start | bytes 10485760 | tf_op jit(solution)/shard_map/all_to_all | solution.py:281
  12.6 2.1 reshape.193.x_ref
  14.6 4.4 %normed_blocks.1 = (bf16[128,2048]{1,0:T(8,128)(2,1)}, bf16[128,2048]{1,0:T(8,128)(2,1)}, bf16[128,2048]{1,0:T(8,128)(2,1)}, bf16[128,2048]{1,0:T(8,128)(2,1)}) custom-call(s32[1]{0:T(128)} %bitcast.5.z_ref, bf16[128,8192]{1,0:T(8,128)(2,1)} %reshape.193.x_ref, f32[1,8192]{1,0:T(1,128)} %bitcast.317), custom_call_target="tpu_custom_call" | custom-call | flops 6291456 | bytes 4194304 | tf_op jit(solution)/shard_map/normed_blocks/pallas_call | solution.py:137
  19.0 2.5 collective-permute-start
  21.5 2.6 collective-permute-start.1
  24.1 8.5 %fusion.76 = (bf16[16,512,2,128]{3,2,1,0:T(2,128)(2,1)}, bf16[16,512,2,128]{3,2,1,0:T(2,128)(2,1)}) fusion(bf16[32,512,2,128]{3,2,1,0:T(2,128)(2,1)} %param.34), kind=kLoop, calls=%fused_computation.239 | loop fusion | bytes 16777216 | tf_op jit(solution)/shard_map/slice | solution.py:332
  32.6 5.7 %merge_output.1 = bf16[2,4,256,1024]{3,2,1,0:T(8,128)(2,1)} custom-call(s32[1]{0:T(128)S(6)} %copy.123.slot_ref, bf16[256,8192]{1,0:T(8,128)(2,1)} %base_ref, bf16[4,64,256]{2,1,0:T(8,128)(2,1)} %bitcast.310, bf16[4,64,8192]{2,1,0:T(8,128)(2,1)} %up_ref.1), custom_call_target="tpu_custom_call" | custom-call | flops 268435456 | bytes 10485760 | tf_op jit(solution)/shard_map/merge_output/pallas_call | solution.py:66
  38.3 6.6 %collective-permute-done = bf16[128,2048]{1,0:T(8,128)(2,1)S(1)} collective-permute-done((bf16[128,2048]{1,0:T(8,128)(2,1)}, bf16[128,2048]{1,0:T(8,128)(2,1)S(1)}, u32[]{:S(2)}, u32[]{:S(2)}) %collective-permute-start) | collective-permute-done | bytes 524320 | tf_op jit(solution)/shard_map/ppermute | solution.py:286
  44.9 15.0 %collective-permute-done.1 = bf16[128,2048]{1,0:T(8,128)(2,1)S(1)} collective-permute-done((bf16[128,2048]{1,0:T(8,128)(2,1)}, bf16[128,2048]{1,0:T(8,128)(2,1)S(1)}, u32[]{:S(2)}, u32[]{:S(2)}) %collective-permute-start.1) | collective-permute-done | bytes 524320 | tf_op jit(solution)/shard_map/ppermute | solution.py:286
  60.6 1.9 collective-permute-done.5
  62.7 9.4 %all-to-all-done = bf16[8,256,1280]{2,1,0:T(8,128)(2,1)} async-done(((bf16[8,256,1280]{2,1,0:T(8,128)(2,1)}), bf16[8,256,1280]{2,1,0:T(8,128)(2,1)}, u32[]{:S(2)}, u32[]{:S(2)}) %all-to-all-start) | async-done | bytes 5242912 | tf_op jit(solution)/shard_map/all_to_all | solution.py:281
  72.1 4.7 %all-to-all-start.1 = ((bf16[8,256,1024]{2,1,0:T(8,128)(2,1)}), bf16[8,256,1024]{2,1,0:T(8,128)(2,1)}, u32[]{:S(2)}, u32[]{:S(2)}) async-start(bf16[8,256,1024]{2,1,0:T(8,128)(2,1)} %bitcast.302), calls=%async_computation.1 | async-start | bytes 8388608 | tf_op jit(solution)/shard_map/all_to_all | solution.py:293
  80.2 8.4 %fusion.77 = (bf16[16,512,2,128]{3,2,1,0:T(2,128)(2,1)}, bf16[16,512,2,128]{3,2,1,0:T(2,128)(2,1)}) fusion(bf16[32,512,2,128]{3,2,1,0:T(2,128)(2,1)} %param.35), kind=kLoop, calls=%fused_computation.240 | loop fusion | bytes 16777216 | tf_op jit(solution)/shard_map/slice | solution.py:332
  89.8 5.6 %products.8 = (f32[128,1280]{1,0:T(8,128)S(1)}, f32[128,1280]{1,0:T(8,128)S(1)}, f32[128,1280]{1,0:T(8,128)S(1)}) custom-call(bf16[64,2048]{1,0:T(8,128)(2,1)S(1)} %get-tuple-element.220.refs_0_, bf16[64,2048]{1,0:T(8,128)(2,1)S(1)} %get-tuple-element.105.refs_1_, bf16[64,2048]{1,0:T(8,128)(2,1)S(1)} %get-tuple-element.218.refs_2_, ...), custom_call_target="tpu_custom_call" | custom-call | flops 1 | bytes 1 | tf_op jit(solution)/shard_map/products/pallas_call | solution.py:216
  97.7 4.8 %collective-permute-start.7 = (f16[128,1280]{1,0:T(8,128)(2,1)}, f16[128,1280]{1,0:T(8,128)(2,1)}, u32[]{:S(2)}, u32[]{:S(2)}) collective-permute-start(f16[128,1280]{1,0:T(8,128)(2,1)} %convert_element_type.106), channel_id=1, source_target_pairs={{0,24},{8,16},{16,8},{24,0},{1,25},{9,17},{17,9},{25,1},{2,26},{10... | collective-permute-start | bytes 983048 | tf_op jit(solution)/shard_map/ppermute | solution.py:306
  103.1 5.7 %products.9 = (f32[128,1280]{1,0:T(8,128)S(1)}, f32[128,1280]{1,0:T(8,128)S(1)}, f32[128,1280]{1,0:T(8,128)S(1)}) custom-call(bf16[64,2048]{1,0:T(8,128)(2,1)S(1)} %get-tuple-element.219.refs_0_, bf16[64,2048]{1,0:T(8,128)(2,1)S(1)} %get-tuple-element.106.refs_1_, bf16[64,2048]{1,0:T(8,128)(2,1)S(1)} %get-tuple-element.217.refs_2_, ...), custom_call_target="tpu_custom_call" | custom-call | flops 1 | bytes 1 | tf_op jit(solution)/shard_map/products/pallas_call | solution.py:216
  108.9 16.4 %all-to-all-done.1 = bf16[8,256,1024]{2,1,0:T(8,128)(2,1)} async-done(((bf16[8,256,1024]{2,1,0:T(8,128)(2,1)}), bf16[8,256,1024]{2,1,0:T(8,128)(2,1)}, u32[]{:S(2)}, u32[]{:S(2)}) %all-to-all-start.1) | async-done | bytes 4194336 | tf_op jit(solution)/shard_map/all_to_all | solution.py:293
  125.3 4.7 %products.10 = f32[128,1280]{1,0:T(8,128)S(1)} custom-call(bf16[64,2048]{1,0:T(8,128)(2,1)S(1)} %get-tuple-element.214.refs_0_, bf16[64,2048]{1,0:T(8,128)(2,1)S(1)} %get-tuple-element.93.refs_1_, bf16[2048,1280]{1,0:T(8,128)(2,1)} %bitcast.4.refs_6_.refs_2_, f32[128,1280]{1,0:T(8,128)S(1)} %get-tuple-element.59.refs_3_, ...), custom_call_target="tpu_custom_call" | custom-call | flops 1 | bytes 1 | tf_op jit(solution)/shard_map/products/pallas_call | solution.py:216
  132.9 1.9 collective-permute-start.26
  134.8 2.5 collective-permute-start.24
  138.9 1.4 copy-done.1
  140.3 1.6 bitcast_reduce_fusion.1
  148.3 4.9 %products.11 = f32[128,1280]{1,0:T(8,128)S(1)} custom-call(bf16[64,2048]{1,0:T(8,128)(2,1)S(1)} %get-tuple-element.213.refs_0_, bf16[64,2048]{1,0:T(8,128)(2,1)S(1)} %get-tuple-element.94.refs_1_, bf16[2048,1280]{1,0:T(8,128)(2,1)} %bitcast.4.refs_6_.refs_2_, bf16[64,2048]{1,0:T(8,128)(2,1)S(1)} %reshape.199.refs_3_), custom_call_target="tpu_custom_call" | custom-call | flops 1 | bytes 1 | tf_op jit(solution)/shard_map/products/pallas_call | solution.py:216
  153.3 1.5 collective-permute-start.11
  154.8 11.6 %collective-permute-done.25 = f16[128,1280]{1,0:T(8,128)(2,1)S(1)} collective-permute-done((f16[128,1280]{1,0:T(8,128)(2,1)S(1)}, f16[128,1280]{1,0:T(8,128)(2,1)S(1)}, u32[]{:S(2)}, u32[]{:S(2)}) %collective-permute-start.25) | collective-permute-done | bytes 327712 | tf_op jit(solution)/shard_map/ppermute | solution.py:306
  166.7 2.7 %collective-permute-start.16 = (bf16[16,2048]{1,0:T(8,128)(2,1)S(1)}, bf16[16,2048]{1,0:T(8,128)(2,1)S(1)}, u32[]{:S(2)}, u32[]{:S(2)}) collective-permute-start(bf16[16,2048]{1,0:T(8,128)(2,1)S(1)} %get-tuple-element.145), channel_id=1, source_target_pairs={{0,24},{8,16},{16,8},{24,0},{1,25},{9,17},{17,9},{25,1},{2,26},{10... | collective-permute-start | bytes 196616 | tf_op jit(solution)/shard_map/ppermute | solution.py:344
  169.4 1.7 collective-permute-start.14
  172.4 1.4 copy-done
  173.8 1.6 bitcast_reduce_fusion
  179.6 1.5 collective-permute-start.30
  183.3 1.5 collective-permute-start.19
  188.2 2.2 collective-permute-start.32
  190.4 3.0 %collective-permute-done.19 = bf16[4,16,2048]{2,1,0:T(8,128)(2,1)S(1)} collective-permute-done((bf16[4,16,2048]{2,1,0:T(8,128)(2,1)S(1)}, bf16[4,16,2048]{2,1,0:T(8,128)(2,1)S(1)}, u32[]{:S(2)}, u32[]{:S(2)}) %collective-permute-start.19) | collective-permute-done | bytes 262176 | tf_op jit(solution)/shard_map/ppermute | solution.py:346
  193.4 2.6 %collective-permute-start.31 = (bf16[16,2048]{1,0:T(8,128)(2,1)S(1)}, bf16[16,2048]{1,0:T(8,128)(2,1)S(1)}, u32[]{:S(2)}, u32[]{:S(2)}) collective-permute-start(bf16[16,2048]{1,0:T(8,128)(2,1)S(1)} %get-tuple-element.186), channel_id=1, source_target_pairs={{0,24},{8,16},{16,8},{24,0},{1,25},{9,17},{17,9},{25,1},{2,26},{10... | collective-permute-start | bytes 196616 | tf_op jit(solution)/shard_map/ppermute | solution.py:344
  196.0 2.5 collective-permute-done.18
  199.8 1.4 collective-permute-start.36
  203.5 4.5 %products.14 = (bf16[128,1024]{1,0:T(8,128)(2,1)S(1)}, bf16[128,1024]{1,0:T(8,128)(2,1)S(1)}, bf16[128,1024]{1,0:T(8,128)(2,1)S(1)}) custom-call(bf16[16,2048]{1,0:T(8,128)(2,1)S(1)} %collective-permute-done.16.refs_0_, bf16[16,2048]{1,0:T(8,128)(2,1)S(1)} %get-tuple-element.143.refs_1_, bf16[16,2048]{1,0:T(8,128)(2,1)S(1)} %get-tuple-element.139.refs_2_, ...), custom_call_target="tpu_custom_call" | custom-call | flops 1 | bytes 1 | tf_op jit(solution)/shard_map/products/pallas_call | solution.py:216
  208.0 2.7 %collective-permute-start.41 = (bf16[128,1024]{1,0:T(8,128)(2,1)S(1)}, bf16[128,1024]{1,0:T(8,128)(2,1)S(1)}, u32[]{:S(2)}, u32[]{:S(2)}) collective-permute-start(bf16[128,1024]{1,0:T(8,128)(2,1)S(1)} %get-tuple-element.66), channel_id=1, source_target_pairs={{0,24},{8,16},{16,8},{24,0},{1,25},{9,17},{17,9},{25,1},{2,26},{10... | collective-permute-start | bytes 786440 | tf_op jit(solution)/shard_map/ppermute | solution.py:354
  210.7 1.8 collective-permute-start.43
  212.6 2.2 collective-permute-done.35
  217.9 4.5 %products.12 = (bf16[128,1024]{1,0:T(8,128)(2,1)S(1)}, bf16[128,1024]{1,0:T(8,128)(2,1)S(1)}, bf16[128,1024]{1,0:T(8,128)(2,1)S(1)}) custom-call(bf16[16,2048]{1,0:T(8,128)(2,1)S(1)} %collective-permute-done.31.refs_0_, bf16[16,2048]{1,0:T(8,128)(2,1)S(1)} %get-tuple-element.182.refs_1_, bf16[16,2048]{1,0:T(8,128)(2,1)S(1)} %get-tuple-element.178.refs_2_, ...), custom_call_target="tpu_custom_call" | custom-call | flops 1 | bytes 1 | tf_op jit(solution)/shard_map/products/pallas_call | solution.py:216
  222.4 3.6 %products.13 = f32[128,1024]{1,0:T(8,128)S(1)} custom-call(bf16[16,2048]{1,0:T(8,128)(2,1)S(1)} %bitcast.293, bf16[16,2048]{1,0:T(8,128)(2,1)S(1)} %get-tuple-element.140.refs_1_, bf16[16,2048]{1,0:T(8,128)(2,1)S(1)} %get-tuple-element.136.refs_2_, bf16[16,2048]{1,0:T(8,128)(2,1)S(1)} %get-tuple-element.132.refs_3_, ...), custom_call_target="tpu_custom_call" | custom-call | flops 1 | bytes 1 | tf_op jit(solution)/shard_map/products/pallas_call | solution.py:216
  226.0 6.1 %collective-permute-done.42 = bf16[128,1024]{1,0:T(8,128)(2,1)S(1)} collective-permute-done((bf16[128,1024]{1,0:T(8,128)(2,1)S(1)}, bf16[128,1024]{1,0:T(8,128)(2,1)S(1)}, u32[]{:S(2)}, u32[]{:S(2)}) %collective-permute-start.42) | collective-permute-done | bytes 262176 | tf_op jit(solution)/shard_map/ppermute | solution.py:354
  232.3 2.4 collective-permute-start.45
  234.8 2.0 collective-permute-start.47
  236.8 3.6 %products.15 = f32[128,1024]{1,0:T(8,128)S(1)} custom-call(bf16[16,2048]{1,0:T(8,128)(2,1)S(1)} %bitcast.294, bf16[16,2048]{1,0:T(8,128)(2,1)S(1)} %get-tuple-element.179.refs_1_, bf16[16,2048]{1,0:T(8,128)(2,1)S(1)} %get-tuple-element.175.refs_2_, bf16[16,2048]{1,0:T(8,128)(2,1)S(1)} %get-tuple-element.171.refs_3_, ...), custom_call_target="tpu_custom_call" | custom-call | flops 1 | bytes 1 | tf_op jit(solution)/shard_map/products/pallas_call | solution.py:216
  240.5 16.4 %collective-permute-done.46 = bf16[128,1024]{1,0:T(8,128)(2,1)S(1)} collective-permute-done((bf16[128,1024]{1,0:T(8,128)(2,1)S(1)}, bf16[128,1024]{1,0:T(8,128)(2,1)S(1)}, u32[]{:S(2)}, u32[]{:S(2)}) %collective-permute-start.46) | collective-permute-done | bytes 262176 | tf_op jit(solution)/shard_map/ppermute | solution.py:354
  (198 shorter events, 40.0 us)
Async XLA Ops:
  7.2 64.9 %all-to-all-start = ((bf16[8,256,1280]{2,1,0:T(8,128)(2,1)}), bf16[8,256,1280]{2,1,0:T(8,128)(2,1)}, u32[]{:S(2)}, u32[]{:S(2)}) async-start(bf16[8,256,1280]{2,1,0:T(8,128)(2,1)} %bitcast.301), calls=%async_computation | async-start | bytes 10485760 | tf_op jit(solution)/shard_map/all_to_all | solution.py:281
  19.0 25.9 %collective-permute-start = (bf16[128,2048]{1,0:T(8,128)(2,1)}, bf16[128,2048]{1,0:T(8,128)(2,1)S(1)}, u32[]{:S(2)}, u32[]{:S(2)}) collective-permute-start(bf16[128,2048]{1,0:T(8,128)(2,1)} %get-tuple-element.46), channel_id=1, source_target_pairs={{0,8},{8,0},{16,24},{24,16},{1,9},{9,1},{17,25},{25,17},{2,10},{10... | collective-permute-start | bytes 1572872 | tf_op jit(solution)/shard_map/ppermute | solution.py:286
  21.5 38.4 %collective-permute-start.1 = (bf16[128,2048]{1,0:T(8,128)(2,1)}, bf16[128,2048]{1,0:T(8,128)(2,1)S(1)}, u32[]{:S(2)}, u32[]{:S(2)}) collective-permute-start(bf16[128,2048]{1,0:T(8,128)(2,1)} %get-tuple-element.47), channel_id=1, source_target_pairs={{0,16},{8,24},{16,0},{24,8},{1,17},{9,25},{17,1},{25,9},{2,18},{10... | collective-permute-start | bytes 1572872 | tf_op jit(solution)/shard_map/ppermute | solution.py:286
  24.1 35.8 %collective-permute-start.2 = (bf16[128,2048]{1,0:T(8,128)(2,1)}, bf16[128,2048]{1,0:T(8,128)(2,1)S(1)}, u32[]{:S(2)}, u32[]{:S(2)}) collective-permute-start(bf16[128,2048]{1,0:T(8,128)(2,1)} %get-tuple-element.48), channel_id=1, source_target_pairs={{0,24},{8,16},{16,8},{24,0},{1,25},{9,17},{17,9},{25,1},{2,26},{10... | collective-permute-start | bytes 1572872 | tf_op jit(solution)/shard_map/ppermute | solution.py:286
  24.1 36.5 %collective-permute-start.3 = (bf16[128,2048]{1,0:T(8,128)(2,1)}, bf16[128,2048]{1,0:T(8,128)(2,1)S(1)}, u32[]{:S(2)}, u32[]{:S(2)}) collective-permute-start(bf16[128,2048]{1,0:T(8,128)(2,1)} %get-tuple-element.49), channel_id=1, source_target_pairs={{0,4},{4,0},{1,5},{5,1},{2,6},{6,2},{3,7},{7,3},{8,12},{12,8},{9,1... | collective-permute-start | bytes 1572872 | tf_op jit(solution)/shard_map/ppermute | solution.py:288
  44.9 15.7 %collective-permute-start.4 = (bf16[128,2048]{1,0:T(8,128)(2,1)S(1)}, bf16[128,2048]{1,0:T(8,128)(2,1)S(1)}, u32[]{:S(2)}, u32[]{:S(2)}) collective-permute-start(bf16[128,2048]{1,0:T(8,128)(2,1)S(1)} %collective-permute-done), channel_id=1, source_target_pairs={{0,4},{4,0},{1,5},{5,1},{2,6},{6,2},{3,7},{7,3},{8,12},{12,8},{9,1... | collective-permute-start | bytes 1572872 | tf_op jit(solution)/shard_map/ppermute | solution.py:288
  59.9 2.6 collective-permute-start.5
  59.9 2.8 %collective-permute-start.6 = (bf16[128,2048]{1,0:T(8,128)(2,1)S(1)}, bf16[128,2048]{1,0:T(8,128)(2,1)}, u32[]{:S(2)}, u32[]{:S(2)}) collective-permute-start(bf16[128,2048]{1,0:T(8,128)(2,1)S(1)} %collective-permute-done.2), channel_id=1, source_target_pairs={{0,4},{4,0},{1,5},{5,1},{2,6},{6,2},{3,7},{7,3},{8,12},{12,8},{9,1... | collective-permute-start | bytes 1572872 | tf_op jit(solution)/shard_map/ppermute | solution.py:288
  72.1 53.2 %all-to-all-start.1 = ((bf16[8,256,1024]{2,1,0:T(8,128)(2,1)}), bf16[8,256,1024]{2,1,0:T(8,128)(2,1)}, u32[]{:S(2)}, u32[]{:S(2)}) async-start(bf16[8,256,1024]{2,1,0:T(8,128)(2,1)} %bitcast.302), calls=%async_computation.1 | async-start | bytes 8388608 | tf_op jit(solution)/shard_map/all_to_all | solution.py:293
  97.7 32.3 %collective-permute-start.7 = (f16[128,1280]{1,0:T(8,128)(2,1)}, f16[128,1280]{1,0:T(8,128)(2,1)}, u32[]{:S(2)}, u32[]{:S(2)}) collective-permute-start(f16[128,1280]{1,0:T(8,128)(2,1)} %convert_element_type.106), channel_id=1, source_target_pairs={{0,24},{8,16},{16,8},{24,0},{1,25},{9,17},{17,9},{25,1},{2,26},{10... | collective-permute-start | bytes 983048 | tf_op jit(solution)/shard_map/ppermute | solution.py:306
  102.5 27.5 %collective-permute-start.9 = (f16[128,1280]{1,0:T(8,128)(2,1)}, f16[128,1280]{1,0:T(8,128)(2,1)}, u32[]{:S(2)}, u32[]{:S(2)}) collective-permute-start(f16[128,1280]{1,0:T(8,128)(2,1)} %convert_element_type.110), channel_id=1, source_target_pairs={{0,8},{8,0},{16,24},{24,16},{1,9},{9,1},{17,25},{25,17},{2,10},{10... | collective-permute-start | bytes 983048 | tf_op jit(solution)/shard_map/ppermute | solution.py:306
  102.5 28.7 %collective-permute-start.8 = (f16[128,1280]{1,0:T(8,128)(2,1)}, f16[128,1280]{1,0:T(8,128)(2,1)}, u32[]{:S(2)}, u32[]{:S(2)}) collective-permute-start(f16[128,1280]{1,0:T(8,128)(2,1)} %convert_element_type.108), channel_id=1, source_target_pairs={{0,16},{8,24},{16,0},{24,8},{1,17},{9,25},{17,1},{25,9},{2,18},{10... | collective-permute-start | bytes 983048 | tf_op jit(solution)/shard_map/ppermute | solution.py:306
  132.6 5.1 %collective-permute-start.10 = (f32[64,1280]{1,0:T(8,128)S(1)}, f32[64,1280]{1,0:T(8,128)S(1)}, u32[]{:S(2)}, u32[]{:S(2)}) collective-permute-start(f32[64,1280]{1,0:T(8,128)S(1)} %slice.451), channel_id=1, source_target_pairs={{0,4},{4,0},{1,5},{5,1},{2,6},{6,2},{3,7},{7,3},{8,12},{12,8},{9,1... | collective-permute-start | bytes 983048 | tf_op jit(solution)/shard_map/ppermute | solution.py:318
  132.9 20.4 %collective-permute-start.26 = (f16[128,1280]{1,0:T(8,128)(2,1)S(1)}, f16[128,1280]{1,0:T(8,128)(2,1)S(1)}, u32[]{:S(2)}, u32[]{:S(2)}) collective-permute-start(f16[128,1280]{1,0:T(8,128)(2,1)S(1)} %convert_element_type.123), channel_id=1, source_target_pairs={{0,8},{8,0},{16,24},{24,16},{1,9},{9,1},{17,25},{25,17},{2,10},{10... | collective-permute-start | bytes 983048 | tf_op jit(solution)/shard_map/ppermute | solution.py:306
  134.8 20.0 %collective-permute-start.24 = (f16[128,1280]{1,0:T(8,128)(2,1)S(1)}, f16[128,1280]{1,0:T(8,128)(2,1)S(1)}, u32[]{:S(2)}, u32[]{:S(2)}) collective-permute-start(f16[128,1280]{1,0:T(8,128)(2,1)S(1)} %convert_element_type.119), channel_id=1, source_target_pairs={{0,24},{8,16},{16,8},{24,0},{1,25},{9,17},{17,9},{25,1},{2,26},{10... | collective-permute-start | bytes 983048 | tf_op jit(solution)/shard_map/ppermute | solution.py:306
  137.3 29.1 %collective-permute-start.25 = (f16[128,1280]{1,0:T(8,128)(2,1)S(1)}, f16[128,1280]{1,0:T(8,128)(2,1)S(1)}, u32[]{:S(2)}, u32[]{:S(2)}) collective-permute-start(f16[128,1280]{1,0:T(8,128)(2,1)S(1)} %convert_element_type.121), channel_id=1, source_target_pairs={{0,16},{8,24},{16,0},{24,8},{1,17},{9,25},{17,1},{25,9},{2,18},{10... | collective-permute-start | bytes 983048 | tf_op jit(solution)/shard_map/ppermute | solution.py:306
  146.2 20.4 %collective-permute-start.13 = (bf16[16,2048]{1,0:T(8,128)(2,1)S(1)}, bf16[16,2048]{1,0:T(8,128)(2,1)S(1)}, u32[]{:S(2)}, u32[]{:S(2)}) collective-permute-start(bf16[16,2048]{1,0:T(8,128)(2,1)S(1)} %get-tuple-element.149), channel_id=1, source_target_pairs={{0,3},{1,2},{2,1},{3,0},{4,7},{5,6},{6,5},{7,4},{8,11},{9,10},{10,... | collective-permute-start | bytes 196616 | tf_op jit(solution)/shard_map/ppermute | solution.py:339
  147.5 19.1 %collective-permute-start.12 = (bf16[16,2048]{1,0:T(8,128)(2,1)S(1)}, bf16[16,2048]{1,0:T(8,128)(2,1)S(1)}, u32[]{:S(2)}, u32[]{:S(2)}) collective-permute-start(bf16[16,2048]{1,0:T(8,128)(2,1)S(1)} %get-tuple-element.150), channel_id=1, source_target_pairs={{0,2},{1,3},{2,0},{3,1},{4,6},{5,7},{6,4},{7,5},{8,10},{9,11},{10,... | collective-permute-start | bytes 196616 | tf_op jit(solution)/shard_map/ppermute | solution.py:339
  153.3 13.4 %collective-permute-start.11 = (bf16[16,2048]{1,0:T(8,128)(2,1)S(1)}, bf16[16,2048]{1,0:T(8,128)(2,1)S(1)}, u32[]{:S(2)}, u32[]{:S(2)}) collective-permute-start(bf16[16,2048]{1,0:T(8,128)(2,1)S(1)} %get-tuple-element.151), channel_id=1, source_target_pairs={{0,1},{1,0},{2,3},{3,2},{4,5},{5,4},{6,7},{7,6},{8,9},{9,8},{10,11... | collective-permute-start | bytes 196616 | tf_op jit(solution)/shard_map/ppermute | solution.py:339
  166.5 4.6 %collective-permute-start.27 = (f32[64,1280]{1,0:T(8,128)S(1)}, f32[64,1280]{1,0:T(8,128)S(1)}, u32[]{:S(2)}, u32[]{:S(2)}) collective-permute-start(f32[64,1280]{1,0:T(8,128)S(1)} %slice.468), channel_id=1, source_target_pairs={{0,4},{4,0},{1,5},{5,1},{2,6},{6,2},{3,7},{7,3},{8,12},{12,8},{9,1... | collective-permute-start | bytes 983048 | tf_op jit(solution)/shard_map/ppermute | solution.py:318
  166.7 15.3 %collective-permute-start.16 = (bf16[16,2048]{1,0:T(8,128)(2,1)S(1)}, bf16[16,2048]{1,0:T(8,128)(2,1)S(1)}, u32[]{:S(2)}, u32[]{:S(2)}) collective-permute-start(bf16[16,2048]{1,0:T(8,128)(2,1)S(1)} %get-tuple-element.145), channel_id=1, source_target_pairs={{0,24},{8,16},{16,8},{24,0},{1,25},{9,17},{17,9},{25,1},{2,26},{10... | collective-permute-start | bytes 196616 | tf_op jit(solution)/shard_map/ppermute | solution.py:344
  169.4 13.7 %collective-permute-start.15 = (bf16[16,2048]{1,0:T(8,128)(2,1)S(1)}, bf16[16,2048]{1,0:T(8,128)(2,1)S(1)}, u32[]{:S(2)}, u32[]{:S(2)}) collective-permute-start(bf16[16,2048]{1,0:T(8,128)(2,1)S(1)} %get-tuple-element.146), channel_id=1, source_target_pairs={{0,16},{8,24},{16,0},{24,8},{1,17},{9,25},{17,1},{25,9},{2,18},{10... | collective-permute-start | bytes 196616 | tf_op jit(solution)/shard_map/ppermute | solution.py:344
  169.4 13.7 %collective-permute-start.14 = (bf16[16,2048]{1,0:T(8,128)(2,1)S(1)}, bf16[16,2048]{1,0:T(8,128)(2,1)S(1)}, u32[]{:S(2)}, u32[]{:S(2)}) collective-permute-start(bf16[16,2048]{1,0:T(8,128)(2,1)S(1)} %get-tuple-element.147), channel_id=1, source_target_pairs={{0,8},{8,0},{16,24},{24,16},{1,9},{9,1},{17,25},{25,17},{2,10},{10... | collective-permute-start | bytes 196616 | tf_op jit(solution)/shard_map/ppermute | solution.py:344
  179.6 5.9 %collective-permute-start.30 = (bf16[16,2048]{1,0:T(8,128)(2,1)S(1)}, bf16[16,2048]{1,0:T(8,128)(2,1)S(1)}, u32[]{:S(2)}, u32[]{:S(2)}) collective-permute-start(bf16[16,2048]{1,0:T(8,128)(2,1)S(1)} %get-tuple-element.188), channel_id=1, source_target_pairs={{0,3},{1,2},{2,1},{3,0},{4,7},{5,6},{6,5},{7,4},{8,11},{9,10},{10,... | collective-permute-start | bytes 196616 | tf_op jit(solution)/shard_map/ppermute | solution.py:339
  181.0 5.3 %collective-permute-start.29 = (bf16[16,2048]{1,0:T(8,128)(2,1)S(1)}, bf16[16,2048]{1,0:T(8,128)(2,1)S(1)}, u32[]{:S(2)}, u32[]{:S(2)}) collective-permute-start(bf16[16,2048]{1,0:T(8,128)(2,1)S(1)} %get-tuple-element.189), channel_id=1, source_target_pairs={{0,2},{1,3},{2,0},{3,1},{4,6},{5,7},{6,4},{7,5},{8,10},{9,11},{10,... | collective-permute-start | bytes 196616 | tf_op jit(solution)/shard_map/ppermute | solution.py:339
  182.0 5.3 %collective-permute-start.28 = (bf16[16,2048]{1,0:T(8,128)(2,1)S(1)}, bf16[16,2048]{1,0:T(8,128)(2,1)S(1)}, u32[]{:S(2)}, u32[]{:S(2)}) collective-permute-start(bf16[16,2048]{1,0:T(8,128)(2,1)S(1)} %get-tuple-element.190), channel_id=1, source_target_pairs={{0,1},{1,0},{2,3},{3,2},{4,5},{5,4},{6,7},{7,6},{8,9},{9,8},{10,11... | collective-permute-start | bytes 196616 | tf_op jit(solution)/shard_map/ppermute | solution.py:339
  183.2 5.0 %collective-permute-start.20 = (bf16[4,16,2048]{2,1,0:T(8,128)(2,1)S(1)}, bf16[4,16,2048]{2,1,0:T(8,128)(2,1)S(1)}, u32[]{:S(2)}, u32[]{:S(2)}) collective-permute-start(bf16[4,16,2048]{2,1,0:T(8,128)(2,1)S(1)} %pad_maximum_fusion.2), channel_id=1, source_target_pairs={{0,4},{4,0},{1,5},{5,1},{2,6},{6,2},{3,7},{7,3},{8,12},{12,8},{9,1... | collective-permute-start | bytes 786440 | tf_op jit(solution)/shard_map/ppermute | solution.py:347
  183.3 10.1 %collective-permute-start.19 = (bf16[4,16,2048]{2,1,0:T(8,128)(2,1)S(1)}, bf16[4,16,2048]{2,1,0:T(8,128)(2,1)S(1)}, u32[]{:S(2)}, u32[]{:S(2)}) collective-permute-start(bf16[4,16,2048]{2,1,0:T(8,128)(2,1)S(1)} %pad_maximum_fusion.2), channel_id=1, source_target_pairs={{0,3},{1,2},{2,1},{3,0},{4,7},{5,6},{6,5},{7,4},{8,11},{9,10},{10,... | collective-permute-start | bytes 786440 | tf_op jit(solution)/shard_map/ppermute | solution.py:346
  185.4 13.1 %collective-permute-start.18 = (bf16[4,16,2048]{2,1,0:T(8,128)(2,1)S(1)}, bf16[4,16,2048]{2,1,0:T(8,128)(2,1)S(1)}, u32[]{:S(2)}, u32[]{:S(2)}) collective-permute-start(bf16[4,16,2048]{2,1,0:T(8,128)(2,1)S(1)} %pad_maximum_fusion.2), channel_id=1, source_target_pairs={{0,2},{1,3},{2,0},{3,1},{4,6},{5,7},{6,4},{7,5},{8,10},{9,11},{10,... | collective-permute-start | bytes 786440 | tf_op jit(solution)/shard_map/ppermute | solution.py:346
  186.3 12.2 %collective-permute-start.17 = (bf16[4,16,2048]{2,1,0:T(8,128)(2,1)S(1)}, bf16[4,16,2048]{2,1,0:T(8,128)(2,1)S(1)}, u32[]{:S(2)}, u32[]{:S(2)}) collective-permute-start(bf16[4,16,2048]{2,1,0:T(8,128)(2,1)S(1)} %pad_maximum_fusion.2), channel_id=1, source_target_pairs={{0,1},{1,0},{2,3},{3,2},{4,5},{5,4},{6,7},{7,6},{8,9},{9,8},{10,11... | collective-permute-start | bytes 786440 | tf_op jit(solution)/shard_map/ppermute | solution.py:346
  187.4 11.8 %collective-permute-start.33 = (bf16[16,2048]{1,0:T(8,128)(2,1)S(1)}, bf16[16,2048]{1,0:T(8,128)(2,1)S(1)}, u32[]{:S(2)}, u32[]{:S(2)}) collective-permute-start(bf16[16,2048]{1,0:T(8,128)(2,1)S(1)} %get-tuple-element.184), channel_id=1, source_target_pairs={{0,16},{8,24},{16,0},{24,8},{1,17},{9,25},{17,1},{25,9},{2,18},{10... | collective-permute-start | bytes 196616 | tf_op jit(solution)/shard_map/ppermute | solution.py:344
  188.2 11.1 %collective-permute-start.32 = (bf16[16,2048]{1,0:T(8,128)(2,1)S(1)}, bf16[16,2048]{1,0:T(8,128)(2,1)S(1)}, u32[]{:S(2)}, u32[]{:S(2)}) collective-permute-start(bf16[16,2048]{1,0:T(8,128)(2,1)S(1)} %get-tuple-element.185), channel_id=1, source_target_pairs={{0,8},{8,0},{16,24},{24,16},{1,9},{9,1},{17,25},{25,17},{2,10},{10... | collective-permute-start | bytes 196616 | tf_op jit(solution)/shard_map/ppermute | solution.py:344
  193.4 6.1 %collective-permute-start.31 = (bf16[16,2048]{1,0:T(8,128)(2,1)S(1)}, bf16[16,2048]{1,0:T(8,128)(2,1)S(1)}, u32[]{:S(2)}, u32[]{:S(2)}) collective-permute-start(bf16[16,2048]{1,0:T(8,128)(2,1)S(1)} %get-tuple-element.186), channel_id=1, source_target_pairs={{0,24},{8,16},{16,8},{24,0},{1,25},{9,17},{17,9},{25,1},{2,26},{10... | collective-permute-start | bytes 196616 | tf_op jit(solution)/shard_map/ppermute | solution.py:344
  198.5 2.7 %collective-permute-start.23 = (bf16[4,16,2048]{2,1,0:T(8,128)(2,1)S(1)}, bf16[4,16,2048]{2,1,0:T(8,128)(2,1)S(1)}, u32[]{:S(2)}, u32[]{:S(2)}) collective-permute-start(bf16[4,16,2048]{2,1,0:T(8,128)(2,1)S(1)} %collective-permute-done.19), channel_id=1, source_target_pairs={{0,4},{4,0},{1,5},{5,1},{2,6},{6,2},{3,7},{7,3},{8,12},{12,8},{9,1... | collective-permute-start | bytes 786440 | tf_op jit(solution)/shard_map/ppermute | solution.py:347
  198.6 3.7 %collective-permute-start.22 = (bf16[4,16,2048]{2,1,0:T(8,128)(2,1)S(1)}, bf16[4,16,2048]{2,1,0:T(8,128)(2,1)S(1)}, u32[]{:S(2)}, u32[]{:S(2)}) collective-permute-start(bf16[4,16,2048]{2,1,0:T(8,128)(2,1)S(1)} %collective-permute-done.18), channel_id=1, source_target_pairs={{0,4},{4,0},{1,5},{5,1},{2,6},{6,2},{3,7},{7,3},{8,12},{12,8},{9,1... | collective-permute-start | bytes 786440 | tf_op jit(solution)/shard_map/ppermute | solution.py:347
  199.1 4.3 %collective-permute-start.21 = (bf16[4,16,2048]{2,1,0:T(8,128)(2,1)S(1)}, bf16[4,16,2048]{2,1,0:T(8,128)(2,1)S(1)}, u32[]{:S(2)}, u32[]{:S(2)}) collective-permute-start(bf16[4,16,2048]{2,1,0:T(8,128)(2,1)S(1)} %collective-permute-done.17), channel_id=1, source_target_pairs={{0,4},{4,0},{1,5},{5,1},{2,6},{6,2},{3,7},{7,3},{8,12},{12,8},{9,1... | collective-permute-start | bytes 786440 | tf_op jit(solution)/shard_map/ppermute | solution.py:347
  199.5 11.2 %collective-permute-start.37 = (bf16[4,16,2048]{2,1,0:T(8,128)(2,1)S(1)}, bf16[4,16,2048]{2,1,0:T(8,128)(2,1)S(1)}, u32[]{:S(2)}, u32[]{:S(2)}) collective-permute-start(bf16[4,16,2048]{2,1,0:T(8,128)(2,1)S(1)} %pad_maximum_fusion.4), channel_id=1, source_target_pairs={{0,4},{4,0},{1,5},{5,1},{2,6},{6,2},{3,7},{7,3},{8,12},{12,8},{9,1... | collective-permute-start | bytes 786440 | tf_op jit(solution)/shard_map/ppermute | solution.py:347
  199.8 10.9 %collective-permute-start.36 = (bf16[4,16,2048]{2,1,0:T(8,128)(2,1)S(1)}, bf16[4,16,2048]{2,1,0:T(8,128)(2,1)S(1)}, u32[]{:S(2)}, u32[]{:S(2)}) collective-permute-start(bf16[4,16,2048]{2,1,0:T(8,128)(2,1)S(1)} %pad_maximum_fusion.4), channel_id=1, source_target_pairs={{0,3},{1,2},{2,1},{3,0},{4,7},{5,6},{6,5},{7,4},{8,11},{9,10},{10,... | collective-permute-start | bytes 786440 | tf_op jit(solution)/shard_map/ppermute | solution.py:346
  201.2 13.5 %collective-permute-start.35 = (bf16[4,16,2048]{2,1,0:T(8,128)(2,1)S(1)}, bf16[4,16,2048]{2,1,0:T(8,128)(2,1)S(1)}, u32[]{:S(2)}, u32[]{:S(2)}) collective-permute-start(bf16[4,16,2048]{2,1,0:T(8,128)(2,1)S(1)} %pad_maximum_fusion.4), channel_id=1, source_target_pairs={{0,2},{1,3},{2,0},{3,1},{4,6},{5,7},{6,4},{7,5},{8,10},{9,11},{10,... | collective-permute-start | bytes 786440 | tf_op jit(solution)/shard_map/ppermute | solution.py:346
  202.2 12.6 %collective-permute-start.34 = (bf16[4,16,2048]{2,1,0:T(8,128)(2,1)S(1)}, bf16[4,16,2048]{2,1,0:T(8,128)(2,1)S(1)}, u32[]{:S(2)}, u32[]{:S(2)}) collective-permute-start(bf16[4,16,2048]{2,1,0:T(8,128)(2,1)S(1)} %pad_maximum_fusion.4), channel_id=1, source_target_pairs={{0,1},{1,0},{2,3},{3,2},{4,5},{5,4},{6,7},{7,6},{8,9},{9,8},{10,11... | collective-permute-start | bytes 786440 | tf_op jit(solution)/shard_map/ppermute | solution.py:346
  208.0 18.0 %collective-permute-start.41 = (bf16[128,1024]{1,0:T(8,128)(2,1)S(1)}, bf16[128,1024]{1,0:T(8,128)(2,1)S(1)}, u32[]{:S(2)}, u32[]{:S(2)}) collective-permute-start(bf16[128,1024]{1,0:T(8,128)(2,1)S(1)} %get-tuple-element.66), channel_id=1, source_target_pairs={{0,24},{8,16},{16,8},{24,0},{1,25},{9,17},{17,9},{25,1},{2,26},{10... | collective-permute-start | bytes 786440 | tf_op jit(solution)/shard_map/ppermute | solution.py:354
  210.7 21.4 %collective-permute-start.42 = (bf16[128,1024]{1,0:T(8,128)(2,1)S(1)}, bf16[128,1024]{1,0:T(8,128)(2,1)S(1)}, u32[]{:S(2)}, u32[]{:S(2)}) collective-permute-start(bf16[128,1024]{1,0:T(8,128)(2,1)S(1)} %get-tuple-element.67), channel_id=1, source_target_pairs={{0,16},{8,24},{16,0},{24,8},{1,17},{9,25},{17,1},{25,9},{2,18},{10... | collective-permute-start | bytes 786440 | tf_op jit(solution)/shard_map/ppermute | solution.py:354
  210.7 21.3 %collective-permute-start.43 = (bf16[128,1024]{1,0:T(8,128)(2,1)S(1)}, bf16[128,1024]{1,0:T(8,128)(2,1)S(1)}, u32[]{:S(2)}, u32[]{:S(2)}) collective-permute-start(bf16[128,1024]{1,0:T(8,128)(2,1)S(1)} %get-tuple-element.68), channel_id=1, source_target_pairs={{0,8},{8,0},{16,24},{24,16},{1,9},{9,1},{17,25},{25,17},{2,10},{10... | collective-permute-start | bytes 786440 | tf_op jit(solution)/shard_map/ppermute | solution.py:354
  214.8 1.9 collective-permute-start.39
  232.2 8.1 %collective-permute-start.44 = (bf16[64,1024]{1,0:T(8,128)(2,1)S(1)}, bf16[64,1024]{1,0:T(8,128)(2,1)S(1)}, u32[]{:S(2)}, u32[]{:S(2)}) collective-permute-start(bf16[64,1024]{1,0:T(8,128)(2,1)S(1)} %slice.520), channel_id=1, source_target_pairs={{0,4},{4,0},{1,5},{5,1},{2,6},{6,2},{3,7},{7,3},{8,12},{12,8},{9,1... | collective-permute-start | bytes 393224 | tf_op jit(solution)/shard_map/ppermute | solution.py:364
  232.3 24.6 %collective-permute-start.45 = (bf16[128,1024]{1,0:T(8,128)(2,1)S(1)}, bf16[128,1024]{1,0:T(8,128)(2,1)S(1)}, u32[]{:S(2)}, u32[]{:S(2)}) collective-permute-start(bf16[128,1024]{1,0:T(8,128)(2,1)S(1)} %get-tuple-element.65.refs_9_), channel_id=1, source_target_pairs={{0,24},{8,16},{16,8},{24,0},{1,25},{9,17},{17,9},{25,1},{2,26},{10... | collective-permute-start | bytes 786440 | tf_op jit(solution)/shard_map/ppermute | solution.py:354
  234.7 22.1 %collective-permute-start.46 = (bf16[128,1024]{1,0:T(8,128)(2,1)S(1)}, bf16[128,1024]{1,0:T(8,128)(2,1)S(1)}, u32[]{:S(2)}, u32[]{:S(2)}) collective-permute-start(bf16[128,1024]{1,0:T(8,128)(2,1)S(1)} %get-tuple-element.69), channel_id=1, source_target_pairs={{0,16},{8,24},{16,0},{24,8},{1,17},{9,25},{17,1},{25,9},{2,18},{10... | collective-permute-start | bytes 786440 | tf_op jit(solution)/shard_map/ppermute | solution.py:354
  234.8 22.1 %collective-permute-start.47 = (bf16[128,1024]{1,0:T(8,128)(2,1)S(1)}, bf16[128,1024]{1,0:T(8,128)(2,1)S(1)}, u32[]{:S(2)}, u32[]{:S(2)}) collective-permute-start(bf16[128,1024]{1,0:T(8,128)(2,1)S(1)} %get-tuple-element.70), channel_id=1, source_target_pairs={{0,8},{8,0},{16,24},{24,16},{1,9},{9,1},{17,25},{25,17},{2,10},{10... | collective-permute-start | bytes 786440 | tf_op jit(solution)/shard_map/ppermute | solution.py:354
  (14 other events, 58.8 us)

commit v2 on v1

--- a/solution.py
+++ b/solution.py
@@ -226,6 +226,22 @@
         cost_estimate=pl.CostEstimate(flops=1, bytes_accessed=1, transcendentals=0),
         name="products",
     )(*blocks, weights, *after)
+
+
+def gate_kernel(*refs):
+    pass
+
+
+def gate(x, after):
+    return pl.pallas_call(
+        gate_kernel,
+        in_specs=[pl.BlockSpec(memory_space=pl.ANY)] * (1 + len(after)),
+        out_specs=pl.BlockSpec(memory_space=pl.ANY),
+        out_shape=jax.ShapeDtypeStruct(x.shape, x.dtype),
+        input_output_aliases={0: 0},
+        cost_estimate=pl.CostEstimate(flops=1, bytes_accessed=1, transcendentals=0),
+        name="gate",
+    )(x, *after)
 
 
 def by_xor(blocks, index):
@@ -309,11 +325,13 @@
     crossing = []
     for h in range(CHUNKS):
         sl = slice(h * part, (h + 1) * part)
-        waits = (before[0], output_weights) if attended is None else (attended,)
+        waits = (before[0],) if attended is None else (attended,)
         terms = sums[h]
         (total,) = products([[mine[0][sl], other[0][sl]]], weights, jnp.float32, waits)
         for term in terms:
             total = total + term.astype(jnp.float32)
+        if attended is None:
+            total = gate(total, (before[0], output_weights))
         here = total[:part]
         there = lax.ppermute(total[part:], "core", core_pairs)
         low = jnp.where(core == 0, here, there)

time: 261 us -> 255 us (0.977)
  other arithmetic: 12.5 us -> 7.6 us
    all_to_all x1, waiting for transfers between devices: 16.4 us -> 0.01 us  [local(): output_weights = lax.all_to_all(merged, ('core', 'tp'), 0, 0, tiled=True)]
    ppermute x6, waiting for transfers between devices: 12.8 us -> 27.6 us  [local(): lax.ppermute(x.astype(WIRE), 'z', plane_pairs[k])]
  transfers between devices with their start and end apart: 51 -> 51, of which waited for: 19 -> 19; matrix products, arithmetic and copies ran while one was open for 15% -> 14% of each run, Pallas kernels for 18% -> 19%
where the time goes in v2:
time: 255 us; the launch traced here: 253 us
  waiting for transfers between devices  95.1 us (37%)
  starting transfers between devices  60 us (24%)
  Pallas kernels  53.9 us (21%)
  local copies, waits for them, and re-layouts  26.2 us (10%)
  matrix products  8.98 us (4%)
  other arithmetic  7.6 us (3%)
    pallas_call x8, Pallas kernels, products(): pl.pallas_call(functools.partial(product_kernel, counts, len(after)), gri...  37.2 us
    ppermute x6, waiting for transfers between devices, local(): lax.ppermute(x.astype(WIRE), 'z', plane_pairs[k])  27.6 us
    ppermute x6, waiting for transfers between devices, local(): lax.ppermute(x, 'z', plane_pairs[k])  22.3 us
    ppermute x3, waiting for transfers between devices, local(): mine[k] = lax.ppermute(blocks[k], 'z', plane_pairs[k])  21.5 us
    ppermute x6, starting transfers between devices, local(): heads.append(lax.ppermute(block, 'z', plane_pairs[k]) if k else block)  10 us
    ppermute x6, starting transfers between devices, local(): lax.ppermute(x.astype(WIRE), 'z', plane_pairs[k])  9.96 us
    all_to_all x1, waiting for transfers between devices, local(): weights = lax.all_to_all(joined, ('core', 'tp'), 0, 0, tiled=True)  9.36 us
    ppermute x6, starting transfers between devices, local(): lax.ppermute(x, 'z', plane_pairs[k])  8.97 us
  transfers between devices with their start and end apart: 51, of which 19 were waited for; matrix products, arithmetic and copies ran while one was open for 14% of the time, Pallas kernels for 19%

profile of v2, /device:TPU:0, one launch (start us, length us, event | category | flops | bytes accessed | tf_op | source)
XLA Modules:
  0.0 253.4 jit_solution(11963357056620895046)
XLA Ops:
  0.7 6.6 %merge_inputs.1 = bf16[2,4,256,1280]{3,2,1,0:T(8,128)(2,1)} custom-call(s32[1]{0:T(128)S(6)} %copy.125.slot_ref, bf16[256,8192]{1,0:T(8,128)(2,1)} %qb_ref.1, bf16[256,1024]{1,0:T(8,128)(2,1)} %kb_ref.1, bf16[256,1024]{1,0:T(8,128)(2,1)} %vb_ref.1, bf16[4,64,256]{2,1,0:T(8,128)(2,1)} %bitcast.307, bf16[4,64,256]{2,1,0:T(8,128)(2,1)} %bitcast.308, ...), custom_call_target="tpu_custom_call" | custom-call | flops 402653184 | bytes 12582912 | tf_op jit(solution)/shard_map/merge_inputs/pallas_call | solution.py:100
  7.2 5.3 %all-to-all-start = ((bf16[8,256,1280]{2,1,0:T(8,128)(2,1)}), bf16[8,256,1280]{2,1,0:T(8,128)(2,1)}, u32[]{:S(2)}, u32[]{:S(2)}) async-start(bf16[8,256,1280]{2,1,0:T(8,128)(2,1)} %bitcast.301), calls=%async_computation | async-start | bytes 10485760 | tf_op jit(solution)/shard_map/all_to_all | solution.py:297
  12.5 2.1 reshape.193.x_ref
  14.6 4.4 %normed_blocks.1 = (bf16[128,2048]{1,0:T(8,128)(2,1)}, bf16[128,2048]{1,0:T(8,128)(2,1)}, bf16[128,2048]{1,0:T(8,128)(2,1)}, bf16[128,2048]{1,0:T(8,128)(2,1)}) custom-call(s32[1]{0:T(128)} %bitcast.5.z_ref, bf16[128,8192]{1,0:T(8,128)(2,1)} %reshape.193.x_ref, f32[1,8192]{1,0:T(1,128)} %bitcast.317), custom_call_target="tpu_custom_call" | custom-call | flops 6291456 | bytes 4194304 | tf_op jit(solution)/shard_map/normed_blocks/pallas_call | solution.py:137
  19.0 2.5 %collective-permute-start = (bf16[128,2048]{1,0:T(8,128)(2,1)}, bf16[128,2048]{1,0:T(8,128)(2,1)S(1)}, u32[]{:S(2)}, u32[]{:S(2)}) collective-permute-start(bf16[128,2048]{1,0:T(8,128)(2,1)} %get-tuple-element.46), channel_id=1, source_target_pairs={{0,8},{8,0},{16,24},{24,16},{1,9},{9,1},{17,25},{25,17},{2,10},{10... | collective-permute-start | bytes 1572872 | tf_op jit(solution)/shard_map/ppermute | solution.py:302
  21.6 2.6 %collective-permute-start.1 = (bf16[128,2048]{1,0:T(8,128)(2,1)}, bf16[128,2048]{1,0:T(8,128)(2,1)S(1)}, u32[]{:S(2)}, u32[]{:S(2)}) collective-permute-start(bf16[128,2048]{1,0:T(8,128)(2,1)} %get-tuple-element.47), channel_id=1, source_target_pairs={{0,16},{8,24},{16,0},{24,8},{1,17},{9,25},{17,1},{25,9},{2,18},{10... | collective-permute-start | bytes 1572872 | tf_op jit(solution)/shard_map/ppermute | solution.py:302
  24.2 5.7 %merge_output.1 = bf16[2,4,256,1024]{3,2,1,0:T(8,128)(2,1)} custom-call(s32[1]{0:T(128)S(6)} %copy.125.slot_ref, bf16[256,8192]{1,0:T(8,128)(2,1)} %base_ref, bf16[4,64,256]{2,1,0:T(8,128)(2,1)} %bitcast.310, bf16[4,64,8192]{2,1,0:T(8,128)(2,1)} %up_ref.1), custom_call_target="tpu_custom_call" | custom-call | flops 268435456 | bytes 10485760 | tf_op jit(solution)/shard_map/merge_output/pallas_call | solution.py:66
  29.9 8.5 %fusion.76 = (bf16[16,512,2,128]{3,2,1,0:T(2,128)(2,1)}, bf16[16,512,2,128]{3,2,1,0:T(2,128)(2,1)}) fusion(bf16[32,512,2,128]{3,2,1,0:T(2,128)(2,1)} %param.34), kind=kLoop, calls=%fused_computation.239 | loop fusion | bytes 16777216 | tf_op jit(solution)/shard_map/slice | solution.py:350
  38.5 6.5 %collective-permute-done = bf16[128,2048]{1,0:T(8,128)(2,1)S(1)} collective-permute-done((bf16[128,2048]{1,0:T(8,128)(2,1)}, bf16[128,2048]{1,0:T(8,128)(2,1)S(1)}, u32[]{:S(2)}, u32[]{:S(2)}) %collective-permute-start) | collective-permute-done | bytes 524320 | tf_op jit(solution)/shard_map/ppermute | solution.py:302
  45.0 15.0 %collective-permute-done.1 = bf16[128,2048]{1,0:T(8,128)(2,1)S(1)} collective-permute-done((bf16[128,2048]{1,0:T(8,128)(2,1)}, bf16[128,2048]{1,0:T(8,128)(2,1)S(1)}, u32[]{:S(2)}, u32[]{:S(2)}) %collective-permute-start.1) | collective-permute-done | bytes 524320 | tf_op jit(solution)/shard_map/ppermute | solution.py:302
  62.8 9.4 %all-to-all-done = bf16[8,256,1280]{2,1,0:T(8,128)(2,1)} async-done(((bf16[8,256,1280]{2,1,0:T(8,128)(2,1)}), bf16[8,256,1280]{2,1,0:T(8,128)(2,1)}, u32[]{:S(2)}, u32[]{:S(2)}) %all-to-all-start) | async-done | bytes 5242912 | tf_op jit(solution)/shard_map/all_to_all | solution.py:297
  72.1 4.7 %all-to-all-start.1 = ((bf16[8,256,1024]{2,1,0:T(8,128)(2,1)}), bf16[8,256,1024]{2,1,0:T(8,128)(2,1)}, u32[]{:S(2)}, u32[]{:S(2)}) async-start(bf16[8,256,1024]{2,1,0:T(8,128)(2,1)} %bitcast.302), calls=%async_computation.1 | async-start | bytes 8388608 | tf_op jit(solution)/shard_map/all_to_all | solution.py:309
  77.0 8.4 %fusion.77 = (bf16[16,512,2,128]{3,2,1,0:T(2,128)(2,1)}, bf16[16,512,2,128]{3,2,1,0:T(2,128)(2,1)}) fusion(bf16[32,512,2,128]{3,2,1,0:T(2,128)(2,1)} %param.35), kind=kLoop, calls=%fused_computation.240 | loop fusion | bytes 16777216 | tf_op jit(solution)/shard_map/slice | solution.py:350
  86.7 5.6 %products.8 = (f32[128,1280]{1,0:T(8,128)S(1)}, f32[128,1280]{1,0:T(8,128)S(1)}, f32[128,1280]{1,0:T(8,128)S(1)}) custom-call(bf16[64,2048]{1,0:T(8,128)(2,1)S(1)} %get-tuple-element.220.refs_0_, bf16[64,2048]{1,0:T(8,128)(2,1)S(1)} %get-tuple-element.105.refs_1_, bf16[64,2048]{1,0:T(8,128)(2,1)S(1)} %get-tuple-element.218.refs_2_, ...), custom_call_target="tpu_custom_call" | custom-call | flops 1 | bytes 1 | tf_op jit(solution)/shard_map/products/pallas_call | solution.py:216
  92.4 4.9 %collective-permute-start.7 = (f16[128,1280]{1,0:T(8,128)(2,1)S(1)}, f16[128,1280]{1,0:T(8,128)(2,1)S(1)}, u32[]{:S(2)}, u32[]{:S(2)}) collective-permute-start(f16[128,1280]{1,0:T(8,128)(2,1)S(1)} %convert_element_type.106), channel_id=1, source_target_pairs={{0,24},{8,16},{16,8},{24,0},{1,25},{9,17},{17,9},{25,1},{2,26},{10... | collective-permute-start | bytes 983048 | tf_op jit(solution)/shard_map/ppermute | solution.py:322
  97.9 5.7 %products.9 = (f32[128,1280]{1,0:T(8,128)S(1)}, f32[128,1280]{1,0:T(8,128)S(1)}, f32[128,1280]{1,0:T(8,128)S(1)}) custom-call(bf16[64,2048]{1,0:T(8,128)(2,1)S(1)} %get-tuple-element.219.refs_0_, bf16[64,2048]{1,0:T(8,128)(2,1)S(1)} %get-tuple-element.106.refs_1_, bf16[64,2048]{1,0:T(8,128)(2,1)S(1)} %get-tuple-element.217.refs_2_, ...), custom_call_target="tpu_custom_call" | custom-call | flops 1 | bytes 1 | tf_op jit(solution)/shard_map/products/pallas_call | solution.py:216
  103.7 4.9 %products.10 = f32[128,1280]{1,0:T(8,128)S(1)} custom-call(bf16[64,2048]{1,0:T(8,128)(2,1)S(1)} %get-tuple-element.214.refs_0_, bf16[64,2048]{1,0:T(8,128)(2,1)S(1)} %get-tuple-element.93.refs_1_, bf16[2048,1280]{1,0:T(8,128)(2,1)} %bitcast.4.refs_6_.refs_2_, f32[128,1280]{1,0:T(8,128)S(1)} %get-tuple-element.59.refs_3_.refs_1_), custom_call_target="tpu_custom_call" | custom-call | flops 1 | bytes 1 | tf_op jit(solution)/shard_map/products/pallas_call | solution.py:216
  108.6 5.0 %collective-permute-done.9 = f16[128,1280]{1,0:T(8,128)(2,1)S(1)} collective-permute-done((f16[128,1280]{1,0:T(8,128)(2,1)S(1)}, f16[128,1280]{1,0:T(8,128)(2,1)S(1)}, u32[]{:S(2)}, u32[]{:S(2)}) %collective-permute-start.9) | collective-permute-done | bytes 327712 | tf_op jit(solution)/shard_map/ppermute | solution.py:322
  113.6 12.0 %collective-permute-done.8 = f16[128,1280]{1,0:T(8,128)(2,1)S(1)} collective-permute-done((f16[128,1280]{1,0:T(8,128)(2,1)S(1)}, f16[128,1280]{1,0:T(8,128)(2,1)S(1)}, u32[]{:S(2)}, u32[]{:S(2)}) %collective-permute-start.8) | collective-permute-done | bytes 327712 | tf_op jit(solution)/shard_map/ppermute | solution.py:322
  128.1 3.7 %collective-permute-start.24 = (f16[128,1280]{1,0:T(8,128)(2,1)S(1)}, f16[128,1280]{1,0:T(8,128)(2,1)S(1)}, u32[]{:S(2)}, u32[]{:S(2)}) collective-permute-start(f16[128,1280]{1,0:T(8,128)(2,1)S(1)} %convert_element_type.119), channel_id=1, source_target_pairs={{0,24},{8,16},{16,8},{24,0},{1,25},{9,17},{17,9},{25,1},{2,26},{10... | collective-permute-start | bytes 983048 | tf_op jit(solution)/shard_map/ppermute | solution.py:322
  133.5 1.6 copy-done.3
  135.1 1.6 bitcast_reduce_fusion.1
  136.7 1.3 fusion.87
  141.1 2.5 %collective-permute-start.13 = (bf16[16,2048]{1,0:T(8,128)(2,1)S(1)}, bf16[16,2048]{1,0:T(8,128)(2,1)S(1)}, u32[]{:S(2)}, u32[]{:S(2)}) collective-permute-start(bf16[16,2048]{1,0:T(8,128)(2,1)S(1)} %get-tuple-element.149), channel_id=1, source_target_pairs={{0,3},{1,2},{2,1},{3,0},{4,7},{5,6},{6,5},{7,4},{8,11},{9,10},{10,... | collective-permute-start | bytes 196616 | tf_op jit(solution)/shard_map/ppermute | solution.py:357
  144.2 4.9 %products.11 = f32[128,1280]{1,0:T(8,128)S(1)} custom-call(bf16[64,2048]{1,0:T(8,128)(2,1)S(1)} %get-tuple-element.213.refs_0_, bf16[64,2048]{1,0:T(8,128)(2,1)S(1)} %get-tuple-element.94.refs_1_, bf16[2048,1280]{1,0:T(8,128)(2,1)} %bitcast.4.refs_6_.refs_2_, bf16[64,2048]{1,0:T(8,128)(2,1)S(1)} %reshape.199.refs_3_), custom_call_target="tpu_custom_call" | custom-call | flops 1 | bytes 1 | tf_op jit(solution)/shard_map/products/pallas_call | solution.py:216
  149.6 10.5 %collective-permute-done.25 = f16[128,1280]{1,0:T(8,128)(2,1)S(1)} collective-permute-done((f16[128,1280]{1,0:T(8,128)(2,1)S(1)}, f16[128,1280]{1,0:T(8,128)(2,1)S(1)}, u32[]{:S(2)}, u32[]{:S(2)}) %collective-permute-start.25) | collective-permute-done | bytes 327712 | tf_op jit(solution)/shard_map/ppermute | solution.py:322
  160.5 2.5 %collective-permute-start.16 = (bf16[16,2048]{1,0:T(8,128)(2,1)S(1)}, bf16[16,2048]{1,0:T(8,128)(2,1)S(1)}, u32[]{:S(2)}, u32[]{:S(2)}) collective-permute-start(bf16[16,2048]{1,0:T(8,128)(2,1)S(1)} %get-tuple-element.145), channel_id=1, source_target_pairs={{0,24},{8,16},{16,8},{24,0},{1,25},{9,17},{17,9},{25,1},{2,26},{10... | collective-permute-start | bytes 196616 | tf_op jit(solution)/shard_map/ppermute | solution.py:362
  163.1 1.9 collective-permute-start.14
  165.9 1.6 copy-done.2
  167.5 1.6 bitcast_reduce_fusion
  169.1 1.3 fusion.88
  174.5 1.3 collective-permute-start.29
  181.8 2.0 collective-permute-start.32
  183.8 3.3 %collective-permute-done.19 = bf16[4,16,2048]{2,1,0:T(8,128)(2,1)S(1)} collective-permute-done((bf16[4,16,2048]{2,1,0:T(8,128)(2,1)S(1)}, bf16[4,16,2048]{2,1,0:T(8,128)(2,1)S(1)}, u32[]{:S(2)}, u32[]{:S(2)}) %collective-permute-start.19) | collective-permute-done | bytes 262176 | tf_op jit(solution)/shard_map/ppermute | solution.py:364
  187.1 2.5 collective-permute-start.31
  189.6 2.6 %collective-permute-done.18 = bf16[4,16,2048]{2,1,0:T(8,128)(2,1)S(1)} collective-permute-done((bf16[4,16,2048]{2,1,0:T(8,128)(2,1)S(1)}, bf16[4,16,2048]{2,1,0:T(8,128)(2,1)S(1)}, u32[]{:S(2)}, u32[]{:S(2)}) %collective-permute-start.18) | collective-permute-done | bytes 262176 | tf_op jit(solution)/shard_map/ppermute | solution.py:364
  194.7 1.3 collective-permute-start.35
  197.2 4.5 %products.14 = (bf16[128,1024]{1,0:T(8,128)(2,1)S(1)}, bf16[128,1024]{1,0:T(8,128)(2,1)S(1)}, bf16[128,1024]{1,0:T(8,128)(2,1)S(1)}) custom-call(bf16[16,2048]{1,0:T(8,128)(2,1)S(1)} %collective-permute-done.16.refs_0_, bf16[16,2048]{1,0:T(8,128)(2,1)S(1)} %get-tuple-element.143.refs_1_, bf16[16,2048]{1,0:T(8,128)(2,1)S(1)} %get-tuple-element.139.refs_2_, ...), custom_call_target="tpu_custom_call" | custom-call | flops 1 | bytes 1 | tf_op jit(solution)/shard_map/products/pallas_call | solution.py:216
  201.7 2.5 %collective-permute-start.41 = (bf16[128,1024]{1,0:T(8,128)(2,1)S(1)}, bf16[128,1024]{1,0:T(8,128)(2,1)S(1)}, u32[]{:S(2)}, u32[]{:S(2)}) collective-permute-start(bf16[128,1024]{1,0:T(8,128)(2,1)S(1)} %get-tuple-element.66), channel_id=1, source_target_pairs={{0,24},{8,16},{16,8},{24,0},{1,25},{9,17},{17,9},{25,1},{2,26},{10... | collective-permute-start | bytes 786440 | tf_op jit(solution)/shard_map/ppermute | solution.py:372
  204.3 2.0 collective-permute-start.43
  206.3 2.2 collective-permute-done.35
  211.6 4.5 %products.12 = (bf16[128,1024]{1,0:T(8,128)(2,1)S(1)}, bf16[128,1024]{1,0:T(8,128)(2,1)S(1)}, bf16[128,1024]{1,0:T(8,128)(2,1)S(1)}) custom-call(bf16[16,2048]{1,0:T(8,128)(2,1)S(1)} %collective-permute-done.31.refs_0_, bf16[16,2048]{1,0:T(8,128)(2,1)S(1)} %get-tuple-element.182.refs_1_, bf16[16,2048]{1,0:T(8,128)(2,1)S(1)} %get-tuple-element.178.refs_2_, ...), custom_call_target="tpu_custom_call" | custom-call | flops 1 | bytes 1 | tf_op jit(solution)/shard_map/products/pallas_call | solution.py:216
  216.1 3.6 %products.13 = f32[128,1024]{1,0:T(8,128)S(1)} custom-call(bf16[16,2048]{1,0:T(8,128)(2,1)S(1)} %bitcast.293, bf16[16,2048]{1,0:T(8,128)(2,1)S(1)} %get-tuple-element.140.refs_1_, bf16[16,2048]{1,0:T(8,128)(2,1)S(1)} %get-tuple-element.136.refs_2_, bf16[16,2048]{1,0:T(8,128)(2,1)S(1)} %get-tuple-element.132.refs_3_, ...), custom_call_target="tpu_custom_call" | custom-call | flops 1 | bytes 1 | tf_op jit(solution)/shard_map/products/pallas_call | solution.py:216
  219.7 5.9 %collective-permute-done.42 = bf16[128,1024]{1,0:T(8,128)(2,1)S(1)} collective-permute-done((bf16[128,1024]{1,0:T(8,128)(2,1)S(1)}, bf16[128,1024]{1,0:T(8,128)(2,1)S(1)}, u32[]{:S(2)}, u32[]{:S(2)}) %collective-permute-start.42) | collective-permute-done | bytes 262176 | tf_op jit(solution)/shard_map/ppermute | solution.py:372
  225.9 2.4 collective-permute-start.45
  228.3 2.0 collective-permute-start.47
  230.3 3.6 %products.15 = f32[128,1024]{1,0:T(8,128)S(1)} custom-call(bf16[16,2048]{1,0:T(8,128)(2,1)S(1)} %bitcast.294, bf16[16,2048]{1,0:T(8,128)(2,1)S(1)} %get-tuple-element.179.refs_1_, bf16[16,2048]{1,0:T(8,128)(2,1)S(1)} %get-tuple-element.175.refs_2_, bf16[16,2048]{1,0:T(8,128)(2,1)S(1)} %get-tuple-element.171.refs_3_, ...), custom_call_target="tpu_custom_call" | custom-call | flops 1 | bytes 1 | tf_op jit(solution)/shard_map/products/pallas_call | solution.py:216
  234.0 16.4 %collective-permute-done.46 = bf16[128,1024]{1,0:T(8,128)(2,1)S(1)} collective-permute-done((bf16[128,1024]{1,0:T(8,128)(2,1)S(1)}, bf16[128,1024]{1,0:T(8,128)(2,1)S(1)}, u32[]{:S(2)}, u32[]{:S(2)}) %collective-permute-start.46) | collective-permute-done | bytes 262176 | tf_op jit(solution)/shard_map/ppermute | solution.py:372
  (197 shorter events, 34.0 us)
Async XLA Ops:
  7.2 64.9 %all-to-all-start = ((bf16[8,256,1280]{2,1,0:T(8,128)(2,1)}), bf16[8,256,1280]{2,1,0:T(8,128)(2,1)}, u32[]{:S(2)}, u32[]{:S(2)}) async-start(bf16[8,256,1280]{2,1,0:T(8,128)(2,1)} %bitcast.301), calls=%async_computation | async-start | bytes 10485760 | tf_op jit(solution)/shard_map/all_to_all | solution.py:297
  19.0 25.9 %collective-permute-start = (bf16[128,2048]{1,0:T(8,128)(2,1)}, bf16[128,2048]{1,0:T(8,128)(2,1)S(1)}, u32[]{:S(2)}, u32[]{:S(2)}) collective-permute-start(bf16[128,2048]{1,0:T(8,128)(2,1)} %get-tuple-element.46), channel_id=1, source_target_pairs={{0,8},{8,0},{16,24},{24,16},{1,9},{9,1},{17,25},{25,17},{2,10},{10... | collective-permute-start | bytes 1572872 | tf_op jit(solution)/shard_map/ppermute | solution.py:302
  21.6 38.4 %collective-permute-start.1 = (bf16[128,2048]{1,0:T(8,128)(2,1)}, bf16[128,2048]{1,0:T(8,128)(2,1)S(1)}, u32[]{:S(2)}, u32[]{:S(2)}) collective-permute-start(bf16[128,2048]{1,0:T(8,128)(2,1)} %get-tuple-element.47), channel_id=1, source_target_pairs={{0,16},{8,24},{16,0},{24,8},{1,17},{9,25},{17,1},{25,9},{2,18},{10... | collective-permute-start | bytes 1572872 | tf_op jit(solution)/shard_map/ppermute | solution.py:302
  24.2 35.8 %collective-permute-start.2 = (bf16[128,2048]{1,0:T(8,128)(2,1)}, bf16[128,2048]{1,0:T(8,128)(2,1)S(1)}, u32[]{:S(2)}, u32[]{:S(2)}) collective-permute-start(bf16[128,2048]{1,0:T(8,128)(2,1)} %get-tuple-element.48), channel_id=1, source_target_pairs={{0,24},{8,16},{16,8},{24,0},{1,25},{9,17},{17,9},{25,1},{2,26},{10... | collective-permute-start | bytes 1572872 | tf_op jit(solution)/shard_map/ppermute | solution.py:302
  24.2 37.1 %collective-permute-start.3 = (bf16[128,2048]{1,0:T(8,128)(2,1)}, bf16[128,2048]{1,0:T(8,128)(2,1)S(1)}, u32[]{:S(2)}, u32[]{:S(2)}) collective-permute-start(bf16[128,2048]{1,0:T(8,128)(2,1)} %get-tuple-element.49), channel_id=1, source_target_pairs={{0,4},{4,0},{1,5},{5,1},{2,6},{6,2},{3,7},{7,3},{8,12},{12,8},{9,1... | collective-permute-start | bytes 1572872 | tf_op jit(solution)/shard_map/ppermute | solution.py:304
  44.9 16.4 %collective-permute-start.4 = (bf16[128,2048]{1,0:T(8,128)(2,1)S(1)}, bf16[128,2048]{1,0:T(8,128)(2,1)S(1)}, u32[]{:S(2)}, u32[]{:S(2)}) collective-permute-start(bf16[128,2048]{1,0:T(8,128)(2,1)S(1)} %collective-permute-done), channel_id=1, source_target_pairs={{0,4},{4,0},{1,5},{5,1},{2,6},{6,2},{3,7},{7,3},{8,12},{12,8},{9,1... | collective-permute-start | bytes 1572872 | tf_op jit(solution)/shard_map/ppermute | solution.py:304
  60.0 2.6 %collective-permute-start.5 = (bf16[128,2048]{1,0:T(8,128)(2,1)S(1)}, bf16[128,2048]{1,0:T(8,128)(2,1)S(1)}, u32[]{:S(2)}, u32[]{:S(2)}) collective-permute-start(bf16[128,2048]{1,0:T(8,128)(2,1)S(1)} %collective-permute-done.1), channel_id=1, source_target_pairs={{0,4},{4,0},{1,5},{5,1},{2,6},{6,2},{3,7},{7,3},{8,12},{12,8},{9,1... | collective-permute-start | bytes 1572872 | tf_op jit(solution)/shard_map/ppermute | solution.py:304
  60.0 2.8 %collective-permute-start.6 = (bf16[128,2048]{1,0:T(8,128)(2,1)S(1)}, bf16[128,2048]{1,0:T(8,128)(2,1)}, u32[]{:S(2)}, u32[]{:S(2)}) collective-permute-start(bf16[128,2048]{1,0:T(8,128)(2,1)S(1)} %collective-permute-done.2), channel_id=1, source_target_pairs={{0,4},{4,0},{1,5},{5,1},{2,6},{6,2},{3,7},{7,3},{8,12},{12,8},{9,1... | collective-permute-start | bytes 1572872 | tf_op jit(solution)/shard_map/ppermute | solution.py:304
  72.1 54.5 %all-to-all-start.1 = ((bf16[8,256,1024]{2,1,0:T(8,128)(2,1)}), bf16[8,256,1024]{2,1,0:T(8,128)(2,1)}, u32[]{:S(2)}, u32[]{:S(2)}) async-start(bf16[8,256,1024]{2,1,0:T(8,128)(2,1)} %bitcast.302), calls=%async_computation.1 | async-start | bytes 8388608 | tf_op jit(solution)/shard_map/all_to_all | solution.py:309
  92.4 16.2 %collective-permute-start.7 = (f16[128,1280]{1,0:T(8,128)(2,1)S(1)}, f16[128,1280]{1,0:T(8,128)(2,1)S(1)}, u32[]{:S(2)}, u32[]{:S(2)}) collective-permute-start(f16[128,1280]{1,0:T(8,128)(2,1)S(1)} %convert_element_type.106), channel_id=1, source_target_pairs={{0,24},{8,16},{16,8},{24,0},{1,25},{9,17},{17,9},{25,1},{2,26},{10... | collective-permute-start | bytes 983048 | tf_op jit(solution)/shard_map/ppermute | solution.py:322
  97.3 16.3 %collective-permute-start.9 = (f16[128,1280]{1,0:T(8,128)(2,1)S(1)}, f16[128,1280]{1,0:T(8,128)(2,1)S(1)}, u32[]{:S(2)}, u32[]{:S(2)}) collective-permute-start(f16[128,1280]{1,0:T(8,128)(2,1)S(1)} %convert_element_type.110), channel_id=1, source_target_pairs={{0,8},{8,0},{16,24},{24,16},{1,9},{9,1},{17,25},{25,17},{2,10},{10... | collective-permute-start | bytes 983048 | tf_op jit(solution)/shard_map/ppermute | solution.py:322
  97.3 28.4 %collective-permute-start.8 = (f16[128,1280]{1,0:T(8,128)(2,1)S(1)}, f16[128,1280]{1,0:T(8,128)(2,1)S(1)}, u32[]{:S(2)}, u32[]{:S(2)}) collective-permute-start(f16[128,1280]{1,0:T(8,128)(2,1)S(1)} %convert_element_type.108), channel_id=1, source_target_pairs={{0,16},{8,24},{16,0},{24,8},{1,17},{9,25},{17,1},{25,9},{2,18},{10... | collective-permute-start | bytes 983048 | tf_op jit(solution)/shard_map/ppermute | solution.py:322
  127.8 4.8 %collective-permute-start.10 = (f32[64,1280]{1,0:T(8,128)S(1)}, f32[64,1280]{1,0:T(8,128)S(1)}, u32[]{:S(2)}, u32[]{:S(2)}) collective-permute-start(f32[64,1280]{1,0:T(8,128)S(1)} %slice.451), channel_id=1, source_target_pairs={{0,4},{4,0},{1,5},{5,1},{2,6},{6,2},{3,7},{7,3},{8,12},{12,8},{9,1... | collective-permute-start | bytes 983048 | tf_op jit(solution)/shard_map/ppermute | solution.py:336
  128.1 21.0 %collective-permute-start.24 = (f16[128,1280]{1,0:T(8,128)(2,1)S(1)}, f16[128,1280]{1,0:T(8,128)(2,1)S(1)}, u32[]{:S(2)}, u32[]{:S(2)}) collective-permute-start(f16[128,1280]{1,0:T(8,128)(2,1)S(1)} %convert_element_type.119), channel_id=1, source_target_pairs={{0,24},{8,16},{16,8},{24,0},{1,25},{9,17},{17,9},{25,1},{2,26},{10... | collective-permute-start | bytes 983048 | tf_op jit(solution)/shard_map/ppermute | solution.py:322
  131.8 17.8 %collective-permute-start.26 = (f16[128,1280]{1,0:T(8,128)(2,1)S(1)}, f16[128,1280]{1,0:T(8,128)(2,1)S(1)}, u32[]{:S(2)}, u32[]{:S(2)}) collective-permute-start(f16[128,1280]{1,0:T(8,128)(2,1)S(1)} %convert_element_type.123), channel_id=1, source_target_pairs={{0,8},{8,0},{16,24},{24,16},{1,9},{9,1},{17,25},{25,17},{2,10},{10... | collective-permute-start | bytes 983048 | tf_op jit(solution)/shard_map/ppermute | solution.py:322
  131.8 28.3 %collective-permute-start.25 = (f16[128,1280]{1,0:T(8,128)(2,1)S(1)}, f16[128,1280]{1,0:T(8,128)(2,1)S(1)}, u32[]{:S(2)}, u32[]{:S(2)}) collective-permute-start(f16[128,1280]{1,0:T(8,128)(2,1)S(1)} %convert_element_type.121), channel_id=1, source_target_pairs={{0,16},{8,24},{16,0},{24,8},{1,17},{9,25},{17,1},{25,9},{2,18},{10... | collective-permute-start | bytes 983048 | tf_op jit(solution)/shard_map/ppermute | solution.py:322
  141.1 19.3 %collective-permute-start.13 = (bf16[16,2048]{1,0:T(8,128)(2,1)S(1)}, bf16[16,2048]{1,0:T(8,128)(2,1)S(1)}, u32[]{:S(2)}, u32[]{:S(2)}) collective-permute-start(bf16[16,2048]{1,0:T(8,128)(2,1)S(1)} %get-tuple-element.149), channel_id=1, source_target_pairs={{0,3},{1,2},{2,1},{3,0},{4,7},{5,6},{6,5},{7,4},{8,11},{9,10},{10,... | collective-permute-start | bytes 196616 | tf_op jit(solution)/shard_map/ppermute | solution.py:357
  143.6 16.8 %collective-permute-start.12 = (bf16[16,2048]{1,0:T(8,128)(2,1)S(1)}, bf16[16,2048]{1,0:T(8,128)(2,1)S(1)}, u32[]{:S(2)}, u32[]{:S(2)}) collective-permute-start(bf16[16,2048]{1,0:T(8,128)(2,1)S(1)} %get-tuple-element.150), channel_id=1, source_target_pairs={{0,2},{1,3},{2,0},{3,1},{4,6},{5,7},{6,4},{7,5},{8,10},{9,11},{10,... | collective-permute-start | bytes 196616 | tf_op jit(solution)/shard_map/ppermute | solution.py:357
  149.1 11.3 %collective-permute-start.11 = (bf16[16,2048]{1,0:T(8,128)(2,1)S(1)}, bf16[16,2048]{1,0:T(8,128)(2,1)S(1)}, u32[]{:S(2)}, u32[]{:S(2)}) collective-permute-start(bf16[16,2048]{1,0:T(8,128)(2,1)S(1)} %get-tuple-element.151), channel_id=1, source_target_pairs={{0,1},{1,0},{2,3},{3,2},{4,5},{5,4},{6,7},{7,6},{8,9},{9,8},{10,11... | collective-permute-start | bytes 196616 | tf_op jit(solution)/shard_map/ppermute | solution.py:357
  160.3 4.6 %collective-permute-start.27 = (f32[64,1280]{1,0:T(8,128)S(1)}, f32[64,1280]{1,0:T(8,128)S(1)}, u32[]{:S(2)}, u32[]{:S(2)}) collective-permute-start(f32[64,1280]{1,0:T(8,128)S(1)} %slice.468), channel_id=1, source_target_pairs={{0,4},{4,0},{1,5},{5,1},{2,6},{6,2},{3,7},{7,3},{8,12},{12,8},{9,1... | collective-permute-start | bytes 983048 | tf_op jit(solution)/shard_map/ppermute | solution.py:336
  160.5 15.3 %collective-permute-start.16 = (bf16[16,2048]{1,0:T(8,128)(2,1)S(1)}, bf16[16,2048]{1,0:T(8,128)(2,1)S(1)}, u32[]{:S(2)}, u32[]{:S(2)}) collective-permute-start(bf16[16,2048]{1,0:T(8,128)(2,1)S(1)} %get-tuple-element.145), channel_id=1, source_target_pairs={{0,24},{8,16},{16,8},{24,0},{1,25},{9,17},{17,9},{25,1},{2,26},{10... | collective-permute-start | bytes 196616 | tf_op jit(solution)/shard_map/ppermute | solution.py:362
  163.1 13.8 %collective-permute-start.15 = (bf16[16,2048]{1,0:T(8,128)(2,1)S(1)}, bf16[16,2048]{1,0:T(8,128)(2,1)S(1)}, u32[]{:S(2)}, u32[]{:S(2)}) collective-permute-start(bf16[16,2048]{1,0:T(8,128)(2,1)S(1)} %get-tuple-element.146), channel_id=1, source_target_pairs={{0,16},{8,24},{16,0},{24,8},{1,17},{9,25},{17,1},{25,9},{2,18},{10... | collective-permute-start | bytes 196616 | tf_op jit(solution)/shard_map/ppermute | solution.py:362
  163.1 13.8 %collective-permute-start.14 = (bf16[16,2048]{1,0:T(8,128)(2,1)S(1)}, bf16[16,2048]{1,0:T(8,128)(2,1)S(1)}, u32[]{:S(2)}, u32[]{:S(2)}) collective-permute-start(bf16[16,2048]{1,0:T(8,128)(2,1)S(1)} %get-tuple-element.147), channel_id=1, source_target_pairs={{0,8},{8,0},{16,24},{24,16},{1,9},{9,1},{17,25},{25,17},{2,10},{10... | collective-permute-start | bytes 196616 | tf_op jit(solution)/shard_map/ppermute | solution.py:362
  173.3 5.8 %collective-permute-start.30 = (bf16[16,2048]{1,0:T(8,128)(2,1)S(1)}, bf16[16,2048]{1,0:T(8,128)(2,1)S(1)}, u32[]{:S(2)}, u32[]{:S(2)}) collective-permute-start(bf16[16,2048]{1,0:T(8,128)(2,1)S(1)} %get-tuple-element.188), channel_id=1, source_target_pairs={{0,3},{1,2},{2,1},{3,0},{4,7},{5,6},{6,5},{7,4},{8,11},{9,10},{10,... | collective-permute-start | bytes 196616 | tf_op jit(solution)/shard_map/ppermute | solution.py:357
  174.5 5.7 %collective-permute-start.29 = (bf16[16,2048]{1,0:T(8,128)(2,1)S(1)}, bf16[16,2048]{1,0:T(8,128)(2,1)S(1)}, u32[]{:S(2)}, u32[]{:S(2)}) collective-permute-start(bf16[16,2048]{1,0:T(8,128)(2,1)S(1)} %get-tuple-element.189), channel_id=1, source_target_pairs={{0,2},{1,3},{2,0},{3,1},{4,6},{5,7},{6,4},{7,5},{8,10},{9,11},{10,... | collective-permute-start | bytes 196616 | tf_op jit(solution)/shard_map/ppermute | solution.py:357
  175.8 4.7 %collective-permute-start.28 = (bf16[16,2048]{1,0:T(8,128)(2,1)S(1)}, bf16[16,2048]{1,0:T(8,128)(2,1)S(1)}, u32[]{:S(2)}, u32[]{:S(2)}) collective-permute-start(bf16[16,2048]{1,0:T(8,128)(2,1)S(1)} %get-tuple-element.190), channel_id=1, source_target_pairs={{0,1},{1,0},{2,3},{3,2},{4,5},{5,4},{6,7},{7,6},{8,9},{9,8},{10,11... | collective-permute-start | bytes 196616 | tf_op jit(solution)/shard_map/ppermute | solution.py:357
  176.9 4.8 %collective-permute-start.20 = (bf16[4,16,2048]{2,1,0:T(8,128)(2,1)S(1)}, bf16[4,16,2048]{2,1,0:T(8,128)(2,1)S(1)}, u32[]{:S(2)}, u32[]{:S(2)}) collective-permute-start(bf16[4,16,2048]{2,1,0:T(8,128)(2,1)S(1)} %pad_maximum_fusion.2), channel_id=1, source_target_pairs={{0,4},{4,0},{1,5},{5,1},{2,6},{6,2},{3,7},{7,3},{8,12},{12,8},{9,1... | collective-permute-start | bytes 786440 | tf_op jit(solution)/shard_map/ppermute | solution.py:365
  177.0 10.1 %collective-permute-start.19 = (bf16[4,16,2048]{2,1,0:T(8,128)(2,1)S(1)}, bf16[4,16,2048]{2,1,0:T(8,128)(2,1)S(1)}, u32[]{:S(2)}, u32[]{:S(2)}) collective-permute-start(bf16[4,16,2048]{2,1,0:T(8,128)(2,1)S(1)} %pad_maximum_fusion.2), channel_id=1, source_target_pairs={{0,3},{1,2},{2,1},{3,0},{4,7},{5,6},{6,5},{7,4},{8,11},{9,10},{10,... | collective-permute-start | bytes 786440 | tf_op jit(solution)/shard_map/ppermute | solution.py:364
  179.2 13.0 %collective-permute-start.18 = (bf16[4,16,2048]{2,1,0:T(8,128)(2,1)S(1)}, bf16[4,16,2048]{2,1,0:T(8,128)(2,1)S(1)}, u32[]{:S(2)}, u32[]{:S(2)}) collective-permute-start(bf16[4,16,2048]{2,1,0:T(8,128)(2,1)S(1)} %pad_maximum_fusion.2), channel_id=1, source_target_pairs={{0,2},{1,3},{2,0},{3,1},{4,6},{5,7},{6,4},{7,5},{8,10},{9,11},{10,... | collective-permute-start | bytes 786440 | tf_op jit(solution)/shard_map/ppermute | solution.py:364
  180.2 12.0 %collective-permute-start.17 = (bf16[4,16,2048]{2,1,0:T(8,128)(2,1)S(1)}, bf16[4,16,2048]{2,1,0:T(8,128)(2,1)S(1)}, u32[]{:S(2)}, u32[]{:S(2)}) collective-permute-start(bf16[4,16,2048]{2,1,0:T(8,128)(2,1)S(1)} %pad_maximum_fusion.2), channel_id=1, source_target_pairs={{0,1},{1,0},{2,3},{3,2},{4,5},{5,4},{6,7},{7,6},{8,9},{9,8},{10,11... | collective-permute-start | bytes 786440 | tf_op jit(solution)/shard_map/ppermute | solution.py:364
  180.7 12.2 %collective-permute-start.33 = (bf16[16,2048]{1,0:T(8,128)(2,1)S(1)}, bf16[16,2048]{1,0:T(8,128)(2,1)S(1)}, u32[]{:S(2)}, u32[]{:S(2)}) collective-permute-start(bf16[16,2048]{1,0:T(8,128)(2,1)S(1)} %get-tuple-element.184), channel_id=1, source_target_pairs={{0,16},{8,24},{16,0},{24,8},{1,17},{9,25},{17,1},{25,9},{2,18},{10... | collective-permute-start | bytes 196616 | tf_op jit(solution)/shard_map/ppermute | solution.py:362
  181.8 11.2 %collective-permute-start.32 = (bf16[16,2048]{1,0:T(8,128)(2,1)S(1)}, bf16[16,2048]{1,0:T(8,128)(2,1)S(1)}, u32[]{:S(2)}, u32[]{:S(2)}) collective-permute-start(bf16[16,2048]{1,0:T(8,128)(2,1)S(1)} %get-tuple-element.185), channel_id=1, source_target_pairs={{0,8},{8,0},{16,24},{24,16},{1,9},{9,1},{17,25},{25,17},{2,10},{10... | collective-permute-start | bytes 196616 | tf_op jit(solution)/shard_map/ppermute | solution.py:362
  187.1 6.1 %collective-permute-start.31 = (bf16[16,2048]{1,0:T(8,128)(2,1)S(1)}, bf16[16,2048]{1,0:T(8,128)(2,1)S(1)}, u32[]{:S(2)}, u32[]{:S(2)}) collective-permute-start(bf16[16,2048]{1,0:T(8,128)(2,1)S(1)} %get-tuple-element.186), channel_id=1, source_target_pairs={{0,24},{8,16},{16,8},{24,0},{1,25},{9,17},{17,9},{25,1},{2,26},{10... | collective-permute-start | bytes 196616 | tf_op jit(solution)/shard_map/ppermute | solution.py:362
  192.2 2.5 collective-permute-start.23
  192.2 3.8 %collective-permute-start.22 = (bf16[4,16,2048]{2,1,0:T(8,128)(2,1)S(1)}, bf16[4,16,2048]{2,1,0:T(8,128)(2,1)S(1)}, u32[]{:S(2)}, u32[]{:S(2)}) collective-permute-start(bf16[4,16,2048]{2,1,0:T(8,128)(2,1)S(1)} %collective-permute-done.18), channel_id=1, source_target_pairs={{0,4},{4,0},{1,5},{5,1},{2,6},{6,2},{3,7},{7,3},{8,12},{12,8},{9,1... | collective-permute-start | bytes 786440 | tf_op jit(solution)/shard_map/ppermute | solution.py:365
  192.8 4.3 %collective-permute-start.21 = (bf16[4,16,2048]{2,1,0:T(8,128)(2,1)S(1)}, bf16[4,16,2048]{2,1,0:T(8,128)(2,1)S(1)}, u32[]{:S(2)}, u32[]{:S(2)}) collective-permute-start(bf16[4,16,2048]{2,1,0:T(8,128)(2,1)S(1)} %collective-permute-done.17), channel_id=1, source_target_pairs={{0,4},{4,0},{1,5},{5,1},{2,6},{6,2},{3,7},{7,3},{8,12},{12,8},{9,1... | collective-permute-start | bytes 786440 | tf_op jit(solution)/shard_map/ppermute | solution.py:365
  193.2 11.0 %collective-permute-start.37 = (bf16[4,16,2048]{2,1,0:T(8,128)(2,1)S(1)}, bf16[4,16,2048]{2,1,0:T(8,128)(2,1)S(1)}, u32[]{:S(2)}, u32[]{:S(2)}) collective-permute-start(bf16[4,16,2048]{2,1,0:T(8,128)(2,1)S(1)} %pad_maximum_fusion.4), channel_id=1, source_target_pairs={{0,4},{4,0},{1,5},{5,1},{2,6},{6,2},{3,7},{7,3},{8,12},{12,8},{9,1... | collective-permute-start | bytes 786440 | tf_op jit(solution)/shard_map/ppermute | solution.py:365
  193.5 10.7 %collective-permute-start.36 = (bf16[4,16,2048]{2,1,0:T(8,128)(2,1)S(1)}, bf16[4,16,2048]{2,1,0:T(8,128)(2,1)S(1)}, u32[]{:S(2)}, u32[]{:S(2)}) collective-permute-start(bf16[4,16,2048]{2,1,0:T(8,128)(2,1)S(1)} %pad_maximum_fusion.4), channel_id=1, source_target_pairs={{0,3},{1,2},{2,1},{3,0},{4,7},{5,6},{6,5},{7,4},{8,11},{9,10},{10,... | collective-permute-start | bytes 786440 | tf_op jit(solution)/shard_map/ppermute | solution.py:364
  194.7 13.8 %collective-permute-start.35 = (bf16[4,16,2048]{2,1,0:T(8,128)(2,1)S(1)}, bf16[4,16,2048]{2,1,0:T(8,128)(2,1)S(1)}, u32[]{:S(2)}, u32[]{:S(2)}) collective-permute-start(bf16[4,16,2048]{2,1,0:T(8,128)(2,1)S(1)} %pad_maximum_fusion.4), channel_id=1, source_target_pairs={{0,2},{1,3},{2,0},{3,1},{4,6},{5,7},{6,4},{7,5},{8,10},{9,11},{10,... | collective-permute-start | bytes 786440 | tf_op jit(solution)/shard_map/ppermute | solution.py:364
  196.1 12.4 %collective-permute-start.34 = (bf16[4,16,2048]{2,1,0:T(8,128)(2,1)S(1)}, bf16[4,16,2048]{2,1,0:T(8,128)(2,1)S(1)}, u32[]{:S(2)}, u32[]{:S(2)}) collective-permute-start(bf16[4,16,2048]{2,1,0:T(8,128)(2,1)S(1)} %pad_maximum_fusion.4), channel_id=1, source_target_pairs={{0,1},{1,0},{2,3},{3,2},{4,5},{5,4},{6,7},{7,6},{8,9},{9,8},{10,11... | collective-permute-start | bytes 786440 | tf_op jit(solution)/shard_map/ppermute | solution.py:364
  201.7 18.0 %collective-permute-start.41 = (bf16[128,1024]{1,0:T(8,128)(2,1)S(1)}, bf16[128,1024]{1,0:T(8,128)(2,1)S(1)}, u32[]{:S(2)}, u32[]{:S(2)}) collective-permute-start(bf16[128,1024]{1,0:T(8,128)(2,1)S(1)} %get-tuple-element.66), channel_id=1, source_target_pairs={{0,24},{8,16},{16,8},{24,0},{1,25},{9,17},{17,9},{25,1},{2,26},{10... | collective-permute-start | bytes 786440 | tf_op jit(solution)/shard_map/ppermute | solution.py:372
  204.2 21.4 %collective-permute-start.42 = (bf16[128,1024]{1,0:T(8,128)(2,1)S(1)}, bf16[128,1024]{1,0:T(8,128)(2,1)S(1)}, u32[]{:S(2)}, u32[]{:S(2)}) collective-permute-start(bf16[128,1024]{1,0:T(8,128)(2,1)S(1)} %get-tuple-element.67), channel_id=1, source_target_pairs={{0,16},{8,24},{16,0},{24,8},{1,17},{9,25},{17,1},{25,9},{2,18},{10... | collective-permute-start | bytes 786440 | tf_op jit(solution)/shard_map/ppermute | solution.py:372
  204.3 21.3 %collective-permute-start.43 = (bf16[128,1024]{1,0:T(8,128)(2,1)S(1)}, bf16[128,1024]{1,0:T(8,128)(2,1)S(1)}, u32[]{:S(2)}, u32[]{:S(2)}) collective-permute-start(bf16[128,1024]{1,0:T(8,128)(2,1)S(1)} %get-tuple-element.68), channel_id=1, source_target_pairs={{0,8},{8,0},{16,24},{24,16},{1,9},{9,1},{17,25},{25,17},{2,10},{10... | collective-permute-start | bytes 786440 | tf_op jit(solution)/shard_map/ppermute | solution.py:372
  208.5 1.9 collective-permute-start.39
  225.8 8.1 %collective-permute-start.44 = (bf16[64,1024]{1,0:T(8,128)(2,1)S(1)}, bf16[64,1024]{1,0:T(8,128)(2,1)S(1)}, u32[]{:S(2)}, u32[]{:S(2)}) collective-permute-start(bf16[64,1024]{1,0:T(8,128)(2,1)S(1)} %slice.520), channel_id=1, source_target_pairs={{0,4},{4,0},{1,5},{5,1},{2,6},{6,2},{3,7},{7,3},{8,12},{12,8},{9,1... | collective-permute-start | bytes 393224 | tf_op jit(solution)/shard_map/ppermute | solution.py:382
  225.9 24.6 %collective-permute-start.45 = (bf16[128,1024]{1,0:T(8,128)(2,1)S(1)}, bf16[128,1024]{1,0:T(8,128)(2,1)S(1)}, u32[]{:S(2)}, u32[]{:S(2)}) collective-permute-start(bf16[128,1024]{1,0:T(8,128)(2,1)S(1)} %get-tuple-element.65.refs_9_), channel_id=1, source_target_pairs={{0,24},{8,16},{16,8},{24,0},{1,25},{9,17},{17,9},{25,1},{2,26},{10... | collective-permute-start | bytes 786440 | tf_op jit(solution)/shard_map/ppermute | solution.py:372
  228.3 22.1 %collective-permute-start.46 = (bf16[128,1024]{1,0:T(8,128)(2,1)S(1)}, bf16[128,1024]{1,0:T(8,128)(2,1)S(1)}, u32[]{:S(2)}, u32[]{:S(2)}) collective-permute-start(bf16[128,1024]{1,0:T(8,128)(2,1)S(1)} %get-tuple-element.69), channel_id=1, source_target_pairs={{0,16},{8,24},{16,0},{24,8},{1,17},{9,25},{17,1},{25,9},{2,18},{10... | collective-permute-start | bytes 786440 | tf_op jit(solution)/shard_map/ppermute | solution.py:372
  228.3 22.1 %collective-permute-start.47 = (bf16[128,1024]{1,0:T(8,128)(2,1)S(1)}, bf16[128,1024]{1,0:T(8,128)(2,1)S(1)}, u32[]{:S(2)}, u32[]{:S(2)}) collective-permute-start(bf16[128,1024]{1,0:T(8,128)(2,1)S(1)} %get-tuple-element.70), channel_id=1, source_target_pairs={{0,8},{8,0},{16,24},{24,16},{1,9},{9,1},{17,25},{25,17},{2,10},{10... | collective-permute-start | bytes 786440 | tf_op jit(solution)/shard_map/ppermute | solution.py:372
  (13 other events, 48.5 us)

commit v3 on v2

--- a/solution.py
+++ b/solution.py
@@ -209,7 +209,7 @@
 
 def products(groups, weights, kind, after=()):
     depth, width = weights.shape
-    tile = 256 if width % 256 == 0 else 128
+    tile = next(n for n in (width // 2, 256, 128) if n % 128 == 0 and width % n == 0)
     counts = [len(group) for group in groups]
     blocks = [block for group in groups for block in group]
     sizes = [sum(block.shape[0] for block in group) for group in groups]

time: 255 us -> 254 us (level)
  Pallas kernels: 53.9 us -> 45.9 us
  waiting for transfers between devices: 95.1 us -> 102 us
    pallas_call x8, Pallas kernels: 37.2 us -> 29.2 us  [products(): pl.pallas_call(functools.partial(product_kernel, counts, len(after)), gri...]
    ppermute x6, waiting for transfers between devices: 27.6 us -> 31.6 us  [local(): lax.ppermute(x.astype(WIRE), 'z', plane_pairs[k])]
  transfers between devices with their start and end apart: 51 -> 51, of which waited for: 19 -> 20; matrix products, arithmetic and copies ran while one was open for 14% -> 15% of each run, Pallas kernels for 19% -> 16%
where the time goes in v3:
time: 254 us; the launch traced here: 253 us
  waiting for transfers between devices  102 us (40%)
  starting transfers between devices  60.8 us (24%)
  Pallas kernels  45.9 us (18%)
  local copies, waits for them, and re-layouts  26.2 us (10%)
  matrix products  8.98 us (4%)
  other arithmetic  7.6 us (3%)
    ppermute x6, waiting for transfers between devices, local(): lax.ppermute(x.astype(WIRE), 'z', plane_pairs[k])  31.6 us
    pallas_call x8, Pallas kernels, products(): pl.pallas_call(functools.partial(product_kernel, counts, len(after)), gri...  29.2 us
    ppermute x6, waiting for transfers between devices, local(): lax.ppermute(x, 'z', plane_pairs[k])  24.1 us
    ppermute x3, waiting for transfers between devices, local(): mine[k] = lax.ppermute(blocks[k], 'z', plane_pairs[k])  21.5 us
    ppermute x6, starting transfers between devices, local(): lax.ppermute(x.astype(WIRE), 'z', plane_pairs[k])  10.8 us
    ppermute x6, starting transfers between devices, local(): heads.append(lax.ppermute(block, 'z', plane_pairs[k]) if k else block)  10 us
    all_to_all x1, waiting for transfers between devices, local(): weights = lax.all_to_all(joined, ('core', 'tp'), 0, 0, tiled=True)  9.36 us
    ppermute x6, starting transfers between devices, local(): lax.ppermute(x, 'z', plane_pairs[k])  8.95 us
  transfers between devices with their start and end apart: 51, of which 20 were waited for; matrix products, arithmetic and copies ran while one was open for 15% of the time, Pallas kernels for 16%

profile of v3, /device:TPU:0, one launch (start us, length us, event | category | flops | bytes accessed | tf_op | source)
XLA Modules:
  0.0 252.7 jit_solution(756635332408364148)
XLA Ops:
  0.7 6.6 %merge_inputs.1 = bf16[2,4,256,1280]{3,2,1,0:T(8,128)(2,1)} custom-call(s32[1]{0:T(128)S(6)} %copy.125.slot_ref, bf16[256,8192]{1,0:T(8,128)(2,1)} %qb_ref.1, bf16[256,1024]{1,0:T(8,128)(2,1)} %kb_ref.1, bf16[256,1024]{1,0:T(8,128)(2,1)} %vb_ref.1, bf16[4,64,256]{2,1,0:T(8,128)(2,1)} %bitcast.307, bf16[4,64,256]{2,1,0:T(8,128)(2,1)} %bitcast.308, ...), custom_call_target="tpu_custom_call" | custom-call | flops 402653184 | bytes 12582912 | tf_op jit(solution)/shard_map/merge_inputs/pallas_call | solution.py:100
  7.2 5.3 %all-to-all-start = ((bf16[8,256,1280]{2,1,0:T(8,128)(2,1)}), bf16[8,256,1280]{2,1,0:T(8,128)(2,1)}, u32[]{:S(2)}, u32[]{:S(2)}) async-start(bf16[8,256,1280]{2,1,0:T(8,128)(2,1)} %bitcast.301), calls=%async_computation | async-start | bytes 10485760 | tf_op jit(solution)/shard_map/all_to_all | solution.py:297
  12.5 2.1 reshape.193.x_ref
  14.6 4.4 %normed_blocks.1 = (bf16[128,2048]{1,0:T(8,128)(2,1)}, bf16[128,2048]{1,0:T(8,128)(2,1)}, bf16[128,2048]{1,0:T(8,128)(2,1)}, bf16[128,2048]{1,0:T(8,128)(2,1)}) custom-call(s32[1]{0:T(128)} %bitcast.5.z_ref, bf16[128,8192]{1,0:T(8,128)(2,1)} %reshape.193.x_ref, f32[1,8192]{1,0:T(1,128)} %bitcast.317), custom_call_target="tpu_custom_call" | custom-call | flops 6291456 | bytes 4194304 | tf_op jit(solution)/shard_map/normed_blocks/pallas_call | solution.py:137
  19.0 2.5 %collective-permute-start = (bf16[128,2048]{1,0:T(8,128)(2,1)}, bf16[128,2048]{1,0:T(8,128)(2,1)S(1)}, u32[]{:S(2)}, u32[]{:S(2)}) collective-permute-start(bf16[128,2048]{1,0:T(8,128)(2,1)} %get-tuple-element.46), channel_id=1, source_target_pairs={{0,8},{8,0},{16,24},{24,16},{1,9},{9,1},{17,25},{25,17},{2,10},{10... | collective-permute-start | bytes 1572872 | tf_op jit(solution)/shard_map/ppermute | solution.py:302
  21.6 2.6 %collective-permute-start.1 = (bf16[128,2048]{1,0:T(8,128)(2,1)}, bf16[128,2048]{1,0:T(8,128)(2,1)S(1)}, u32[]{:S(2)}, u32[]{:S(2)}) collective-permute-start(bf16[128,2048]{1,0:T(8,128)(2,1)} %get-tuple-element.47), channel_id=1, source_target_pairs={{0,16},{8,24},{16,0},{24,8},{1,17},{9,25},{17,1},{25,9},{2,18},{10... | collective-permute-start | bytes 1572872 | tf_op jit(solution)/shard_map/ppermute | solution.py:302
  24.2 5.7 %merge_output.1 = bf16[2,4,256,1024]{3,2,1,0:T(8,128)(2,1)} custom-call(s32[1]{0:T(128)S(6)} %copy.125.slot_ref, bf16[256,8192]{1,0:T(8,128)(2,1)} %base_ref, bf16[4,64,256]{2,1,0:T(8,128)(2,1)} %bitcast.310, bf16[4,64,8192]{2,1,0:T(8,128)(2,1)} %up_ref.1), custom_call_target="tpu_custom_call" | custom-call | flops 268435456 | bytes 10485760 | tf_op jit(solution)/shard_map/merge_output/pallas_call | solution.py:66
  29.9 8.5 %fusion.76 = (bf16[16,512,2,128]{3,2,1,0:T(2,128)(2,1)}, bf16[16,512,2,128]{3,2,1,0:T(2,128)(2,1)}) fusion(bf16[32,512,2,128]{3,2,1,0:T(2,128)(2,1)} %param.34), kind=kLoop, calls=%fused_computation.239 | loop fusion | bytes 16777216 | tf_op jit(solution)/shard_map/slice | solution.py:350
  38.5 6.5 %collective-permute-done = bf16[128,2048]{1,0:T(8,128)(2,1)S(1)} collective-permute-done((bf16[128,2048]{1,0:T(8,128)(2,1)}, bf16[128,2048]{1,0:T(8,128)(2,1)S(1)}, u32[]{:S(2)}, u32[]{:S(2)}) %collective-permute-start) | collective-permute-done | bytes 524320 | tf_op jit(solution)/shard_map/ppermute | solution.py:302
  45.0 15.0 %collective-permute-done.1 = bf16[128,2048]{1,0:T(8,128)(2,1)S(1)} collective-permute-done((bf16[128,2048]{1,0:T(8,128)(2,1)}, bf16[128,2048]{1,0:T(8,128)(2,1)S(1)}, u32[]{:S(2)}, u32[]{:S(2)}) %collective-permute-start.1) | collective-permute-done | bytes 524320 | tf_op jit(solution)/shard_map/ppermute | solution.py:302
  62.8 9.4 %all-to-all-done = bf16[8,256,1280]{2,1,0:T(8,128)(2,1)} async-done(((bf16[8,256,1280]{2,1,0:T(8,128)(2,1)}), bf16[8,256,1280]{2,1,0:T(8,128)(2,1)}, u32[]{:S(2)}, u32[]{:S(2)}) %all-to-all-start) | async-done | bytes 5242912 | tf_op jit(solution)/shard_map/all_to_all | solution.py:297
  72.1 4.7 %all-to-all-start.1 = ((bf16[8,256,1024]{2,1,0:T(8,128)(2,1)}), bf16[8,256,1024]{2,1,0:T(8,128)(2,1)}, u32[]{:S(2)}, u32[]{:S(2)}) async-start(bf16[8,256,1024]{2,1,0:T(8,128)(2,1)} %bitcast.302), calls=%async_computation.1 | async-start | bytes 8388608 | tf_op jit(solution)/shard_map/all_to_all | solution.py:309
  77.0 8.4 %fusion.77 = (bf16[16,512,2,128]{3,2,1,0:T(2,128)(2,1)}, bf16[16,512,2,128]{3,2,1,0:T(2,128)(2,1)}) fusion(bf16[32,512,2,128]{3,2,1,0:T(2,128)(2,1)} %param.35), kind=kLoop, calls=%fused_computation.240 | loop fusion | bytes 16777216 | tf_op jit(solution)/shard_map/slice | solution.py:350
  86.7 4.8 %products.8 = (f32[128,1280]{1,0:T(8,128)S(1)}, f32[128,1280]{1,0:T(8,128)S(1)}, f32[128,1280]{1,0:T(8,128)S(1)}) custom-call(bf16[64,2048]{1,0:T(8,128)(2,1)S(1)} %get-tuple-element.220.refs_0_, bf16[64,2048]{1,0:T(8,128)(2,1)S(1)} %get-tuple-element.105.refs_1_, bf16[64,2048]{1,0:T(8,128)(2,1)S(1)} %get-tuple-element.218.refs_2_, ...), custom_call_target="tpu_custom_call" | custom-call | flops 1 | bytes 1 | tf_op jit(solution)/shard_map/products/pallas_call | solution.py:216
  91.6 4.9 %collective-permute-start.7 = (f16[128,1280]{1,0:T(8,128)(2,1)S(1)}, f16[128,1280]{1,0:T(8,128)(2,1)S(1)}, u32[]{:S(2)}, u32[]{:S(2)}) collective-permute-start(f16[128,1280]{1,0:T(8,128)(2,1)S(1)} %convert_element_type.106), channel_id=1, source_target_pairs={{0,24},{8,16},{16,8},{24,0},{1,25},{9,17},{17,9},{25,1},{2,26},{10... | collective-permute-start | bytes 983048 | tf_op jit(solution)/shard_map/ppermute | solution.py:322
  97.1 4.8 %products.9 = (f32[128,1280]{1,0:T(8,128)S(1)}, f32[128,1280]{1,0:T(8,128)S(1)}, f32[128,1280]{1,0:T(8,128)S(1)}) custom-call(bf16[64,2048]{1,0:T(8,128)(2,1)S(1)} %get-tuple-element.219.refs_0_, bf16[64,2048]{1,0:T(8,128)(2,1)S(1)} %get-tuple-element.106.refs_1_, bf16[64,2048]{1,0:T(8,128)(2,1)S(1)} %get-tuple-element.217.refs_2_, ...), custom_call_target="tpu_custom_call" | custom-call | flops 1 | bytes 1 | tf_op jit(solution)/shard_map/products/pallas_call | solution.py:216
  102.0 3.3 %products.10 = f32[128,1280]{1,0:T(8,128)S(1)} custom-call(bf16[64,2048]{1,0:T(8,128)(2,1)S(1)} %get-tuple-element.214.refs_0_, bf16[64,2048]{1,0:T(8,128)(2,1)S(1)} %get-tuple-element.93.refs_1_, bf16[2048,1280]{1,0:T(8,128)(2,1)} %bitcast.4.refs_6_.refs_2_, f32[128,1280]{1,0:T(8,128)S(1)} %get-tuple-element.59.refs_3_.refs_1_), custom_call_target="tpu_custom_call" | custom-call | flops 1 | bytes 1 | tf_op jit(solution)/shard_map/products/pallas_call | solution.py:216
  105.3 7.4 %collective-permute-done.9 = f16[128,1280]{1,0:T(8,128)(2,1)S(1)} collective-permute-done((f16[128,1280]{1,0:T(8,128)(2,1)S(1)}, f16[128,1280]{1,0:T(8,128)(2,1)S(1)}, u32[]{:S(2)}, u32[]{:S(2)}) %collective-permute-start.9) | collective-permute-done | bytes 327712 | tf_op jit(solution)/shard_map/ppermute | solution.py:322
  112.8 12.0 %collective-permute-done.8 = f16[128,1280]{1,0:T(8,128)(2,1)S(1)} collective-permute-done((f16[128,1280]{1,0:T(8,128)(2,1)S(1)}, f16[128,1280]{1,0:T(8,128)(2,1)S(1)}, u32[]{:S(2)}, u32[]{:S(2)}) %collective-permute-start.8) | collective-permute-done | bytes 327712 | tf_op jit(solution)/shard_map/ppermute | solution.py:322
  127.2 4.6 %collective-permute-start.24 = (f16[128,1280]{1,0:T(8,128)(2,1)S(1)}, f16[128,1280]{1,0:T(8,128)(2,1)S(1)}, u32[]{:S(2)}, u32[]{:S(2)}) collective-permute-start(f16[128,1280]{1,0:T(8,128)(2,1)S(1)} %convert_element_type.119), channel_id=1, source_target_pairs={{0,24},{8,16},{16,8},{24,0},{1,25},{9,17},{17,9},{25,1},{2,26},{10... | collective-permute-start | bytes 983048 | tf_op jit(solution)/shard_map/ppermute | solution.py:322
  133.4 1.6 copy-done.3
  135.1 1.6 bitcast_reduce_fusion.1
  136.7 1.3 fusion.87
  141.0 1.8 collective-permute-start.13
  143.4 3.4 %products.11 = f32[128,1280]{1,0:T(8,128)S(1)} custom-call(bf16[64,2048]{1,0:T(8,128)(2,1)S(1)} %get-tuple-element.213.refs_0_, bf16[64,2048]{1,0:T(8,128)(2,1)S(1)} %get-tuple-element.94.refs_1_, bf16[2048,1280]{1,0:T(8,128)(2,1)} %bitcast.4.refs_6_.refs_2_, bf16[64,2048]{1,0:T(8,128)(2,1)S(1)} %reshape.199.refs_3_), custom_call_target="tpu_custom_call" | custom-call | flops 1 | bytes 1 | tf_op jit(solution)/shard_map/products/pallas_call | solution.py:216
  148.1 12.0 %collective-permute-done.25 = f16[128,1280]{1,0:T(8,128)(2,1)S(1)} collective-permute-done((f16[128,1280]{1,0:T(8,128)(2,1)S(1)}, f16[128,1280]{1,0:T(8,128)(2,1)S(1)}, u32[]{:S(2)}, u32[]{:S(2)}) %collective-permute-start.25) | collective-permute-done | bytes 327712 | tf_op jit(solution)/shard_map/ppermute | solution.py:322
  160.5 2.5 %collective-permute-start.16 = (bf16[16,2048]{1,0:T(8,128)(2,1)S(1)}, bf16[16,2048]{1,0:T(8,128)(2,1)S(1)}, u32[]{:S(2)}, u32[]{:S(2)}) collective-permute-start(bf16[16,2048]{1,0:T(8,128)(2,1)S(1)} %get-tuple-element.145), channel_id=1, source_target_pairs={{0,24},{8,16},{16,8},{24,0},{1,25},{9,17},{17,9},{25,1},{2,26},{10... | collective-permute-start | bytes 196616 | tf_op jit(solution)/shard_map/ppermute | solution.py:362
  163.1 1.9 collective-permute-start.14
  165.9 1.6 copy-done.2
  167.5 1.6 bitcast_reduce_fusion
  169.1 1.3 fusion.88
  174.5 1.4 collective-permute-start.29
  181.8 2.0 collective-permute-start.32
  183.8 3.3 %collective-permute-done.19 = bf16[4,16,2048]{2,1,0:T(8,128)(2,1)S(1)} collective-permute-done((bf16[4,16,2048]{2,1,0:T(8,128)(2,1)S(1)}, bf16[4,16,2048]{2,1,0:T(8,128)(2,1)S(1)}, u32[]{:S(2)}, u32[]{:S(2)}) %collective-permute-start.19) | collective-permute-done | bytes 262176 | tf_op jit(solution)/shard_map/ppermute | solution.py:364
  187.1 2.5 collective-permute-start.31
  189.6 2.5 collective-permute-done.18
  194.7 1.4 collective-permute-start.35
  197.1 3.8 %products.14 = (bf16[128,1024]{1,0:T(8,128)(2,1)S(1)}, bf16[128,1024]{1,0:T(8,128)(2,1)S(1)}, bf16[128,1024]{1,0:T(8,128)(2,1)S(1)}) custom-call(bf16[16,2048]{1,0:T(8,128)(2,1)S(1)} %collective-permute-done.16.refs_0_, bf16[16,2048]{1,0:T(8,128)(2,1)S(1)} %get-tuple-element.143.refs_1_, bf16[16,2048]{1,0:T(8,128)(2,1)S(1)} %get-tuple-element.139.refs_2_, ...), custom_call_target="tpu_custom_call" | custom-call | flops 1 | bytes 1 | tf_op jit(solution)/shard_map/products/pallas_call | solution.py:216
  200.9 2.6 %collective-permute-start.41 = (bf16[128,1024]{1,0:T(8,128)(2,1)S(1)}, bf16[128,1024]{1,0:T(8,128)(2,1)S(1)}, u32[]{:S(2)}, u32[]{:S(2)}) collective-permute-start(bf16[128,1024]{1,0:T(8,128)(2,1)S(1)} %get-tuple-element.66), channel_id=1, source_target_pairs={{0,24},{8,16},{16,8},{24,0},{1,25},{9,17},{17,9},{25,1},{2,26},{10... | collective-permute-start | bytes 786440 | tf_op jit(solution)/shard_map/ppermute | solution.py:372
  203.6 1.9 collective-permute-start.43
  205.5 3.0 %collective-permute-done.35 = bf16[4,16,2048]{2,1,0:T(8,128)(2,1)S(1)} collective-permute-done((bf16[4,16,2048]{2,1,0:T(8,128)(2,1)S(1)}, bf16[4,16,2048]{2,1,0:T(8,128)(2,1)S(1)}, u32[]{:S(2)}, u32[]{:S(2)}) %collective-permute-start.35) | collective-permute-done | bytes 262176 | tf_op jit(solution)/shard_map/ppermute | solution.py:364
  211.5 3.8 %products.12 = (bf16[128,1024]{1,0:T(8,128)(2,1)S(1)}, bf16[128,1024]{1,0:T(8,128)(2,1)S(1)}, bf16[128,1024]{1,0:T(8,128)(2,1)S(1)}) custom-call(bf16[16,2048]{1,0:T(8,128)(2,1)S(1)} %collective-permute-done.31.refs_0_, bf16[16,2048]{1,0:T(8,128)(2,1)S(1)} %get-tuple-element.182.refs_1_, bf16[16,2048]{1,0:T(8,128)(2,1)S(1)} %get-tuple-element.178.refs_2_, ...), custom_call_target="tpu_custom_call" | custom-call | flops 1 | bytes 1 | tf_op jit(solution)/shard_map/products/pallas_call | solution.py:216
  215.3 2.7 %products.13 = f32[128,1024]{1,0:T(8,128)S(1)} custom-call(bf16[16,2048]{1,0:T(8,128)(2,1)S(1)} %bitcast.293, bf16[16,2048]{1,0:T(8,128)(2,1)S(1)} %get-tuple-element.140.refs_1_, bf16[16,2048]{1,0:T(8,128)(2,1)S(1)} %get-tuple-element.136.refs_2_, bf16[16,2048]{1,0:T(8,128)(2,1)S(1)} %get-tuple-element.132.refs_3_, ...), custom_call_target="tpu_custom_call" | custom-call | flops 1 | bytes 1 | tf_op jit(solution)/shard_map/products/pallas_call | solution.py:216
  218.1 6.8 %collective-permute-done.42 = bf16[128,1024]{1,0:T(8,128)(2,1)S(1)} collective-permute-done((bf16[128,1024]{1,0:T(8,128)(2,1)S(1)}, bf16[128,1024]{1,0:T(8,128)(2,1)S(1)}, u32[]{:S(2)}, u32[]{:S(2)}) %collective-permute-start.42) | collective-permute-done | bytes 262176 | tf_op jit(solution)/shard_map/ppermute | solution.py:372
  225.1 2.4 collective-permute-start.45
  227.6 2.0 collective-permute-start.47
  229.6 2.7 %products.15 = f32[128,1024]{1,0:T(8,128)S(1)} custom-call(bf16[16,2048]{1,0:T(8,128)(2,1)S(1)} %bitcast.294, bf16[16,2048]{1,0:T(8,128)(2,1)S(1)} %get-tuple-element.179.refs_1_, bf16[16,2048]{1,0:T(8,128)(2,1)S(1)} %get-tuple-element.175.refs_2_, bf16[16,2048]{1,0:T(8,128)(2,1)S(1)} %get-tuple-element.171.refs_3_, ...), custom_call_target="tpu_custom_call" | custom-call | flops 1 | bytes 1 | tf_op jit(solution)/shard_map/products/pallas_call | solution.py:216
  232.4 17.3 %collective-permute-done.46 = bf16[128,1024]{1,0:T(8,128)(2,1)S(1)} collective-permute-done((bf16[128,1024]{1,0:T(8,128)(2,1)S(1)}, bf16[128,1024]{1,0:T(8,128)(2,1)S(1)}, u32[]{:S(2)}, u32[]{:S(2)}) %collective-permute-start.46) | collective-permute-done | bytes 262176 | tf_op jit(solution)/shard_map/ppermute | solution.py:372
  (197 shorter events, 34.8 us)
Async XLA Ops:
  7.2 64.9 %all-to-all-start = ((bf16[8,256,1280]{2,1,0:T(8,128)(2,1)}), bf16[8,256,1280]{2,1,0:T(8,128)(2,1)}, u32[]{:S(2)}, u32[]{:S(2)}) async-start(bf16[8,256,1280]{2,1,0:T(8,128)(2,1)} %bitcast.301), calls=%async_computation | async-start | bytes 10485760 | tf_op jit(solution)/shard_map/all_to_all | solution.py:297
  19.0 25.9 %collective-permute-start = (bf16[128,2048]{1,0:T(8,128)(2,1)}, bf16[128,2048]{1,0:T(8,128)(2,1)S(1)}, u32[]{:S(2)}, u32[]{:S(2)}) collective-permute-start(bf16[128,2048]{1,0:T(8,128)(2,1)} %get-tuple-element.46), channel_id=1, source_target_pairs={{0,8},{8,0},{16,24},{24,16},{1,9},{9,1},{17,25},{25,17},{2,10},{10... | collective-permute-start | bytes 1572872 | tf_op jit(solution)/shard_map/ppermute | solution.py:302
  21.6 38.4 %collective-permute-start.1 = (bf16[128,2048]{1,0:T(8,128)(2,1)}, bf16[128,2048]{1,0:T(8,128)(2,1)S(1)}, u32[]{:S(2)}, u32[]{:S(2)}) collective-permute-start(bf16[128,2048]{1,0:T(8,128)(2,1)} %get-tuple-element.47), channel_id=1, source_target_pairs={{0,16},{8,24},{16,0},{24,8},{1,17},{9,25},{17,1},{25,9},{2,18},{10... | collective-permute-start | bytes 1572872 | tf_op jit(solution)/shard_map/ppermute | solution.py:302
  24.2 35.8 %collective-permute-start.2 = (bf16[128,2048]{1,0:T(8,128)(2,1)}, bf16[128,2048]{1,0:T(8,128)(2,1)S(1)}, u32[]{:S(2)}, u32[]{:S(2)}) collective-permute-start(bf16[128,2048]{1,0:T(8,128)(2,1)} %get-tuple-element.48), channel_id=1, source_target_pairs={{0,24},{8,16},{16,8},{24,0},{1,25},{9,17},{17,9},{25,1},{2,26},{10... | collective-permute-start | bytes 1572872 | tf_op jit(solution)/shard_map/ppermute | solution.py:302
  24.2 37.1 %collective-permute-start.3 = (bf16[128,2048]{1,0:T(8,128)(2,1)}, bf16[128,2048]{1,0:T(8,128)(2,1)S(1)}, u32[]{:S(2)}, u32[]{:S(2)}) collective-permute-start(bf16[128,2048]{1,0:T(8,128)(2,1)} %get-tuple-element.49), channel_id=1, source_target_pairs={{0,4},{4,0},{1,5},{5,1},{2,6},{6,2},{3,7},{7,3},{8,12},{12,8},{9,1... | collective-permute-start | bytes 1572872 | tf_op jit(solution)/shard_map/ppermute | solution.py:304
  44.9 16.4 %collective-permute-start.4 = (bf16[128,2048]{1,0:T(8,128)(2,1)S(1)}, bf16[128,2048]{1,0:T(8,128)(2,1)S(1)}, u32[]{:S(2)}, u32[]{:S(2)}) collective-permute-start(bf16[128,2048]{1,0:T(8,128)(2,1)S(1)} %collective-permute-done), channel_id=1, source_target_pairs={{0,4},{4,0},{1,5},{5,1},{2,6},{6,2},{3,7},{7,3},{8,12},{12,8},{9,1... | collective-permute-start | bytes 1572872 | tf_op jit(solution)/shard_map/ppermute | solution.py:304
  60.0 2.6 %collective-permute-start.5 = (bf16[128,2048]{1,0:T(8,128)(2,1)S(1)}, bf16[128,2048]{1,0:T(8,128)(2,1)S(1)}, u32[]{:S(2)}, u32[]{:S(2)}) collective-permute-start(bf16[128,2048]{1,0:T(8,128)(2,1)S(1)} %collective-permute-done.1), channel_id=1, source_target_pairs={{0,4},{4,0},{1,5},{5,1},{2,6},{6,2},{3,7},{7,3},{8,12},{12,8},{9,1... | collective-permute-start | bytes 1572872 | tf_op jit(solution)/shard_map/ppermute | solution.py:304
  60.0 2.8 %collective-permute-start.6 = (bf16[128,2048]{1,0:T(8,128)(2,1)S(1)}, bf16[128,2048]{1,0:T(8,128)(2,1)}, u32[]{:S(2)}, u32[]{:S(2)}) collective-permute-start(bf16[128,2048]{1,0:T(8,128)(2,1)S(1)} %collective-permute-done.2), channel_id=1, source_target_pairs={{0,4},{4,0},{1,5},{5,1},{2,6},{6,2},{3,7},{7,3},{8,12},{12,8},{9,1... | collective-permute-start | bytes 1572872 | tf_op jit(solution)/shard_map/ppermute | solution.py:304
  72.1 53.7 %all-to-all-start.1 = ((bf16[8,256,1024]{2,1,0:T(8,128)(2,1)}), bf16[8,256,1024]{2,1,0:T(8,128)(2,1)}, u32[]{:S(2)}, u32[]{:S(2)}) async-start(bf16[8,256,1024]{2,1,0:T(8,128)(2,1)} %bitcast.302), calls=%async_computation.1 | async-start | bytes 8388608 | tf_op jit(solution)/shard_map/all_to_all | solution.py:309
  91.6 13.8 %collective-permute-start.7 = (f16[128,1280]{1,0:T(8,128)(2,1)S(1)}, f16[128,1280]{1,0:T(8,128)(2,1)S(1)}, u32[]{:S(2)}, u32[]{:S(2)}) collective-permute-start(f16[128,1280]{1,0:T(8,128)(2,1)S(1)} %convert_element_type.106), channel_id=1, source_target_pairs={{0,24},{8,16},{16,8},{24,0},{1,25},{9,17},{17,9},{25,1},{2,26},{10... | collective-permute-start | bytes 983048 | tf_op jit(solution)/shard_map/ppermute | solution.py:322
  96.4 16.3 %collective-permute-start.9 = (f16[128,1280]{1,0:T(8,128)(2,1)S(1)}, f16[128,1280]{1,0:T(8,128)(2,1)S(1)}, u32[]{:S(2)}, u32[]{:S(2)}) collective-permute-start(f16[128,1280]{1,0:T(8,128)(2,1)S(1)} %convert_element_type.110), channel_id=1, source_target_pairs={{0,8},{8,0},{16,24},{24,16},{1,9},{9,1},{17,25},{25,17},{2,10},{10... | collective-permute-start | bytes 983048 | tf_op jit(solution)/shard_map/ppermute | solution.py:322
  96.4 28.4 %collective-permute-start.8 = (f16[128,1280]{1,0:T(8,128)(2,1)S(1)}, f16[128,1280]{1,0:T(8,128)(2,1)S(1)}, u32[]{:S(2)}, u32[]{:S(2)}) collective-permute-start(f16[128,1280]{1,0:T(8,128)(2,1)S(1)} %convert_element_type.108), channel_id=1, source_target_pairs={{0,16},{8,24},{16,0},{24,8},{1,17},{9,25},{17,1},{25,9},{2,18},{10... | collective-permute-start | bytes 983048 | tf_op jit(solution)/shard_map/ppermute | solution.py:322
  126.9 5.6 %collective-permute-start.10 = (f32[64,1280]{1,0:T(8,128)S(1)}, f32[64,1280]{1,0:T(8,128)S(1)}, u32[]{:S(2)}, u32[]{:S(2)}) collective-permute-start(f32[64,1280]{1,0:T(8,128)S(1)} %slice.451), channel_id=1, source_target_pairs={{0,4},{4,0},{1,5},{5,1},{2,6},{6,2},{3,7},{7,3},{8,12},{12,8},{9,1... | collective-permute-start | bytes 983048 | tf_op jit(solution)/shard_map/ppermute | solution.py:336
  127.2 19.5 %collective-permute-start.24 = (f16[128,1280]{1,0:T(8,128)(2,1)S(1)}, f16[128,1280]{1,0:T(8,128)(2,1)S(1)}, u32[]{:S(2)}, u32[]{:S(2)}) collective-permute-start(f16[128,1280]{1,0:T(8,128)(2,1)S(1)} %convert_element_type.119), channel_id=1, source_target_pairs={{0,24},{8,16},{16,8},{24,0},{1,25},{9,17},{17,9},{25,1},{2,26},{10... | collective-permute-start | bytes 983048 | tf_op jit(solution)/shard_map/ppermute | solution.py:322
  131.8 16.3 %collective-permute-start.26 = (f16[128,1280]{1,0:T(8,128)(2,1)S(1)}, f16[128,1280]{1,0:T(8,128)(2,1)S(1)}, u32[]{:S(2)}, u32[]{:S(2)}) collective-permute-start(f16[128,1280]{1,0:T(8,128)(2,1)S(1)} %convert_element_type.123), channel_id=1, source_target_pairs={{0,8},{8,0},{16,24},{24,16},{1,9},{9,1},{17,25},{25,17},{2,10},{10... | collective-permute-start | bytes 983048 | tf_op jit(solution)/shard_map/ppermute | solution.py:322
  131.8 28.3 %collective-permute-start.25 = (f16[128,1280]{1,0:T(8,128)(2,1)S(1)}, f16[128,1280]{1,0:T(8,128)(2,1)S(1)}, u32[]{:S(2)}, u32[]{:S(2)}) collective-permute-start(f16[128,1280]{1,0:T(8,128)(2,1)S(1)} %convert_element_type.121), channel_id=1, source_target_pairs={{0,16},{8,24},{16,0},{24,8},{1,17},{9,25},{17,1},{25,9},{2,18},{10... | collective-permute-start | bytes 983048 | tf_op jit(solution)/shard_map/ppermute | solution.py:322
  141.0 19.4 %collective-permute-start.13 = (bf16[16,2048]{1,0:T(8,128)(2,1)S(1)}, bf16[16,2048]{1,0:T(8,128)(2,1)S(1)}, u32[]{:S(2)}, u32[]{:S(2)}) collective-permute-start(bf16[16,2048]{1,0:T(8,128)(2,1)S(1)} %get-tuple-element.149), channel_id=1, source_target_pairs={{0,3},{1,2},{2,1},{3,0},{4,7},{5,6},{6,5},{7,4},{8,11},{9,10},{10,... | collective-permute-start | bytes 196616 | tf_op jit(solution)/shard_map/ppermute | solution.py:357
  142.8 17.7 %collective-permute-start.12 = (bf16[16,2048]{1,0:T(8,128)(2,1)S(1)}, bf16[16,2048]{1,0:T(8,128)(2,1)S(1)}, u32[]{:S(2)}, u32[]{:S(2)}) collective-permute-start(bf16[16,2048]{1,0:T(8,128)(2,1)S(1)} %get-tuple-element.150), channel_id=1, source_target_pairs={{0,2},{1,3},{2,0},{3,1},{4,6},{5,7},{6,4},{7,5},{8,10},{9,11},{10,... | collective-permute-start | bytes 196616 | tf_op jit(solution)/shard_map/ppermute | solution.py:357
  146.7 13.7 %collective-permute-start.11 = (bf16[16,2048]{1,0:T(8,128)(2,1)S(1)}, bf16[16,2048]{1,0:T(8,128)(2,1)S(1)}, u32[]{:S(2)}, u32[]{:S(2)}) collective-permute-start(bf16[16,2048]{1,0:T(8,128)(2,1)S(1)} %get-tuple-element.151), channel_id=1, source_target_pairs={{0,1},{1,0},{2,3},{3,2},{4,5},{5,4},{6,7},{7,6},{8,9},{9,8},{10,11... | collective-permute-start | bytes 196616 | tf_op jit(solution)/shard_map/ppermute | solution.py:357
  160.3 4.6 %collective-permute-start.27 = (f32[64,1280]{1,0:T(8,128)S(1)}, f32[64,1280]{1,0:T(8,128)S(1)}, u32[]{:S(2)}, u32[]{:S(2)}) collective-permute-start(f32[64,1280]{1,0:T(8,128)S(1)} %slice.468), channel_id=1, source_target_pairs={{0,4},{4,0},{1,5},{5,1},{2,6},{6,2},{3,7},{7,3},{8,12},{12,8},{9,1... | collective-permute-start | bytes 983048 | tf_op jit(solution)/shard_map/ppermute | solution.py:336
  160.5 15.3 %collective-permute-start.16 = (bf16[16,2048]{1,0:T(8,128)(2,1)S(1)}, bf16[16,2048]{1,0:T(8,128)(2,1)S(1)}, u32[]{:S(2)}, u32[]{:S(2)}) collective-permute-start(bf16[16,2048]{1,0:T(8,128)(2,1)S(1)} %get-tuple-element.145), channel_id=1, source_target_pairs={{0,24},{8,16},{16,8},{24,0},{1,25},{9,17},{17,9},{25,1},{2,26},{10... | collective-permute-start | bytes 196616 | tf_op jit(solution)/shard_map/ppermute | solution.py:362
  163.1 13.8 %collective-permute-start.15 = (bf16[16,2048]{1,0:T(8,128)(2,1)S(1)}, bf16[16,2048]{1,0:T(8,128)(2,1)S(1)}, u32[]{:S(2)}, u32[]{:S(2)}) collective-permute-start(bf16[16,2048]{1,0:T(8,128)(2,1)S(1)} %get-tuple-element.146), channel_id=1, source_target_pairs={{0,16},{8,24},{16,0},{24,8},{1,17},{9,25},{17,1},{25,9},{2,18},{10... | collective-permute-start | bytes 196616 | tf_op jit(solution)/shard_map/ppermute | solution.py:362
  163.1 13.8 %collective-permute-start.14 = (bf16[16,2048]{1,0:T(8,128)(2,1)S(1)}, bf16[16,2048]{1,0:T(8,128)(2,1)S(1)}, u32[]{:S(2)}, u32[]{:S(2)}) collective-permute-start(bf16[16,2048]{1,0:T(8,128)(2,1)S(1)} %get-tuple-element.147), channel_id=1, source_target_pairs={{0,8},{8,0},{16,24},{24,16},{1,9},{9,1},{17,25},{25,17},{2,10},{10... | collective-permute-start | bytes 196616 | tf_op jit(solution)/shard_map/ppermute | solution.py:362
  173.3 5.8 %collective-permute-start.30 = (bf16[16,2048]{1,0:T(8,128)(2,1)S(1)}, bf16[16,2048]{1,0:T(8,128)(2,1)S(1)}, u32[]{:S(2)}, u32[]{:S(2)}) collective-permute-start(bf16[16,2048]{1,0:T(8,128)(2,1)S(1)} %get-tuple-element.188), channel_id=1, source_target_pairs={{0,3},{1,2},{2,1},{3,0},{4,7},{5,6},{6,5},{7,4},{8,11},{9,10},{10,... | collective-permute-start | bytes 196616 | tf_op jit(solution)/shard_map/ppermute | solution.py:357
  174.5 5.7 %collective-permute-start.29 = (bf16[16,2048]{1,0:T(8,128)(2,1)S(1)}, bf16[16,2048]{1,0:T(8,128)(2,1)S(1)}, u32[]{:S(2)}, u32[]{:S(2)}) collective-permute-start(bf16[16,2048]{1,0:T(8,128)(2,1)S(1)} %get-tuple-element.189), channel_id=1, source_target_pairs={{0,2},{1,3},{2,0},{3,1},{4,6},{5,7},{6,4},{7,5},{8,10},{9,11},{10,... | collective-permute-start | bytes 196616 | tf_op jit(solution)/shard_map/ppermute | solution.py:357
  175.8 4.7 %collective-permute-start.28 = (bf16[16,2048]{1,0:T(8,128)(2,1)S(1)}, bf16[16,2048]{1,0:T(8,128)(2,1)S(1)}, u32[]{:S(2)}, u32[]{:S(2)}) collective-permute-start(bf16[16,2048]{1,0:T(8,128)(2,1)S(1)} %get-tuple-element.190), channel_id=1, source_target_pairs={{0,1},{1,0},{2,3},{3,2},{4,5},{5,4},{6,7},{7,6},{8,9},{9,8},{10,11... | collective-permute-start | bytes 196616 | tf_op jit(solution)/shard_map/ppermute | solution.py:357
  176.9 4.8 %collective-permute-start.20 = (bf16[4,16,2048]{2,1,0:T(8,128)(2,1)S(1)}, bf16[4,16,2048]{2,1,0:T(8,128)(2,1)S(1)}, u32[]{:S(2)}, u32[]{:S(2)}) collective-permute-start(bf16[4,16,2048]{2,1,0:T(8,128)(2,1)S(1)} %pad_maximum_fusion.2), channel_id=1, source_target_pairs={{0,4},{4,0},{1,5},{5,1},{2,6},{6,2},{3,7},{7,3},{8,12},{12,8},{9,1... | collective-permute-start | bytes 786440 | tf_op jit(solution)/shard_map/ppermute | solution.py:365
  177.0 10.1 %collective-permute-start.19 = (bf16[4,16,2048]{2,1,0:T(8,128)(2,1)S(1)}, bf16[4,16,2048]{2,1,0:T(8,128)(2,1)S(1)}, u32[]{:S(2)}, u32[]{:S(2)}) collective-permute-start(bf16[4,16,2048]{2,1,0:T(8,128)(2,1)S(1)} %pad_maximum_fusion.2), channel_id=1, source_target_pairs={{0,3},{1,2},{2,1},{3,0},{4,7},{5,6},{6,5},{7,4},{8,11},{9,10},{10,... | collective-permute-start | bytes 786440 | tf_op jit(solution)/shard_map/ppermute | solution.py:364
  179.1 13.0 %collective-permute-start.18 = (bf16[4,16,2048]{2,1,0:T(8,128)(2,1)S(1)}, bf16[4,16,2048]{2,1,0:T(8,128)(2,1)S(1)}, u32[]{:S(2)}, u32[]{:S(2)}) collective-permute-start(bf16[4,16,2048]{2,1,0:T(8,128)(2,1)S(1)} %pad_maximum_fusion.2), channel_id=1, source_target_pairs={{0,2},{1,3},{2,0},{3,1},{4,6},{5,7},{6,4},{7,5},{8,10},{9,11},{10,... | collective-permute-start | bytes 786440 | tf_op jit(solution)/shard_map/ppermute | solution.py:364
  180.2 12.0 %collective-permute-start.17 = (bf16[4,16,2048]{2,1,0:T(8,128)(2,1)S(1)}, bf16[4,16,2048]{2,1,0:T(8,128)(2,1)S(1)}, u32[]{:S(2)}, u32[]{:S(2)}) collective-permute-start(bf16[4,16,2048]{2,1,0:T(8,128)(2,1)S(1)} %pad_maximum_fusion.2), channel_id=1, source_target_pairs={{0,1},{1,0},{2,3},{3,2},{4,5},{5,4},{6,7},{7,6},{8,9},{9,8},{10,11... | collective-permute-start | bytes 786440 | tf_op jit(solution)/shard_map/ppermute | solution.py:364
  180.7 12.1 %collective-permute-start.33 = (bf16[16,2048]{1,0:T(8,128)(2,1)S(1)}, bf16[16,2048]{1,0:T(8,128)(2,1)S(1)}, u32[]{:S(2)}, u32[]{:S(2)}) collective-permute-start(bf16[16,2048]{1,0:T(8,128)(2,1)S(1)} %get-tuple-element.184), channel_id=1, source_target_pairs={{0,16},{8,24},{16,0},{24,8},{1,17},{9,25},{17,1},{25,9},{2,18},{10... | collective-permute-start | bytes 196616 | tf_op jit(solution)/shard_map/ppermute | solution.py:362
  181.8 11.1 %collective-permute-start.32 = (bf16[16,2048]{1,0:T(8,128)(2,1)S(1)}, bf16[16,2048]{1,0:T(8,128)(2,1)S(1)}, u32[]{:S(2)}, u32[]{:S(2)}) collective-permute-start(bf16[16,2048]{1,0:T(8,128)(2,1)S(1)} %get-tuple-element.185), channel_id=1, source_target_pairs={{0,8},{8,0},{16,24},{24,16},{1,9},{9,1},{17,25},{25,17},{2,10},{10... | collective-permute-start | bytes 196616 | tf_op jit(solution)/shard_map/ppermute | solution.py:362
  187.1 6.1 %collective-permute-start.31 = (bf16[16,2048]{1,0:T(8,128)(2,1)S(1)}, bf16[16,2048]{1,0:T(8,128)(2,1)S(1)}, u32[]{:S(2)}, u32[]{:S(2)}) collective-permute-start(bf16[16,2048]{1,0:T(8,128)(2,1)S(1)} %get-tuple-element.186), channel_id=1, source_target_pairs={{0,24},{8,16},{16,8},{24,0},{1,25},{9,17},{17,9},{25,1},{2,26},{10... | collective-permute-start | bytes 196616 | tf_op jit(solution)/shard_map/ppermute | solution.py:362
  192.2 2.5 collective-permute-start.23
  192.2 3.9 %collective-permute-start.22 = (bf16[4,16,2048]{2,1,0:T(8,128)(2,1)S(1)}, bf16[4,16,2048]{2,1,0:T(8,128)(2,1)S(1)}, u32[]{:S(2)}, u32[]{:S(2)}) collective-permute-start(bf16[4,16,2048]{2,1,0:T(8,128)(2,1)S(1)} %collective-permute-done.18), channel_id=1, source_target_pairs={{0,4},{4,0},{1,5},{5,1},{2,6},{6,2},{3,7},{7,3},{8,12},{12,8},{9,1... | collective-permute-start | bytes 786440 | tf_op jit(solution)/shard_map/ppermute | solution.py:365
  192.8 4.3 %collective-permute-start.21 = (bf16[4,16,2048]{2,1,0:T(8,128)(2,1)S(1)}, bf16[4,16,2048]{2,1,0:T(8,128)(2,1)S(1)}, u32[]{:S(2)}, u32[]{:S(2)}) collective-permute-start(bf16[4,16,2048]{2,1,0:T(8,128)(2,1)S(1)} %collective-permute-done.17), channel_id=1, source_target_pairs={{0,4},{4,0},{1,5},{5,1},{2,6},{6,2},{3,7},{7,3},{8,12},{12,8},{9,1... | collective-permute-start | bytes 786440 | tf_op jit(solution)/shard_map/ppermute | solution.py:365
  193.2 10.3 %collective-permute-start.37 = (bf16[4,16,2048]{2,1,0:T(8,128)(2,1)S(1)}, bf16[4,16,2048]{2,1,0:T(8,128)(2,1)S(1)}, u32[]{:S(2)}, u32[]{:S(2)}) collective-permute-start(bf16[4,16,2048]{2,1,0:T(8,128)(2,1)S(1)} %pad_maximum_fusion.4), channel_id=1, source_target_pairs={{0,4},{4,0},{1,5},{5,1},{2,6},{6,2},{3,7},{7,3},{8,12},{12,8},{9,1... | collective-permute-start | bytes 786440 | tf_op jit(solution)/shard_map/ppermute | solution.py:365
  193.5 10.1 %collective-permute-start.36 = (bf16[4,16,2048]{2,1,0:T(8,128)(2,1)S(1)}, bf16[4,16,2048]{2,1,0:T(8,128)(2,1)S(1)}, u32[]{:S(2)}, u32[]{:S(2)}) collective-permute-start(bf16[4,16,2048]{2,1,0:T(8,128)(2,1)S(1)} %pad_maximum_fusion.4), channel_id=1, source_target_pairs={{0,3},{1,2},{2,1},{3,0},{4,7},{5,6},{6,5},{7,4},{8,11},{9,10},{10,... | collective-permute-start | bytes 786440 | tf_op jit(solution)/shard_map/ppermute | solution.py:364
  194.7 13.8 %collective-permute-start.35 = (bf16[4,16,2048]{2,1,0:T(8,128)(2,1)S(1)}, bf16[4,16,2048]{2,1,0:T(8,128)(2,1)S(1)}, u32[]{:S(2)}, u32[]{:S(2)}) collective-permute-start(bf16[4,16,2048]{2,1,0:T(8,128)(2,1)S(1)} %pad_maximum_fusion.4), channel_id=1, source_target_pairs={{0,2},{1,3},{2,0},{3,1},{4,6},{5,7},{6,4},{7,5},{8,10},{9,11},{10,... | collective-permute-start | bytes 786440 | tf_op jit(solution)/shard_map/ppermute | solution.py:364
  196.1 12.4 %collective-permute-start.34 = (bf16[4,16,2048]{2,1,0:T(8,128)(2,1)S(1)}, bf16[4,16,2048]{2,1,0:T(8,128)(2,1)S(1)}, u32[]{:S(2)}, u32[]{:S(2)}) collective-permute-start(bf16[4,16,2048]{2,1,0:T(8,128)(2,1)S(1)} %pad_maximum_fusion.4), channel_id=1, source_target_pairs={{0,1},{1,0},{2,3},{3,2},{4,5},{5,4},{6,7},{7,6},{8,9},{9,8},{10,11... | collective-permute-start | bytes 786440 | tf_op jit(solution)/shard_map/ppermute | solution.py:364
  200.9 17.1 %collective-permute-start.41 = (bf16[128,1024]{1,0:T(8,128)(2,1)S(1)}, bf16[128,1024]{1,0:T(8,128)(2,1)S(1)}, u32[]{:S(2)}, u32[]{:S(2)}) collective-permute-start(bf16[128,1024]{1,0:T(8,128)(2,1)S(1)} %get-tuple-element.66), channel_id=1, source_target_pairs={{0,24},{8,16},{16,8},{24,0},{1,25},{9,17},{17,9},{25,1},{2,26},{10... | collective-permute-start | bytes 786440 | tf_op jit(solution)/shard_map/ppermute | solution.py:372
  203.5 21.4 %collective-permute-start.42 = (bf16[128,1024]{1,0:T(8,128)(2,1)S(1)}, bf16[128,1024]{1,0:T(8,128)(2,1)S(1)}, u32[]{:S(2)}, u32[]{:S(2)}) collective-permute-start(bf16[128,1024]{1,0:T(8,128)(2,1)S(1)} %get-tuple-element.67), channel_id=1, source_target_pairs={{0,16},{8,24},{16,0},{24,8},{1,17},{9,25},{17,1},{25,9},{2,18},{10... | collective-permute-start | bytes 786440 | tf_op jit(solution)/shard_map/ppermute | solution.py:372
  203.6 21.3 %collective-permute-start.43 = (bf16[128,1024]{1,0:T(8,128)(2,1)S(1)}, bf16[128,1024]{1,0:T(8,128)(2,1)S(1)}, u32[]{:S(2)}, u32[]{:S(2)}) collective-permute-start(bf16[128,1024]{1,0:T(8,128)(2,1)S(1)} %get-tuple-element.68), channel_id=1, source_target_pairs={{0,8},{8,0},{16,24},{24,16},{1,9},{9,1},{17,25},{25,17},{2,10},{10... | collective-permute-start | bytes 786440 | tf_op jit(solution)/shard_map/ppermute | solution.py:372
  208.5 1.9 collective-permute-start.39
  225.1 7.3 %collective-permute-start.44 = (bf16[64,1024]{1,0:T(8,128)(2,1)S(1)}, bf16[64,1024]{1,0:T(8,128)(2,1)S(1)}, u32[]{:S(2)}, u32[]{:S(2)}) collective-permute-start(bf16[64,1024]{1,0:T(8,128)(2,1)S(1)} %slice.520), channel_id=1, source_target_pairs={{0,4},{4,0},{1,5},{5,1},{2,6},{6,2},{3,7},{7,3},{8,12},{12,8},{9,1... | collective-permute-start | bytes 393224 | tf_op jit(solution)/shard_map/ppermute | solution.py:382
  225.1 24.6 %collective-permute-start.45 = (bf16[128,1024]{1,0:T(8,128)(2,1)S(1)}, bf16[128,1024]{1,0:T(8,128)(2,1)S(1)}, u32[]{:S(2)}, u32[]{:S(2)}) collective-permute-start(bf16[128,1024]{1,0:T(8,128)(2,1)S(1)} %get-tuple-element.65.refs_9_), channel_id=1, source_target_pairs={{0,24},{8,16},{16,8},{24,0},{1,25},{9,17},{17,9},{25,1},{2,26},{10... | collective-permute-start | bytes 786440 | tf_op jit(solution)/shard_map/ppermute | solution.py:372
  227.6 22.1 %collective-permute-start.46 = (bf16[128,1024]{1,0:T(8,128)(2,1)S(1)}, bf16[128,1024]{1,0:T(8,128)(2,1)S(1)}, u32[]{:S(2)}, u32[]{:S(2)}) collective-permute-start(bf16[128,1024]{1,0:T(8,128)(2,1)S(1)} %get-tuple-element.69), channel_id=1, source_target_pairs={{0,16},{8,24},{16,0},{24,8},{1,17},{9,25},{17,1},{25,9},{2,18},{10... | collective-permute-start | bytes 786440 | tf_op jit(solution)/shard_map/ppermute | solution.py:372
  227.6 22.1 %collective-permute-start.47 = (bf16[128,1024]{1,0:T(8,128)(2,1)S(1)}, bf16[128,1024]{1,0:T(8,128)(2,1)S(1)}, u32[]{:S(2)}, u32[]{:S(2)}) collective-permute-start(bf16[128,1024]{1,0:T(8,128)(2,1)S(1)} %get-tuple-element.70), channel_id=1, source_target_pairs={{0,8},{8,0},{16,24},{24,16},{1,9},{9,1},{17,25},{25,17},{2,10},{10... | collective-permute-start | bytes 786440 | tf_op jit(solution)/shard_map/ppermute | solution.py:372
  (13 other events, 46.9 us)
